TPU v7x, 32 devices: a whole 2x2x4 slice. The times are simulated.
32 devices in a mesh: dp: 4 (over y, x), seq: 8 (over z, core).
Axes of the slice: x: 2, y: 2, z: 4, core: 2. Of those that a mesh axis runs over, the one named last changes fastest.
Arguments:
- tokens: bfloat16 [2, 8192, 768], P(None, ('dp', 'seq')), may hold values from -6 to 6
- cotangent: bfloat16 [2, 8192, 768], P(None, ('dp', 'seq')), may hold values from -6 to 6
- lengths: int32 [2, 4, 16], P(None, 'dp'), may hold values from 0 to 512, as said below
- ln_gain: bfloat16 [768], P('seq'), may hold values from 0.5 to 1.5
- ln_bias: bfloat16 [768], P('seq'), may hold values from -3 to 3
- w_value: bfloat16 [768, 3072], P('seq'), may hold values from -0.21875 to 0.21875
- w_filter: bfloat16 [768, 1536], P('seq'), may hold values from -0.21875 to 0.21875
- w_fore: bfloat16 [1536, 3072], P('seq'), may hold values from -0.15625 to 0.15625
- w_back: bfloat16 [1536, 3072], P('seq'), may hold values from -0.15625 to 0.15625
- w_out: bfloat16 [3072, 768], P('seq'), may hold values from -0.21875 to 0.21875
- ssm_coef: float32 [2, 1536, 64], P(None, 'seq'), may hold values from -1 to 1
- ssm_rate: float32 [2, 1536, 64], P(None, 'seq'), may hold values from 0.001 to 0.12
- ssm_freq: float32 [2, 1536, 64], P(None, 'seq'), may hold values from 0 to 0.3
Outputs:
- mixed: bfloat16 [2, 8192, 768], P(None, ('dp', 'seq'))
- grad_tokens: bfloat16 [2, 8192, 768], P(None, ('dp', 'seq'))
- grad_gain: float32 [768], P('seq')
- grad_bias: float32 [768], P('seq')
- grad_value: float32 [768, 3072], P('seq')
- grad_filter: float32 [768, 1536], P('seq')
- grad_fore: float32 [1536, 3072], P('seq')
- grad_back: float32 [1536, 3072], P('seq')
- grad_out: float32 [3072, 768], P('seq')
- grad_coef: float32 [2, 1536, 64], P(None, 'seq')
- grad_rate: float32 [2, 1536, 64], P(None, 'seq')
- grad_freq: float32 [2, 1536, 64], P(None, 'seq')
Inputs may be any that keep to these rules, and one draw needn't show every extreme that they name: For each micro-batch m and stream g, lengths[m, g] lists the items of the stream's 2048 tokens in order, each of 128 or 512 tokens, followed by zeros; the items fill the stream exactly, and each stream has items of both lengths.
All inputs are finite; a program needn't handle non-finite values.
Results may differ from a plain program's by a relative error of at most 0.0087.
Values may be sent and summed in bfloat16 or wider, within the bound.
A program may use at most 368 MiB of HBM per device.

v0:
```python
from functools import partial

import jax
import jax.numpy as jnp
from jax import lax
from jax.sharding import PartitionSpec as P

LONG = 512
SHORT = 128


EPSILON = 1e-05
HIGHEST = lax.Precision.HIGHEST


def dot_plain(left_side, right_side):
    return jnp.dot(left_side, right_side, preferred_element_type=jnp.float32)


def dot_inner(left_side, right_side):
    return lax.dot_general(
        left_side, right_side, (((0,), (0,)), ((), ())), preferred_element_type=jnp.float32
    )


def dot_outer(left_side, right_side):
    return lax.dot_general(
        left_side, right_side, (((1,), (1,)), ((), ())), preferred_element_type=jnp.float32
    )


def layer_norm(token_rows, gain_vec, bias_vec):
    centre = jnp.mean(token_rows, axis=-1, keepdims=True)
    shifted = token_rows - centre
    spread = jnp.mean(shifted * shifted, axis=-1, keepdims=True)
    return shifted * lax.rsqrt(spread + EPSILON) * gain_vec + bias_vec


def make_kernels(ssm_coef, ssm_rate, ssm_freq):
    lag_steps = jnp.arange(LONG).astype(jnp.float32)

    def one_side(weights, decays, angular):
        wave_terms = (
            jnp.sqrt(decays)[:, :, None]
            * jnp.exp(-decays[:, :, None] * lag_steps)
            * jnp.cos(angular[:, :, None] * lag_steps)
        )
        return jnp.einsum("cn,cnl->cl", weights, wave_terms, precision=HIGHEST)

    return jnp.stack(
        [
            one_side(ssm_coef[0], ssm_rate[0], ssm_freq[0]),
            one_side(ssm_coef[1], ssm_rate[1], ssm_freq[1]),
        ]
    )


def banded(kernel_rows, lag_table):
    valid = (lag_table >= 0) & (lag_table < LONG)
    safe_lag = jnp.clip(lag_table, 0, LONG - 1)
    picked = jnp.take(kernel_rows, safe_lag.reshape(-1), axis=1).reshape(
        kernel_rows.shape[0], lag_table.shape[0], lag_table.shape[1]
    )
    return jnp.where(valid[None], picked, 0.0)


def build_toeplitz(kernels):
    rows_block = SHORT
    window_len = rows_block + LONG
    row_ids = jnp.arange(rows_block)[:, None]
    col_ids = jnp.arange(window_len)[None, :]
    causal_matrix = banded(kernels[0], row_ids + LONG - col_ids)
    anti_matrix = banded(kernels[1], col_ids - row_ids)
    return (causal_matrix, anti_matrix)


def item_index(positions, item_starts, item_sizes):
    present = (item_starts[None, :] <= positions[:, None]) & (item_sizes[None, :] > 0)
    return jnp.sum(present.astype(jnp.int32), axis=1) - 1


def apply_items(matrix, windows, window_items, row_items):
    keep_mask = (window_items == row_items).astype(jnp.float32)
    masked = windows * keep_mask[None]
    return lax.dot_general(
        matrix,
        masked,
        (((2,), (2,)), ((0,), (0,))),
        precision=HIGHEST,
        preferred_element_type=jnp.float32,
    )


def convolve(toeplitz, signal, item_starts, item_sizes):
    causal_matrix, anti_matrix = toeplitz
    length_all, channels = signal.shape
    rows_block = SHORT
    step_rows = 4 * LONG
    blocks = step_rows // rows_block
    reach_blocks = (LONG + rows_block) // rows_block
    lead_blocks = LONG // rows_block
    lines = jnp.transpose(
        jnp.concatenate(
            [
                jnp.zeros((LONG, channels), jnp.float32),
                signal,
                jnp.zeros((LONG, channels), jnp.float32),
            ],
            0,
        )
    )

    def one_step(step_index):
        anchor = step_index * step_rows
        segment = lax.dynamic_slice_in_dim(lines, anchor, step_rows + 2 * LONG, 1)
        positions = anchor - LONG + jnp.arange(step_rows + 2 * LONG)
        owners = item_index(positions, item_starts, item_sizes)
        seg_blocks = segment.reshape(channels, -1, rows_block)
        own_blocks = owners.reshape(-1, rows_block)
        row_items = own_blocks[lead_blocks : lead_blocks + blocks, :1]
        fore_win = jnp.concatenate(
            [seg_blocks[:, shift_at : shift_at + blocks] for shift_at in range(reach_blocks)], 2
        )
        fore_items = jnp.concatenate(
            [own_blocks[shift_at : shift_at + blocks] for shift_at in range(reach_blocks)], 1
        )
        back_win = jnp.concatenate(
            [
                seg_blocks[:, lead_blocks + shift_at : lead_blocks + shift_at + blocks]
                for shift_at in range(reach_blocks)
            ],
            2,
        )
        back_items = jnp.concatenate(
            [
                own_blocks[lead_blocks + shift_at : lead_blocks + shift_at + blocks]
                for shift_at in range(reach_blocks)
            ],
            1,
        )
        fore_out = apply_items(causal_matrix, fore_win, fore_items, row_items)
        back_out = apply_items(anti_matrix, back_win, back_items, row_items)
        fore_flat = jnp.transpose(fore_out, (0, 2, 1)).reshape(channels, step_rows)
        back_flat = jnp.transpose(back_out, (0, 2, 1)).reshape(channels, step_rows)
        return (fore_flat, back_flat)

    fore_all, back_all = lax.map(jax.checkpoint(one_step), jnp.arange(length_all // step_rows))
    fore_rows = jnp.transpose(jnp.transpose(fore_all, (1, 0, 2)).reshape(channels, length_all))
    back_rows = jnp.transpose(jnp.transpose(back_all, (1, 0, 2)).reshape(channels, length_all))
    return (fore_rows, back_rows)


def shards(
    tokens,
    cotangent,
    lengths,
    ln_gain,
    ln_bias,
    w_value,
    w_filter,
    w_fore,
    w_back,
    w_out,
    ssm_coef,
    ssm_rate,
    ssm_freq,
):
    micro_count = tokens.shape[0]
    kernels, kernel_pull = jax.vjp(make_kernels, ssm_coef, ssm_rate, ssm_freq)
    toeplitz, toeplitz_pull = jax.vjp(build_toeplitz, kernels)
    outputs_mixed = []
    outputs_grad = []
    summed = None
    toeplitz_sum = None
    for micro_index in range(micro_count):
        full_params = (
            lax.all_gather(ln_gain, "seq", axis=0, tiled=True),
            lax.all_gather(ln_bias, "seq", axis=0, tiled=True),
            lax.all_gather(w_value, "seq", axis=0, tiled=True),
            lax.all_gather(w_filter, "seq", axis=0, tiled=True),
            lax.all_gather(w_fore, "seq", axis=0, tiled=True),
            lax.all_gather(w_back, "seq", axis=0, tiled=True),
            lax.all_gather(w_out, "seq", axis=0, tiled=True),
        )
        gain_full, bias_full, value_w, filter_w, fore_w, back_w, out_w = full_params
        token_rows = tokens[micro_index].astype(jnp.float32)
        normed, norm_pull = jax.vjp(
            layer_norm, token_rows, gain_full.astype(jnp.float32), bias_full.astype(jnp.float32)
        )
        normed_low = normed.astype(jnp.bfloat16)
        pre_value = dot_plain(normed_low, value_w)
        pre_filter = dot_plain(normed_low, filter_w)
        value_act, value_pull = jax.vjp(jax.nn.gelu, pre_value)
        filter_act, filter_pull = jax.vjp(jax.nn.gelu, pre_filter)
        channel_rows = lax.all_to_all(
            filter_act.astype(jnp.bfloat16), "seq", split_axis=1, concat_axis=0, tiled=True
        )
        item_sizes = lengths[micro_index, 0]
        item_starts = jnp.cumsum(item_sizes) - item_sizes
        conv_items = partial(convolve, item_starts=item_starts, item_sizes=item_sizes)
        (fore_conv, back_conv), conv_pull = jax.vjp(
            conv_items, toeplitz, channel_rows.astype(jnp.float32)
        )
        fore_low, back_low = (
            lax.all_to_all(
                fore_conv.astype(jnp.bfloat16), "seq", split_axis=0, concat_axis=1, tiled=True
            ),
            lax.all_to_all(
                back_conv.astype(jnp.bfloat16), "seq", split_axis=0, concat_axis=1, tiled=True
            ),
        )
        proj_fore = dot_plain(fore_low, fore_w)
        proj_back = dot_plain(back_low, back_w)
        hidden_low = (proj_fore * proj_back * value_act).astype(jnp.bfloat16)
        outputs_mixed.append((token_rows + dot_plain(hidden_low, out_w)).astype(jnp.bfloat16))
        cot_rows = cotangent[micro_index]
        grad_hidden = dot_outer(cot_rows, out_w)
        out_grad = dot_inner(hidden_low, cot_rows)
        grad_proj_fore = (grad_hidden * proj_back * value_act).astype(jnp.bfloat16)
        grad_proj_back = (grad_hidden * proj_fore * value_act).astype(jnp.bfloat16)
        grad_value_act = grad_hidden * proj_fore * proj_back
        fore_grad = dot_inner(fore_low, grad_proj_fore)
        back_grad = dot_inner(back_low, grad_proj_back)
        grad_fore_low = dot_outer(grad_proj_fore, fore_w).astype(jnp.bfloat16)
        grad_back_low = dot_outer(grad_proj_back, back_w).astype(jnp.bfloat16)
        sent_fore, sent_back = (
            lax.all_to_all(grad_fore_low, "seq", split_axis=1, concat_axis=0, tiled=True),
            lax.all_to_all(grad_back_low, "seq", split_axis=1, concat_axis=0, tiled=True),
        )
        toeplitz_grad, channel_grad = conv_pull(
            (sent_fore.astype(jnp.float32), sent_back.astype(jnp.float32))
        )
        grad_filter_act = lax.all_to_all(
            channel_grad.astype(jnp.bfloat16), "seq", split_axis=0, concat_axis=1, tiled=True
        )
        grad_pre_filter = filter_pull(grad_filter_act.astype(jnp.float32))[0].astype(jnp.bfloat16)
        grad_pre_value = value_pull(grad_value_act)[0].astype(jnp.bfloat16)
        value_grad = dot_inner(normed_low, grad_pre_value)
        filter_grad = dot_inner(normed_low, grad_pre_filter)
        grad_normed = dot_outer(grad_pre_value, value_w) + dot_outer(grad_pre_filter, filter_w)
        grad_rows, gain_grad, bias_grad = norm_pull(grad_normed)
        outputs_grad.append((cot_rows.astype(jnp.float32) + grad_rows).astype(jnp.bfloat16))
        piece_grads = (
            lax.psum_scatter(gain_grad, "seq", scatter_dimension=0, tiled=True),
            lax.psum_scatter(bias_grad, "seq", scatter_dimension=0, tiled=True),
            lax.psum_scatter(value_grad, "seq", scatter_dimension=0, tiled=True),
            lax.psum_scatter(filter_grad, "seq", scatter_dimension=0, tiled=True),
            lax.psum_scatter(fore_grad, "seq", scatter_dimension=0, tiled=True),
            lax.psum_scatter(back_grad, "seq", scatter_dimension=0, tiled=True),
            lax.psum_scatter(out_grad, "seq", scatter_dimension=0, tiled=True),
        )
        summed = piece_grads if summed is None else jax.tree.map(jnp.add, summed, piece_grads)
        toeplitz_sum = (
            toeplitz_grad
            if toeplitz_sum is None
            else jax.tree.map(jnp.add, toeplitz_sum, toeplitz_grad)
        )
    kernel_grads = toeplitz_pull(toeplitz_sum)[0]
    coef_grad, rate_grad, freq_grad = kernel_pull(kernel_grads)
    totals = lax.psum(
        (
            summed[0],
            summed[1],
            summed[2],
            summed[3],
            summed[4],
            summed[5],
            summed[6],
            coef_grad,
            rate_grad,
            freq_grad,
        ),
        "dp",
    )
    mixed = jnp.stack(outputs_mixed)
    grad_tokens = jnp.stack(outputs_grad)
    return (
        mixed,
        grad_tokens,
        totals[0],
        totals[1],
        totals[2],
        totals[3],
        totals[4],
        totals[5],
        totals[6],
        totals[7],
        totals[8],
        totals[9],
    )


def solution(mesh):
    return jax.shard_map(
        shards,
        mesh=mesh,
        in_specs=(
            P(None, ("dp", "seq"), None),
            P(None, ("dp", "seq"), None),
            P(None, "dp", None),
            P("seq"),
            P("seq"),
            P("seq", None),
            P("seq", None),
            P("seq", None),
            P("seq", None),
            P("seq", None),
            P(None, "seq", None),
            P(None, "seq", None),
            P(None, "seq", None),
        ),
        out_specs=(
            P(None, ("dp", "seq"), None),
            P(None, ("dp", "seq"), None),
            P("seq"),
            P("seq"),
            P("seq", None),
            P("seq", None),
            P("seq", None),
            P("seq", None),
            P("seq", None),
            P(None, "seq", None),
            P(None, "seq", None),
            P(None, "seq", None),
        ),
        check_vma=False,
    )
```

profile of v0, /device:TPU:0, one launch (start us, length us, event | category | flops | bytes accessed | tf_op | source)
XLA Modules:
  0.0 3919.2 jit_solution(5189295500698688124)
XLA Ops:
  18.1 177.8 %multiply_reduce_fusion.2 = (f32[192,512]{1,0:T(8,128)}, f32[192,512]{1,0:T(8,128)S(1)}) fusion(f32[192,64]{1,0:T(8,128)S(1)} %copy.214, f32[192,64]{1,0:T(8,128)S(1)} %copy.159, f32[192,64]{1,0:T(8,128)S(1)} %get-tuple-element.322, f32[192,64]{1,0:T(8,128)S(1)} %get-tuple-element.321, f32[512]{0:T(512)S(1)} %iota_convert_fusion, f32[192,64]{1,0:T(8,128)S(1)} %copy.213, ...), kind=kLoop, calls=%fused_computation.42 | loop fusion | flops 75300864 | bytes 1181696
  196.2 306.4 %gather_fusion = f32[81920,192]{1,0:T(8,128)} fusion(f32[192,512]{0,1:T(8,128)S(1)} %copy.192, s32[81920]{0:T(1024)S(1)} %get-tuple-element.310), kind=kCustom, calls=%fused_computation.clone | custom fusion | bytes 126156800 | tf_op jit(solution)/shard_map/jvp(jit(_take))/gather | solution.py:61
  502.6 54.3 %broadcast_select_fusion.1 = f32[81920,192]{1,0:T(8,128)} fusion(f32[81920,192]{1,0:T(8,128)} %gather_fusion, pred[81920]{0:T(1024)(128)(4,1)S(1)} %copy-done.86), kind=kLoop, calls=%fused_computation.7 | loop fusion | flops 15728640 | bytes 125911040 | tf_op jit(solution)/shard_map/jvp(jit(_take))/select_n | solution.py:61
  557.0 77.7 %copy.207 = f32[192,128,640]{2,1,0:T(8,128)} copy(f32[192,128,640]{0,2,1:T(8,128)} %bitcast.20) | data formatting | bytes 125829120 | tf_op jit(solution)/shard_map/jvp()/reshape | solution.py:61
  638.3 30.2 all-reduce.35
  673.3 306.4 %gather_fusion.1 = f32[81920,192]{1,0:T(8,128)} fusion(f32[192,512]{0,1:T(8,128)S(1)} %copy.196, s32[81920]{0:T(1024)S(1)} %copy-done.67), kind=kCustom, calls=%fused_computation.1.clone | custom fusion | bytes 126156800 | tf_op jit(solution)/shard_map/jvp(jit(_take))/gather | solution.py:61
  979.8 54.3 %broadcast_select_fusion = f32[81920,192]{1,0:T(8,128)} fusion(f32[81920,192]{1,0:T(8,128)} %gather_fusion.1, pred[81920]{0:T(1024)(128)(4,1)S(1)} %copy-done.85), kind=kLoop, calls=%fused_computation.6 | loop fusion | flops 15728640 | bytes 125911040 | tf_op jit(solution)/shard_map/jvp(jit(_take))/select_n | solution.py:61
  1034.0 77.5 %copy.208 = f32[192,128,640]{2,1,0:T(8,128)} copy(f32[192,128,640]{0,2,1:T(8,128)} %bitcast.33) | data formatting | bytes 125829120 | tf_op jit(solution)/shard_map/jvp()/reshape | solution.py:61
  1111.6 42.7 %broadcast_select_fusion.3 = f32[192,128,640]{2,1,0:T(8,128)} fusion(f32[192,128,640]{2,1,0:T(8,128)} %copy.207, pred[128,640]{1,0:T(8,128)(4,1)S(1)} %copy-done.63), kind=kLoop, calls=%fused_computation.17 | loop fusion | flops 15728640 | bytes 125911040 | tf_op jit(solution)/shard_map/jvp(jit(_where))/select_n | solution.py:64
  1154.5 41.8 %broadcast_select_fusion.2 = f32[192,128,640]{2,1,0:T(8,128)} fusion(f32[192,128,640]{2,1,0:T(8,128)} %copy.208, pred[128,640]{1,0:T(8,128)(4,1)S(1)} %copy-done.65), kind=kLoop, calls=%fused_computation.16 | loop fusion | flops 15728640 | bytes 125911040 | tf_op jit(solution)/shard_map/jvp(jit(_where))/select_n | solution.py:64
  1209.9 15.7 all-to-all-done.3
  1229.8 20.4 all-to-all-done
  1258.9 64.7 %fusion.86 = bf16[192,16,128]{2,1,0:T(8,128)(2,1)S(1)} fusion(f32[192,128,640]{2,1,0:T(8,128)} %broadcast_select_fusion.3, f32[192,16,640]{2,1,0:T(8,128)S(1)} %get-tuple-element.288, f32[16,640]{1,0:T(8,128)S(1)} %get-tuple-element.384), kind=kOutput, calls=%fused_computation.187 | convolution fusion | flops 3022258176 | bytes 71606272 | tf_op jit(solution)/shard_map/jvp()/while/body/eval_jaxpr/dot_general | solution.py:85
  1335.0 64.9 %fusion.80 = bf16[192,16,128]{2,1,0:T(8,128)(2,1)S(1)} fusion(f32[192,128,640]{2,1,0:T(8,128)} %broadcast_select_fusion.3, f32[192,16,640]{2,1,0:T(8,128)} %copy-done.7, f32[16,640]{1,0:T(8,128)S(1)} %get-tuple-element.382), kind=kOutput, calls=%fused_computation.185 | convolution fusion | flops 3022258176 | bytes 71606272 | tf_op jit(solution)/shard_map/jvp()/while/body/eval_jaxpr/dot_general | solution.py:85
  1400.0 64.8 %fusion.89 = bf16[192,16,128]{2,1,0:T(8,128)(2,1)S(1)} fusion(f32[192,128,640]{2,1,0:T(8,128)} %broadcast_select_fusion.2, f32[192,16,640]{2,1,0:T(8,128)S(1)} %bitcast.596, f32[16,640]{1,0:T(8,128)S(1)} %get-tuple-element.383), kind=kOutput, calls=%fused_computation.188 | convolution fusion | flops 3022258176 | bytes 71606272 | tf_op jit(solution)/shard_map/jvp()/while/body/eval_jaxpr/dot_general | solution.py:85
  1464.8 64.9 %fusion.83 = bf16[192,16,128]{2,1,0:T(8,128)(2,1)S(1)} fusion(f32[192,128,640]{2,1,0:T(8,128)} %broadcast_select_fusion.2, f32[192,16,640]{2,1,0:T(8,128)S(1)} %get-tuple-element.277, f32[16,640]{1,0:T(8,128)S(1)} %get-tuple-element.381), kind=kOutput, calls=%fused_computation.186 | convolution fusion | flops 3022258176 | bytes 71606272 | tf_op jit(solution)/shard_map/jvp()/while/body/eval_jaxpr/dot_general | solution.py:85
  1547.2 8.0 fusion.182
  1563.3 8.1 fusion.183
  1571.4 10.5 multiply_convert_fusion
  1595.2 8.1 fusion.180
  1606.0 10.1 all-to-all-done.2
  1619.9 8.0 fusion.181
  1629.1 10.8 multiply_convert_fusion.2
  1644.9 7.8 convolution_convert_fusion.3
  1654.9 7.2 convolution_convert_fusion.2
  1671.9 40.5 %broadcast_multiply_fusion = f32[192,16,640]{2,1,0:T(8,128)} fusion(f32[16,640]{1,0:T(8,128)S(1)} %get-tuple-element.378, f32[192,16,128]{2,1,0:T(8,128)S(1)} %bitcast.599, f32[192,128,640]{2,1,0:T(8,128)} %broadcast_select_fusion.3), kind=kOutput, calls=%fused_computation.72 | convolution fusion | flops 3021864960 | bytes 72392704 | tf_op jit(solution)/shard_map/transpose(jvp())/while/body/eval_jaxpr/checkpoint/dot_general | solution.py:85
  1712.5 40.1 %broadcast_multiply_fusion.1 = f32[192,16,640]{2,1,0:T(8,128)} fusion(f32[16,640]{1,0:T(8,128)S(1)} %get-tuple-element.377, f32[192,16,128]{2,1,0:T(8,128)S(1)} %bitcast.597, f32[192,128,640]{2,1,0:T(8,128)} %broadcast_select_fusion.2), kind=kOutput, calls=%fused_computation.74 | convolution fusion | flops 3021864960 | bytes 72392704 | tf_op jit(solution)/shard_map/transpose(jvp())/while/body/eval_jaxpr/checkpoint/dot_general | solution.py:85
  1768.7 9.9 all-to-all-done.7
  1785.0 39.8 %broadcast_multiply_fusion.2 = f32[192,16,640]{2,1,0:T(8,128)S(1)} fusion(f32[16,640]{1,0:T(8,128)S(1)} %get-tuple-element.380, f32[192,16,128]{2,1,0:T(8,128)S(1)} %bitcast.603, f32[192,128,640]{2,1,0:T(8,128)} %broadcast_select_fusion.3), kind=kOutput, calls=%fused_computation.76 | convolution fusion | flops 3021864960 | bytes 72392704 | tf_op jit(solution)/shard_map/transpose(jvp())/while/body/eval_jaxpr/checkpoint/dot_general | solution.py:85
  1824.9 39.2 %broadcast_multiply_fusion.3 = f32[192,16,640]{2,1,0:T(8,128)S(1)} fusion(f32[16,640]{1,0:T(8,128)S(1)} %get-tuple-element.379, f32[192,16,128]{2,1,0:T(8,128)S(1)} %bitcast.601, f32[192,128,640]{2,1,0:T(8,128)} %broadcast_select_fusion.2), kind=kOutput, calls=%fused_computation.78 | convolution fusion | flops 3021864960 | bytes 72392704 | tf_op jit(solution)/shard_map/transpose(jvp())/while/body/eval_jaxpr/checkpoint/dot_general | solution.py:85
  1877.7 17.6 all-to-all-done.8
  1925.4 8.0 fusion.186
  1933.4 12.4 convolution_add_fusion.1
  1947.4 8.0 fusion.187
  1955.4 12.4 convolution_add_fusion
  1977.7 54.1 %fusion.27 = f32[192,128,640]{2,1,0:T(8,128)} fusion(f32[192,16,128]{2,1,0:T(8,128)S(1)} %bitcast.604, f32[192,16,640]{2,1,0:T(8,128)S(1)} %get-tuple-element.267, f32[16,640]{1,0:T(8,128)S(1)} %copy-done.46), kind=kOutput, calls=%fused_computation.51 | convolution fusion | flops 3021864960 | bytes 72392704 | tf_op jit(solution)/shard_map/transpose(jvp())/while/body/eval_jaxpr/checkpoint/dot_general | solution.py:85
  2031.8 61.0 %add_select_fusion = f32[192,128,640]{2,1,0:T(8,128)} fusion(f32[192,128,640]{2,1,0:T(8,128)} %fusion.27, pred[128,640]{1,0:T(8,128)(4,1)S(1)} %copy-done.64, f32[192,16,128]{2,1,0:T(8,128)S(1)} %bitcast.600, f32[192,16,640]{2,1,0:T(8,128)S(1)} %get-tuple-element.257, f32[16,640]{1,0:T(8,128)S(1)} %copy-done.62), kind=kOutput, calls=%fused_computation.4 | convolution fusion | flops 3053322240 | bytes 135389184 | tf_op jit(solution)/shard_map/transpose(jvp())/while/body/eval_jaxpr/checkpoint/dot_general | solution.py:85
  2092.8 86.4 %copy.210 = f32[192,128,640]{0,2,1:T(8,128)} copy(f32[192,128,640]{2,1,0:T(8,128)} %add_select_fusion) | data formatting | bytes 125829120 | tf_op jit(solution)/shard_map/transpose(jvp())/reshape | solution.py:61
  2179.3 56.0 %fusion.30 = f32[192,128,640]{2,1,0:T(8,128)} fusion(f32[192,16,128]{2,1,0:T(8,128)S(1)} %bitcast.602, f32[192,16,640]{2,1,0:T(8,128)} %copy-done.17, f32[16,640]{1,0:T(8,128)S(1)} %copy-done.44), kind=kOutput, calls=%fused_computation.54 | convolution fusion | flops 3021864960 | bytes 72392704 | tf_op jit(solution)/shard_map/transpose(jvp())/while/body/eval_jaxpr/checkpoint/dot_general | solution.py:85
  2235.3 61.4 %add_select_fusion.1 = f32[192,128,640]{2,1,0:T(8,128)} fusion(f32[192,128,640]{2,1,0:T(8,128)} %fusion.30, pred[128,640]{1,0:T(8,128)(4,1)S(1)} %copy-done.66, f32[192,16,128]{2,1,0:T(8,128)S(1)} %bitcast.598, f32[192,16,640]{2,1,0:T(8,128)} %copy-done.16, f32[16,640]{1,0:T(8,128)S(1)} %copy-done.60), kind=kOutput, calls=%fused_computation.5 | convolution fusion | flops 3053322240 | bytes 135389184 | tf_op jit(solution)/shard_map/transpose(jvp())/while/body/eval_jaxpr/checkpoint/dot_general | solution.py:85
  2296.8 86.3 %copy.209 = f32[192,128,640]{0,2,1:T(8,128)} copy(f32[192,128,640]{2,1,0:T(8,128)} %add_select_fusion.1) | data formatting | bytes 125829120 | tf_op jit(solution)/shard_map/transpose(jvp())/reshape | solution.py:61
  2383.1 458.8 %scatter_custom_fusion.1 = f32[192,512]{0,1:T(8,128)S(1)} fusion(s32[81920]{0:T(1024)} %get-tuple-element.309, f32[81920,192]{1,0:T(8,128)} %bitcast.115, f32[]{:T(128)} %constant.105.clone.1), kind=kCustom, calls=%fused_computation.276 | custom fusion | flops 15728640 | bytes 393728 | tf_op jit(solution)/shard_map/transpose(jvp(jit(_take)))/scatter-add | solution.py:61
  2841.9 458.9 %scatter_custom_fusion = f32[192,512]{0,1:T(8,128)S(1)} fusion(s32[81920]{0:T(1024)} %get-tuple-element.311, f32[81920,192]{1,0:T(8,128)} %bitcast.111, f32[]{:T(128)} %constant.105.clone.1), kind=kCustom, calls=%fused_computation.278 | custom fusion | flops 15728640 | bytes 393728 | tf_op jit(solution)/shard_map/transpose(jvp(jit(_take)))/scatter-add | solution.py:61
  3301.4 186.1 %multiply_reduce_fusion.1 = (f32[192,64]{1,0:T(8,128)S(1)}, f32[192,64]{1,0:T(8,128)S(1)}) fusion(f32[192,512]{1,0:T(8,128)S(1)} %copy.215, f32[192,64]{1,0:T(8,128)S(1)} %copy-done.102, f32[192,64]{1,0:T(8,128)S(1)} %copy-done.94, f32[192,64]{1,0:T(8,128)S(1)} %copy-done.92, f32[512]{0:T(512)S(1)} %copy-done.144, f32[192,64]{1,0:T(8,128)S(1)} %copy-done.106, ...), kind=kLoop, calls=%fused_computation.41 | loop fusion | flops 75472896 | bytes 1181696
  3488.4 239.4 %fusion.9 = (f32[192,64]{1,0:T(8,128)S(1)}, f32[192,64]{1,0:T(8,128)S(1)}, f32[192,64]{1,0:T(8,128)S(1)}, f32[192,64]{1,0:T(8,128)S(1)}, f32[192,64]{1,0:T(8,128)S(1)}, /*index=5*/f32[192,64]{1,0:T(8,128)S(1)}) fusion(f32[192,512]{1,0:T(8,128)S(1)} %copy.215, f32[192,64]{1,0:T(8,128)S(1)} %copy-done.100, f32[192,64]{1,0:T(8,128)S(1)} %copy-done.102, ...), kind=kLoop, calls=%fused_computation.23 | loop fusion | flops 201252864 | bytes 1476608 | tf_op jit(solution)/shard_map/transpose(jvp())/reduce_sum | solution.py:46
  3745.6 15.6 all-reduce.32
  3761.4 10.5 all-reduce.33
  3773.9 126.7 %all-reduce.38.cloned.1.call-done = (f32[96,3072]{1,0:T(8,128)}, f32[96,1536]{1,0:T(8,128)}, f32[192,3072]{1,0:T(8,128)}, f32[192,3072]{1,0:T(8,128)}, f32[384,7...) async-done(((f32[96,3072]{1,0:T(8,128)}, f32[96,1536]{1,0:T(8,128)}, f32[192,3072]{1,0:T(8,128)}, f32[192,3072]{1,0:T(8,128)}, ...) | async-done | bytes 7962640 | tf_op jit(solution)/shard_map/psum | solution.py:260
  (580 shorter events, 228.7 us)
Async XLA Ops:
  7.2 1189.0 %all-gather.6.cloned.1.call-start = ((), (), s32[]{:S(2)}) async-start(), calls=%async_computation.17 | async-start | bytes 2654208 | tf_op jit(solution)/shard_map/all_gather | solution.py:180
  7.9 1530.4 %all-gather.12.cloned.1.call-start = ((), (), s32[]{:S(2)}) async-start(), calls=%async_computation.20 | async-start | bytes 5308416 | tf_op jit(solution)/shard_map/all_gather | solution.py:179
  8.7 1538.5 %all-gather.8.cloned.1.call-start = ((), (), s32[]{:S(2)}) async-start(), calls=%async_computation.18 | async-start | bytes 10616832 | tf_op jit(solution)/shard_map/all_gather | solution.py:181
  9.4 1553.9 %all-gather.10.cloned.1.call-start = ((), (), s32[]{:S(2)}) async-start(), calls=%async_computation.19 | async-start | bytes 10616832 | tf_op jit(solution)/shard_map/all_gather | solution.py:182
  10.0 1561.4 %all-gather.14.cloned.1.call-start = ((), (), s32[]{:S(2)}) async-start(), calls=%async_computation.21 | async-start | bytes 5308416 | tf_op jit(solution)/shard_map/all_gather | solution.py:183
  17.4 178.5 %copy-start.99 = (f32[192,64]{1,0:T(8,128)}, f32[192,64]{1,0:T(8,128)S(1)}, u32[]{:S(2)}) copy-start(f32[192,64]{1,0:T(8,128)S(1)} %copy.214) | copy-start | bytes 147460
  17.5 178.4 %copy-start.101 = (f32[192,64]{1,0:T(8,128)}, f32[192,64]{1,0:T(8,128)S(1)}, u32[]{:S(2)}) copy-start(f32[192,64]{1,0:T(8,128)S(1)} %copy.159) | copy-start | bytes 147460
  17.7 178.3 %copy-start.73 = (f32[1,192,64]{2,1,0:T(8,128)}, f32[1,192,64]{2,1,0:T(8,128)S(1)}, u32[]{:S(2)}) copy-start(f32[1,192,64]{2,1,0:T(8,128)S(1)} %copy.212) | copy-start | bytes 147460
  17.8 178.2 %copy-start.75 = (f32[1,192,64]{2,1,0:T(8,128)}, f32[1,192,64]{2,1,0:T(8,128)S(1)}, u32[]{:S(2)}) copy-start(f32[1,192,64]{2,1,0:T(8,128)S(1)} %copy.211) | copy-start | bytes 147460
  17.9 178.1 %copy-start.103 = (f32[192,64]{1,0:T(8,128)}, f32[192,64]{1,0:T(8,128)S(1)}, u32[]{:S(2)}) copy-start(f32[192,64]{1,0:T(8,128)S(1)} %copy.213) | copy-start | bytes 147460
  18.0 178.0 %copy-start.105 = (f32[192,64]{1,0:T(8,128)}, f32[192,64]{1,0:T(8,128)S(1)}, u32[]{:S(2)}) copy-start(f32[192,64]{1,0:T(8,128)S(1)} %copy.155) | copy-start | bytes 147460
  18.0 177.9 %copy-start.91 = (f32[192,64]{1,0:T(8,128)}, f32[192,64]{1,0:T(8,128)S(1)}, u32[]{:S(2)}) copy-start(f32[192,64]{1,0:T(8,128)S(1)} %get-tuple-element.321) | copy-start | bytes 147460
  18.1 177.9 %copy-start.93 = (f32[192,64]{1,0:T(8,128)}, f32[192,64]{1,0:T(8,128)S(1)}, u32[]{:S(2)}) copy-start(f32[192,64]{1,0:T(8,128)S(1)} %get-tuple-element.322) | copy-start | bytes 147460
  18.1 177.9 %copy-start.95 = (f32[192,64]{1,0:T(8,128)}, f32[192,64]{1,0:T(8,128)S(1)}, u32[]{:S(2)}) copy-start(f32[192,64]{1,0:T(8,128)S(1)} %get-tuple-element.390) | copy-start | bytes 147460
  18.1 177.9 %copy-start.97 = (f32[192,64]{1,0:T(8,128)}, f32[192,64]{1,0:T(8,128)S(1)}, u32[]{:S(2)}) copy-start(f32[192,64]{1,0:T(8,128)S(1)} %get-tuple-element.391) | copy-start | bytes 147460
  196.2 306.4 %copy-start.86 = (pred[81920]{0:T(1024)(128)(4,1)S(1)}, pred[81920]{0:T(1024)(128)(4,1)}, u32[]{:S(2)}) copy-start(pred[81920]{0:T(1024)(128)(4,1)} %compare_and_fusion.1) | copy-start | bytes 245764
  557.0 116.3 %copy-start.67 = (s32[81920]{0:T(1024)S(1)}, s32[81920]{0:T(1024)}, u32[]{:S(2)}) copy-start(s32[81920]{0:T(1024)} %get-tuple-element.312) | copy-start | bytes 983044
  635.4 344.3 %copy-start.131 = (f32[256]{0:T(256)}, f32[256]{0:T(256)S(1)}, u32[]{:S(2)}) copy-start(f32[256]{0:T(256)S(1)} %get-tuple-element.196) | copy-start | bytes 3076
  673.3 306.4 %copy-start.85 = (pred[81920]{0:T(1024)(128)(4,1)S(1)}, pred[81920]{0:T(1024)(128)(4,1)}, u32[]{:S(2)}) copy-start(pred[81920]{0:T(1024)(128)(4,1)} %compare_and_fusion) | copy-start | bytes 245764
  1201.2 24.5 all-to-all-start.3
  1225.7 24.5 all-to-all-start
  1324.7 208.5 %all-to-all-start.4 = ((bf16[8,256,192]{1,2,0:T(8,128)(2,1)}), bf16[8,256,192]{1,2,0:T(8,128)(2,1)S(1)}, u32[]{:S(2)}, u32[]{:S(2)}) async-start(bf16[8,256,192]{1,2,0:T(8,128)(2,1)} %bitcast.570), calls=%async_computation.4 | async-start | bytes 1572864 | tf_op jit(solution)/shard_map/all_to_all | solution.py:205
  1533.2 26.0 all-to-all-start.5
  1559.2 30.7 all-to-all-start.1
  1590.0 26.2 all-to-all-start.2
  1616.1 24.6 all-to-all-start.9
  1640.8 25.1 all-to-all-start.10
  1665.8 86.7 %all-to-all-start.6 = ((bf16[256,8,192]{0,2,1:T(8,128)(2,1)}), bf16[256,8,192]{0,2,1:T(8,128)(2,1)}, u32[]{:S(2)}, u32[]{:S(2)}) async-start(bf16[256,8,192]{0,2,1:T(8,128)(2,1)} %bitcast.62), calls=%async_computation.6 | async-start | bytes 1572864 | tf_op jit(solution)/shard_map/all_to_all | solution.py:227
  1752.6 26.0 all-to-all-start.7
  1778.6 90.6 %all-to-all-start.11 = ((bf16[8,256,192]{1,2,0:T(8,128)(2,1)}), bf16[8,256,192]{1,2,0:T(8,128)(2,1)}, u32[]{:S(2)}, u32[]{:S(2)}) async-start(bf16[8,256,192]{1,2,0:T(8,128)(2,1)} %bitcast.567), calls=%async_computation.11 | async-start | bytes 1572864 | tf_op jit(solution)/shard_map/all_to_all | solution.py:233
  1869.2 26.0 all-to-all-start.8
  1874.3 1855.0 %reduce-scatter.8.cloned.1.call-start = ((), (), s32[]{:S(2)}) async-start(), calls=%async_computation.23 | async-start | bytes 5308416 | tf_op jit(solution)/shard_map/reduce_scatter | solution.py:247
  1907.3 1822.0 %reduce-scatter.6.cloned.1.call-start = ((), (), s32[]{:S(2)}) async-start(), calls=%async_computation.22 | async-start | bytes 10616832 | tf_op jit(solution)/shard_map/reduce_scatter | solution.py:246
  1915.6 1813.7 %reduce-scatter.14.cloned.1.call-start = ((), (), s32[]{:S(2)}) async-start(), calls=%async_computation.26 | async-start | bytes 10616832 | tf_op jit(solution)/shard_map/reduce_scatter | solution.py:250
  1923.8 1805.6 %reduce-scatter.10.cloned.1.call-start = ((), (), s32[]{:S(2)}) async-start(), calls=%async_computation.24 | async-start | bytes 21233664 | tf_op jit(solution)/shard_map/reduce_scatter | solution.py:248
  1945.8 1783.5 %reduce-scatter.12.cloned.1.call-start = ((), (), s32[]{:S(2)}) async-start(), calls=%async_computation.25 | async-start | bytes 21233664 | tf_op jit(solution)/shard_map/reduce_scatter | solution.py:249
  1967.8 1932.7 %all-reduce.38.cloned.1.call-start = ((), (), s32[]{:S(2)}) async-start(), calls=%async_computation.27 | async-start | bytes 16384000 | tf_op jit(solution)/shard_map/psum | solution.py:260
  2383.0 918.3 %copy-start.92 = (f32[192,64]{1,0:T(8,128)S(1)}, f32[192,64]{1,0:T(8,128)}, u32[]{:S(2)}) copy-start(f32[192,64]{1,0:T(8,128)} %copy-done.91) | copy-start | bytes 147460
  2383.0 918.3 %copy-start.94 = (f32[192,64]{1,0:T(8,128)S(1)}, f32[192,64]{1,0:T(8,128)}, u32[]{:S(2)}) copy-start(f32[192,64]{1,0:T(8,128)} %copy-done.93) | copy-start | bytes 147460
  2383.0 918.3 %copy-start.96 = (f32[192,64]{1,0:T(8,128)S(1)}, f32[192,64]{1,0:T(8,128)}, u32[]{:S(2)}) copy-start(f32[192,64]{1,0:T(8,128)} %copy-done.95) | copy-start | bytes 147460
  2383.0 918.3 %copy-start.98 = (f32[192,64]{1,0:T(8,128)S(1)}, f32[192,64]{1,0:T(8,128)}, u32[]{:S(2)}) copy-start(f32[192,64]{1,0:T(8,128)} %copy-done.97) | copy-start | bytes 147460
  2383.1 918.3 %copy-start.102 = (f32[192,64]{1,0:T(8,128)S(1)}, f32[192,64]{1,0:T(8,128)}, u32[]{:S(2)}) copy-start(f32[192,64]{1,0:T(8,128)} %copy-done.101) | copy-start | bytes 147460
  2383.1 918.3 %copy-start.106 = (f32[192,64]{1,0:T(8,128)S(1)}, f32[192,64]{1,0:T(8,128)}, u32[]{:S(2)}) copy-start(f32[192,64]{1,0:T(8,128)} %copy-done.105) | copy-start | bytes 147460
  2383.1 918.3 %copy-start.144 = (f32[512]{0:T(512)S(1)}, f32[512]{0:T(512)}, u32[]{:S(2)}) copy-start(f32[512]{0:T(512)} %copy-done.143) | copy-start | bytes 6148
  3301.4 187.0 %copy-start.100 = (f32[192,64]{1,0:T(8,128)S(1)}, f32[192,64]{1,0:T(8,128)}, u32[]{:S(2)}) copy-start(f32[192,64]{1,0:T(8,128)} %copy-done.99) | copy-start | bytes 147460
  3301.4 187.0 %copy-start.104 = (f32[192,64]{1,0:T(8,128)S(1)}, f32[192,64]{1,0:T(8,128)}, u32[]{:S(2)}) copy-start(f32[192,64]{1,0:T(8,128)} %copy-done.103) | copy-start | bytes 147460
  3488.4 239.5 %copy-start.76 = (f32[1,192,64]{2,1,0:T(8,128)S(1)}, f32[1,192,64]{2,1,0:T(8,128)}, u32[]{:S(2)}) copy-start(f32[1,192,64]{2,1,0:T(8,128)} %copy-done.75) | copy-start | bytes 147460
  3488.4 239.5 %copy-start.74 = (f32[1,192,64]{2,1,0:T(8,128)S(1)}, f32[1,192,64]{2,1,0:T(8,128)}, u32[]{:S(2)}) copy-start(f32[1,192,64]{2,1,0:T(8,128)} %copy-done.73) | copy-start | bytes 147460
  (134 other events, 3163.0 us)
Sparse Core Ops, SparseCore 0:
  9.7 34.3 all-gather.5
  45.7 50.8 all-gather.11
  98.2 89.5 all-gather.7
  189.3 89.2 all-gather.9
  280.0 50.1 all-gather.13
  1907.5 53.8 reduce-scatter.7
  1963.7 97.8 reduce-scatter.5
  2063.9 97.8 reduce-scatter.13
  2164.1 186.3 reduce-scatter.9
  2352.7 186.3 reduce-scatter.11
  3729.5 171.0 all-reduce.37
where the time goes:
time: 3930 us; the launch traced here: 3920 us
  other arithmetic  1750 us (45%)
  local copies, waits for them, and re-layouts  1020 us (26%)
  matrix products  817 us (21%)
  waiting for transfers between devices  210 us (5%)
  blocking collectives  56.3 us (1%)
  starting transfers between devices  53.4 us (1%)
    scatter-add x2, other arithmetic, banded(): jnp.take(kernel_rows, safe_lag.reshape(-1), axis=1)  918 us
    dot_general x12, matrix products, apply_items(): lax.dot_general(matrix, masked, (((2,), (2,)), ((0,), (0,))), precision=H...  652 us
    gather x2, local copies, waits for them, and re-layouts, banded(): jnp.take(kernel_rows, safe_lag.reshape(-1), axis=1)  613 us
    unnamed x11, other arithmetic  366 us
    reshape x4, local copies, waits for them, and re-layouts, banded(): jnp.take(kernel_rows, safe_lag.reshape(-1), axis=1)  328 us
    reduce_sum x1, other arithmetic, one_side(): angular[:, :, None] * lag_steps  239 us
    psum x1, waiting for transfers between devices, shards(): lax.psum((summed[0], summed[1], summed[2], summed[3], summed[4], summed[5...  127 us
    select_n x4, other arithmetic, banded(): jnp.take(kernel_rows, safe_lag.reshape(-1), axis=1)  110 us
  transfers between devices with their start and end apart: 23, of which 9 were waited for; matrix products, arithmetic and copies ran while one was open for 90% of the time, Pallas kernels for 0%

commit v1 on v0

v1 whole, which is shorter than its diff:
```python
import functools

import numpy as np

import jax
import jax.numpy as jnp
from jax import lax
from jax.experimental import pallas as pl
from jax.experimental.pallas import tpu as pltpu
from jax.sharding import PartitionSpec as P

MESH = pl.DeviceIdType.MESH
LONG = 512
EPSILON = 1e-05
HIGHEST = lax.Precision.HIGHEST
LOW = jnp.bfloat16
F32 = jnp.float32


BLK = 128
REACH = 3


def wave_tables():
    k = np.arange(BLK)[:, None] + 0.5
    n = np.arange(-BLK, BLK)[None, :]
    angle = 2 * np.pi * k * n / (2 * BLK)
    return np.concatenate([np.cos(angle), -np.sin(angle)], 0).astype(np.float32)


def dot(a, b, ca, cb):
    return lax.dot_general(a, b, (((ca,), (cb,)), ((), ())), preferred_element_type=jnp.float32)


def kernel_spectra(wave_ref, kern_ref, spec_ref, tile):
    for side in range(2):
        rows = jnp.concatenate([kern_ref[a, b, side] for a in range(kern_ref.shape[0]) for b in range(kern_ref.shape[1])], 0)
        spec_ref[side, 0] = dot(wave_ref[:, BLK:], rows[:, :BLK], 1, 1)
        for d in range(1, REACH + 1):
            spec_ref[side, d] = dot(wave_ref[...], rows[:, (d - 1) * BLK:(d + 1) * BLK], 1, 1)


def block_of(parts, micro, at):
    for p in parts:
        n = p.shape[1] // BLK
        if at < n:
            return p[micro, at * BLK:(at + 1) * BLK]
        at -= n


def fore_kernel(mask_ref, wave_ref, kern_ref, *refs):
    parts = refs[:5]
    fore_ref, back_ref, spec_ref, x_ref, y_ref = refs[5:]
    tile = fore_ref.shape[-1]
    kernel_spectra(wave_ref, kern_ref, spec_ref, tile)
    fwd = wave_ref[:, BLK:]
    for micro in range(2):
        for b in range(8):
            x_ref[b] = dot(fwd, block_of(parts, micro, b), 1, 0)

        @pl.loop(0, BLK // 8)
        def _(r):
            re = pl.ds(pl.multiple_of(r * 8, 8), 8)
            im = pl.ds(pl.multiple_of(r * 8 + BLK, 8), 8)
            for lane in range(tile // 128):
                ln = slice(lane * 128, lane * 128 + 128)
                xr = [x_ref[b, re, ln] for b in range(8)]
                xi = [x_ref[b, im, ln] for b in range(8)]
                for side in range(2):
                    cr = [spec_ref[side, d, re, ln] for d in range(4)]
                    ci = [spec_ref[side, d, im, ln] for d in range(4)]
                    for own in range(2):
                        yr = yi = None
                        for d in range(4):
                            at = own + 3 + (d if side else -d)
                            pr = cr[d] * xr[at]
                            pi = cr[d] * xi[at]
                            qr = ci[d] * xi[at]
                            qi = ci[d] * xr[at]
                            if side:
                                tr, ti = pr + qr, pi - qi
                            else:
                                tr, ti = pr - qr, pi + qi
                            if d:
                                m = mask_ref[(micro * 2 + own) * 7 + 3 + (d if side else -d)]
                                tr, ti = tr * m, ti * m
                            yr = tr if yr is None else yr + tr
                            yi = ti if yi is None else yi + ti
                        y_ref[side, own, re, ln] = yr
                        y_ref[side, own, im, ln] = yi
        for own in range(2):
            for side, o in ((0, fore_ref), (1, back_ref)):
                y = dot(fwd, y_ref[side, own].astype(jnp.bfloat16), 0, 0)
                o[micro, own * BLK:(own + 1) * BLK] = (y * (1.0 / BLK)).astype(jnp.bfloat16)


def back_kernel(mask_ref, wave_ref, kern_ref, *refs):
    parts = refs[:5]
    fparts = refs[5:8]
    bparts = refs[8:11]
    gfil_ref, gk_ref, spec_ref, x_ref, f_ref, b_ref, y_ref, r_ref = refs[11:]
    tile = gfil_ref.shape[-1]
    kernel_spectra(wave_ref, kern_ref, spec_ref, tile)
    fwd = wave_ref[:, BLK:]
    for micro in range(2):
        for b in range(8):
            x_ref[b] = dot(fwd, block_of(parts, micro, b), 1, 0)
        for b in range(5):
            f_ref[b] = dot(fwd, block_of(fparts, micro, b), 1, 0)
            b_ref[b] = dot(fwd, block_of(bparts, micro, b), 1, 0)

        @pl.loop(0, BLK // 8)
        def _(r):
            re = pl.ds(pl.multiple_of(r * 8, 8), 8)
            im = pl.ds(pl.multiple_of(r * 8 + BLK, 8), 8)
            for lane in range(tile // 128):
                ln = slice(lane * 128, lane * 128 + 128)
                fr = [f_ref[b, re, ln] for b in range(5)]
                fi = [f_ref[b, im, ln] for b in range(5)]
                gr = [b_ref[b, re, ln] for b in range(5)]
                gi = [b_ref[b, im, ln] for b in range(5)]
                acc = [[None, None], [None, None]]
                for d in range(4):
                    for side in range(2):
                        cr = spec_ref[side, d, re, ln]
                        ci = spec_ref[side, d, im, ln]
                        for own in range(2):
                            if side == 0:
                                vr, vi = fr[own + d], fi[own + d]
                                tr, ti = cr * vr + ci * vi, cr * vi - ci * vr
                                e = d
                            else:
                                vr, vi = gr[own + 3 - d], gi[own + 3 - d]
                                tr, ti = cr * vr - ci * vi, cr * vi + ci * vr
                                e = -d
                            if d:
                                m = mask_ref[(micro * 2 + own) * 7 + 3 + e]
                                tr, ti = tr * m, ti * m
                            a = acc[own]
                            acc[own] = [tr if a[0] is None else a[0] + tr, ti if a[1] is None else a[1] + ti]
                for own in range(2):
                    y_ref[own, re, ln] = acc[own][0]
                    y_ref[own, im, ln] = acc[own][1]
                for side in range(2):
                    for d in range(4):
                        sr = si = None
                        for own in range(2):
                            e = d if side else -d
                            xr, xi = x_ref[own + 3 + e, re, ln], x_ref[own + 3 + e, im, ln]
                            if side == 0:
                                vr, vi = fr[own], fi[own]
                                tr, ti = vr * xr + vi * xi, vi * xr - vr * xi
                            else:
                                vr, vi = gr[own + 3], gi[own + 3]
                                tr, ti = vr * xr + vi * xi, vr * xi - vi * xr
                            if d:
                                m = mask_ref[(micro * 2 + own) * 7 + 3 + e]
                                tr, ti = tr * m, ti * m
                            sr = tr if sr is None else sr + tr
                            si = ti if si is None else si + ti
                        if micro:
                            sr = sr + r_ref[side, d, re, ln]
                            si = si + r_ref[side, d, im, ln]
                        r_ref[side, d, re, ln] = sr
                        r_ref[side, d, im, ln] = si
        for own in range(2):
            y = dot(fwd, y_ref[own].astype(jnp.bfloat16), 0, 0)
            gfil_ref[micro, own * BLK:(own + 1) * BLK] = (y * (1.0 / BLK)).astype(jnp.bfloat16)
    A, B = gk_ref.shape[:2]
    for side in range(2):
        rows = [dot(r_ref[side, d].astype(jnp.bfloat16), wave_ref[:, BLK:] if d == 0 else wave_ref[...], 0, 0) for d in range(4)]
        for d in range(4):
            seg = rows[d][:, -BLK:]
            if d < 3:
                seg = seg + rows[d + 1][:, :BLK]
            seg = (seg * (1.0 / BLK)).astype(jnp.bfloat16)
            w = tile // (A * B)
            for a in range(A):
                for b in range(B):
                    at = (a * B + b) * w
                    gk_ref[a, b, side, :, d * BLK:(d + 1) * BLK] = seg[at:at + w]


def _specs(parts, tile):
    return [pl.BlockSpec((2, p.shape[1], tile), lambda i: (0, 0, i)) for p in parts]


def conv_call(body, mask, wave, kern, parts, outs, scratch, step):
    channels = parts[0].shape[-1]
    steps = kern.shape[0] // step
    tile = channels // steps
    kspec = pl.BlockSpec((step,) + kern.shape[1:], lambda i: (i, 0, 0, 0, 0))
    out_specs = []
    for o in outs:
        if len(o.shape) == 3:
            out_specs.append(pl.BlockSpec((2, o.shape[1], tile), lambda i: (0, 0, i)))
        else:
            out_specs.append(kspec)
    return pl.pallas_call(
        body,
        grid=(steps,),
        out_shape=outs,
        in_specs=[pl.BlockSpec(memory_space=pltpu.SMEM), pl.BlockSpec(memory_space=pltpu.VMEM), kspec] + _specs(parts, tile),
        out_specs=out_specs,
        scratch_shapes=[pltpu.VMEM(sh + (tile,), jnp.float32) for sh in scratch],
        compiler_params=pltpu.CompilerParams(vmem_limit_bytes=56 * 2**20),
        cost_estimate=pl.CostEstimate(flops=10**10, bytes_accessed=3 * 10**7, transcendentals=0),
    )(mask, wave, kern, *parts)


def conv_forward(mask, wave, kern, parts, step):
    own = parts[2]
    sh = jax.ShapeDtypeStruct(own.shape, jnp.bfloat16)
    return conv_call(fore_kernel, mask, wave, kern, parts, [sh, sh], [(2, 4, 256), (8, 256), (2, 2, 256)], step)


def conv_backward(mask, wave, kern, parts, fparts, bparts, step):
    own = parts[2]
    return conv_call(back_kernel, mask, wave, kern, list(parts) + list(fparts) + list(bparts),
                     [jax.ShapeDtypeStruct(own.shape, jnp.bfloat16), jax.ShapeDtypeStruct(kern.shape, jnp.bfloat16)],
                     [(2, 4, 256), (8, 256), (5, 256), (5, 256), (2, 256), (2, 4, 256)], step)


AHEAD = 1
L2 = 2
L3 = 4

def place(n_z):
    dp = lax.axis_index("dp"); s = lax.axis_index("seq")
    return dp, s, s // 2, lax.rem(s, 2)

def cut(ref, geom, q, h=None):
    kind = geom
    R, C = ref.shape[-2:]
    if kind == "col":
        cols = pl.ds(pl.multiple_of(q * (C // 4), 128), C // 4)
        rows = slice(None) if h is None else pl.ds(h * (R // 2), R // 2)
        return ref.at[rows, cols]
    if kind == "row":
        n = R // 4
        if h is None:
            return ref.at[pl.ds(pl.multiple_of(q * n, 16), n)]
        return ref.at[pl.ds(pl.multiple_of(q * n + h * (n // 2), 16), n // 2)]

GEOM = {"filter": "col", "kern": "row", "value": "col", "fore": "col", "back": "col", "out": "row"}

def ag_kernel(names, *refs):
    n = len(names)
    src = refs[:n]; out = refs[n:2 * n]
    stage = refs[2 * n:3 * n]
    isem, lsem, zs, zr, xs, xr, ys, yr, fxs, fxr, fys, fyr, ss, sr, ss0, sr0 = refs[3 * n:]
    dp, s, z, c = place(4)
    core = (dp, s + 1 - 2 * c)
    xn = (dp + 1 - 2 * lax.rem(dp, 2), s)
    yn = (lax.rem(dp + 2, 4), s)
    q = dp; qx = xn[0]; qy = yn[0]; qd = lax.rem(qx + 2, 4)
    def zdev(k): return (dp, lax.rem(s + 2 * k, 8))
    bar = pltpu.get_barrier_semaphore()
    for d in [core, xn, yn] + [zdev(k) for k in (1, 2, 3)]:
        pl.semaphore_signal(bar, inc=1, device_id=d, device_id_type=MESH)
    pl.semaphore_wait(bar, 6)

    def rc(a_ref, b_ref, s1, s2, dev):
        return pltpu.make_async_remote_copy(src_ref=a_ref, dst_ref=b_ref, send_sem=s1, recv_sem=s2, device_id=dev, device_id_type=MESH)
    g = [GEOM[m] for m in names]
    sends = []
    locs = []
    lins = []
    zsend = {}
    for a in range(n):
        if names[a] == "kern":
            lc = pltpu.make_async_copy(stage[a], cut(out[a].at[s], g[a], q), lsem.at[a])
        else:
            lc = pltpu.make_async_copy(stage[a], out[a].at[s], lsem.at[a])
        locs.append(lc)
        li = pltpu.make_async_copy(src[a], stage[a], isem.at[a]); li.start(); lins.append(li)
        for k in (1, 2, 3):
            piece = src[a] if names[a] == "kern" else cut(src[a], g[a], q)
            cp = rc(piece, cut(out[a].at[s], g[a], q), zs.at[a, k - 1], zr.at[a, k - 1], zdev(k))
            zsend[a, k] = cp
    def zgo(a):
        if a >= n: return
        for k in (1, 3, 2): zsend[a, k].start()
    def sibgo(a):
        if names[a] != "kern":
            cp = rc(src[a], out[a].at[s], ss0.at[a], sr0.at[a], core)
            cp.start(); sends.append(cp)
    for a in range(AHEAD): zgo(a)
    for a in range(n):
        lins[a].wait(); locs[a].start()
    sibgo(0)
    units = []
    for a in range(n):
        if names[a] == "kern": units.append((a, 0))
        for k in (1, 3, 2): units.append((a, k))
    xc, yc, fx, fy, sb = {}, {}, {}, {}, {}
    def blk(a, k):
        return out[a].at[lax.rem(s + 8 - 2 * k, 8)]
    def st1(u):
        a, k = u
        if k == 0:
            locs[a].wait()
        else:
            zsend[a, k].wait_recv()
        b = cut(blk(a, k), g[a], q)
        xc[u] = rc(b, b, xs.at[a, k], xr.at[a, k], xn); xc[u].start()
        yc[u] = rc(b, b, ys.at[a, k], yr.at[a, k], yn); yc[u].start()
    def st2(u):
        a, k = u
        xc[u].wait_recv()
        b = cut(blk(a, k), g[a], qx, 0)
        fy[u] = rc(b, b, fys.at[a, k], fyr.at[a, k], yn); fy[u].start()
        yc[u].wait_recv()
        b = cut(blk(a, k), g[a], qy, 1)
        fx[u] = rc(b, b, fxs.at[a, k], fxr.at[a, k], xn); fx[u].start()
    def st3(u):
        a, k = u
        fx[u].wait_recv(); fy[u].wait_recv()
        b = blk(a, k)
        sb[u] = rc(b, b, ss.at[a, k], sr.at[a, k], core); sb[u].start()
    for t in range(len(units) + L3):
        if t < len(units):
            st1(units[t])
            if units[t][1] == 2:
                zgo(units[t][0] + AHEAD)
                if units[t][0] + 1 < n: sibgo(units[t][0] + 1)
        if 0 <= t - L2 < len(units): st2(units[t - L2])
        if 0 <= t - L3 < len(units): st3(units[t - L3])
    for u in units:
        a, k = u
        sb[u].wait_recv()
        for d in (xc, yc, fx, fy, sb): d[u].wait_send()
    for cp in zsend.values(): cp.wait_send()
    for cp in sends: cp.wait()
    for a in range(n):
        if names[a] != "kern": locs[a].wait()

def gather_weights(names, arrs):
    n = len(names)
    shapes = []
    for m, a in zip(names, arrs):
        R, C = a.shape
        if m == "kern": R = R * 4
        shapes.append(jax.ShapeDtypeStruct((8, R, C), a.dtype))
    D = pltpu.SemaphoreType.DMA
    outs = pl.pallas_call(
        functools.partial(ag_kernel, names),
        out_shape=shapes,
        in_specs=[pl.BlockSpec(memory_space=pl.ANY)] * n,
        out_specs=[pl.BlockSpec(memory_space=pl.ANY)] * n,
        scratch_shapes=[pltpu.VMEM(a.shape, a.dtype) for a in arrs] + [D((n,)), D((n,)), D((n, 3)), D((n, 3))] + [D((n, 4))] * 10 + [D((n,)), D((n,))],
        compiler_params=pltpu.CompilerParams(collective_id=0, has_side_effects=True),
    )(*arrs)
    return outs


SLOTS = 3
LB, LC, LD, LE = 1, 2, 3, 4

def add_into(dst, srcs):
    R = dst.shape[-2]
    @pl.loop(0, R // 16)
    def _(r):
        rows = pl.ds(pl.multiple_of(r * 16, 16), 16)
        t = dst[rows, :].astype(jnp.float32)
        for s_ in srcs:
            t = t + s_[rows, :].astype(jnp.float32)
        dst[rows, :] = t.astype(jnp.bfloat16)

def rs_kernel(names, *refs):
    n = len(names)
    G = refs[:n]; out = refs[n:2 * n]
    P = refs[2 * n:3 * n]; bx = refs[3 * n:4 * n]; by = refs[4 * n:5 * n]; bc = refs[5 * n:6 * n]
    stg = refs[6 * n]
    lsem, as_, ar, xs, xr, ys, yr, cs, cr, gxs, gxr, gys, gyr, hxs, hxr, hys, hyr, osem = refs[6 * n + 1:]
    dp, s, z, c = place(4)
    core = (dp, s + 1 - 2 * c)
    xn = (dp + 1 - 2 * lax.rem(dp, 2), s)
    yn = (lax.rem(dp + 2, 4), s)
    q = dp; qx = xn[0]; qy = yn[0]; qd = lax.rem(qx + 2, 4)
    def zdev(k): return (dp, lax.rem(s + 2 * k, 8))
    bar = pltpu.get_barrier_semaphore()
    for d in [core, xn, yn] + [zdev(k) for k in (1, 2, 3)]:
        pl.semaphore_signal(bar, inc=1, device_id=d, device_id_type=MESH)
    pl.semaphore_wait(bar, 6)
    def rc(a_ref, b_ref, s1, s2, dev):
        return pltpu.make_async_remote_copy(src_ref=a_ref, dst_ref=b_ref, send_sem=s1, recv_sem=s2, device_id=dev, device_id_type=MESH)
    g = [GEOM[m] for m in names]
    units = [(a, k) for a in range(n) for k in (1, 2, 3, 0)]
    pend = []
    A, X, Y, C, LCP = {}, {}, {}, {}, {}
    def so(k, other):
        base = lax.rem(s + 2 * k, 8)
        return base + 1 - 2 * c if other else base
    def stA(i):
        a, k = units[i]
        A[i] = rc(G[a].at[so(k, True)], P[a].at[k], as_.at[a, k], ar.at[a, k], core); A[i].start()
    def load(i):
        a, k = units[i]
        R, Cc = G[a].shape[-2:]
        LCP[i] = pltpu.make_async_copy(G[a].at[so(k, False)], stg.at[i % SLOTS, pl.ds(0, R), pl.ds(0, Cc)] if False else stg[a].at[i % SLOTS], lsem.at[i % SLOTS])
        LCP[i].start()
    def stB(i):
        a, k = units[i]
        A[i].wait_recv(); LCP[i].wait()
        p = P[a].at[k]
        add_into(p, [stg[a].at[i % SLOTS]])
        X[i, 1] = rc(cut(p, g[a], qd, 0), bx[a].at[k, 1], xs.at[a, k, 1], xr.at[a, k, 1], xn)
        X[i, 0] = rc(cut(p, g[a], qx, 0), bx[a].at[k, 0], xs.at[a, k, 0], xr.at[a, k, 0], xn)
        Y[i, 1] = rc(cut(p, g[a], qd, 1), by[a].at[k, 1], ys.at[a, k, 1], yr.at[a, k, 1], yn)
        Y[i, 0] = rc(cut(p, g[a], qy, 1), by[a].at[k, 0], ys.at[a, k, 0], yr.at[a, k, 0], yn)
        for j in (1, 0): X[i, j].start(); Y[i, j].start()
    def stC(i):
        a, k = units[i]
        p = P[a].at[k]
        X[i, 1].wait_recv()
        add_into(cut(p, g[a], qy, 0), [bx[a].at[k, 1]])
        Y[i, 2] = rc(cut(p, g[a], qy, 0), by[a].at[k, 2], ys.at[a, k, 2], yr.at[a, k, 2], yn); Y[i, 2].start()
        Y[i, 1].wait_recv()
        add_into(cut(p, g[a], qx, 1), [by[a].at[k, 1]])
        X[i, 2] = rc(cut(p, g[a], qx, 1), bx[a].at[k, 2], xs.at[a, k, 2], xr.at[a, k, 2], xn); X[i, 2].start()
    def stD(i):
        a, k = units[i]
        p = P[a].at[k]
        X[i, 0].wait_recv(); Y[i, 2].wait_recv()
        add_into(cut(p, g[a], q, 0), [bx[a].at[k, 0], by[a].at[k, 2]])
        Y[i, 0].wait_recv(); X[i, 2].wait_recv()
        add_into(cut(p, g[a], q, 1), [by[a].at[k, 0], bx[a].at[k, 2]])
        if k:
            C[i] = rc(cut(p, g[a], q), bc[a].at[k - 1], cs.at[a, k - 1], cr.at[a, k - 1], zdev(k)); C[i].start()
    ag = {}
    def stE(a):
        for k in (1, 2, 3): C[units.index((a, k))].wait_recv()
        p = cut(P[a].at[0], g[a], q)
        add_into(p, [bc[a].at[j] for j in range(3)])
        own = out[a] if names[a] == "kern" else cut(out[a], g[a], q)
        o = pltpu.make_async_copy(p, own, osem.at[a]); o.start()
        ag[a, "o"] = o
        if names[a] != "kern":
            ag[a, "x"] = rc(p, own, gxs.at[a], gxr.at[a], xn); ag[a, "x"].start()
            ag[a, "y"] = rc(p, own, gys.at[a], gyr.at[a], yn); ag[a, "y"].start()
    def stF(a):
        if names[a] == "kern": return
        ag[a, "x"].wait_recv()
        b = cut(out[a], g[a], qx, 0)
        ag[a, "fy"] = rc(b, b, hys.at[a], hyr.at[a], yn); ag[a, "fy"].start()
        ag[a, "y"].wait_recv()
        b = cut(out[a], g[a], qy, 1)
        ag[a, "fx"] = rc(b, b, hxs.at[a], hxr.at[a], xn); ag[a, "fx"].start()
    N = len(units)
    for i in range(min(AHEAD_A, N)): stA(i)
    for i in range(min(SLOTS - 1, N)): load(i)
    for t in range(N + LE + 5):
        if t < N:
            if t + AHEAD_A < N: stA(t + AHEAD_A)
            if t + SLOTS - 1 < N: load(t + SLOTS - 1)
            stB(t)
        if 0 <= t - LC < N: stC(t - LC)
        if 0 <= t - LD < N: stD(t - LD)
        j = t - LE
        if 0 <= j < N and j % 4 == 3: stE(j // 4)
        j = t - LE - 2
        if 0 <= j < N and j % 4 == 3: stF(j // 4)
    for a in range(n):
        if names[a] != "kern":
            for w in ("fx", "fy"): ag[a, w].wait()
            for w in ("x", "y"): ag[a, w].wait_send()
        ag[a, "o"].wait()
    for d in (A, X, Y, C):
        for v in d.values(): v.wait_send()
AHEAD_A = 3

def halfshape(m, R, C):
    return (R // 2, C // 4) if GEOM[m] == "col" else (R // 8, C)
def qshape(m, R, C):
    return (R, C // 4) if GEOM[m] == "col" else (R // 4, C)

def reduce_weights(names, arrs):
    n = len(names)
    D = pltpu.SemaphoreType.DMA
    V = lambda sh: pltpu.VMEM(sh, jnp.bfloat16)
    shp = [a.shape[1:] for a in arrs]
    outs = pl.pallas_call(
        functools.partial(rs_kernel, names),
        out_shape=[jax.ShapeDtypeStruct(qshape(m, *sh) if m == "kern" else sh, jnp.bfloat16) for m, sh in zip(names, shp)],
        in_specs=[pl.BlockSpec(memory_space=pl.ANY)] * n,
        out_specs=[pl.BlockSpec(memory_space=pl.ANY)] * n,
        scratch_shapes=[V((4,) + sh) for sh in shp]
        + [V((4, 3) + halfshape(m, *sh)) for m, sh in zip(names, shp)] * 2
        + [V((3,) + qshape(m, *sh)) for m, sh in zip(names, shp)]
        + [[V((SLOTS,) + sh) for sh in shp]]
        + [D((SLOTS,)), D((n, 4)), D((n, 4))] + [D((n, 4, 3))] * 4 + [D((n, 3))] * 2 + [D((n,))] * 9,
        compiler_params=pltpu.CompilerParams(collective_id=1, has_side_effects=True, vmem_limit_bytes=62 * 2**20),
    )(*arrs)
    return outs


STEP_A = 32


def mode_powers(rate, freq):
    coarse = (jnp.arange(LONG // STEP_A) * STEP_A).astype(F32)
    fine = jnp.arange(STEP_A).astype(F32)

    def powers(lags):
        size = jnp.exp(-rate[:, None, :] * lags[None, :, None])
        turn = freq[:, None, :] * lags[None, :, None]
        return size * jnp.cos(turn), size * jnp.sin(turn)

    return powers(coarse), powers(fine)


def make_kernels(coef, rate, freq):
    (ar, ai), (br, bi) = mode_powers(rate, freq)
    weight = (coef * jnp.sqrt(rate))[:, None, :]
    left = jnp.concatenate([weight * ar, -weight * ai], -1)
    right = jnp.concatenate([br, bi], -1)
    rows = jnp.einsum("ran,rbn->rab", left, right, precision=HIGHEST, preferred_element_type=F32)
    return rows.reshape(rows.shape[0], LONG)


def pull_kernels(grad, coef, rate, freq):
    (ar, ai), (br, bi) = mode_powers(rate, freq)
    rows = grad.reshape(grad.shape[0], LONG // STEP_A, STEP_A)
    lags = jnp.arange(LONG).astype(F32).reshape(LONG // STEP_A, STEP_A)
    both = jnp.concatenate([rows, rows * lags[None]], 1)
    fine = jnp.concatenate([br, bi], -1)
    inner = jnp.einsum("rab,rbn->ran", both, fine, precision=HIGHEST, preferred_element_type=F32)
    n = rate.shape[-1]
    a = LONG // STEP_A
    zero_r, zero_i = inner[:, :a, :n], inner[:, :a, n:]
    one_r, one_i = inner[:, a:, :n], inner[:, a:, n:]
    plain = jnp.sum(ar * zero_r - ai * zero_i, 1)
    lag_r = jnp.sum(ar * one_r - ai * one_i, 1)
    lag_i = jnp.sum(ar * one_i + ai * one_r, 1)
    root = jnp.sqrt(rate)
    return root * plain, coef * (plain / (2 * root) - root * lag_r), -coef * root * lag_i


def dot_plain(left_side, right_side):
    return jnp.dot(left_side, right_side, preferred_element_type=F32)


def dot_inner(left_side, right_side):
    return lax.dot_general(left_side, right_side, (((0,), (0,)), ((), ())), preferred_element_type=F32)


def dot_outer(left_side, right_side):
    return lax.dot_general(left_side, right_side, (((1,), (1,)), ((), ())), preferred_element_type=F32)


def layer_norm(rows, gain, bias):
    centre = jnp.mean(rows, axis=-1, keepdims=True)
    shifted = rows - centre
    spread = jnp.mean(shifted * shifted, axis=-1, keepdims=True)
    return shifted * lax.rsqrt(spread + EPSILON) * gain + bias


def shift(array, by, count):
    pairs = [(i, i + by) for i in range(count) if 0 <= i + by < count]
    return lax.ppermute(array, "seq", pairs)


def from_left(array, count):
    return [shift(array[:, BLK:], 2, count), shift(array, 1, count)]


def from_right(array, count):
    return [shift(array, -1, count), shift(array[:, :BLK], -2, count)]


def same_item(lengths, own_blocks, count):
    starts = jnp.cumsum(lengths, axis=1) - lengths
    total = own_blocks * count
    places = jnp.arange(total) * BLK
    present = (starts[:, None, :] <= places[None, :, None]) & (lengths[:, None, :] > 0)
    owner = jnp.sum(present.astype(jnp.int32), -1)
    first = lax.axis_index("seq") * own_blocks
    padded = jnp.pad(owner, ((0, 0), (REACH, REACH)), constant_values=-1)
    near = lax.dynamic_slice_in_dim(padded, first, own_blocks + 2 * REACH, 1)
    return jnp.stack(
        [
            jnp.stack([(near[:, o + REACH] == near[:, o + REACH + e]) for e in range(-REACH, REACH + 1)], -1)
            for o in range(own_blocks)
        ],
        1,
    ).astype(F32)


def shards(
    n_dp,
    n_seq,
    tokens,
    cotangent,
    lengths,
    ln_gain,
    ln_bias,
    w_value,
    w_filter,
    w_fore,
    w_back,
    w_out,
    ssm_coef,
    ssm_rate,
    ssm_freq,
):
    linked = n_dp == 4 and n_seq == 8
    micros, rows_each, width = tokens.shape
    rows = micros * rows_each
    channels = ssm_coef.shape[1]
    modes = ssm_coef.shape[2]
    parts = 4 if linked else 1
    some = channels // parts
    first = lax.axis_index("dp") * some if linked else 0

    def mine(array):
        return lax.dynamic_slice_in_dim(array, first, some, 1).reshape(2 * some, modes)

    coef, rate, freq = mine(ssm_coef), mine(ssm_rate), mine(ssm_freq)
    kernels = make_kernels(coef, rate, freq).astype(LOW)
    if linked:
        own = {"filter": w_filter, "kern": kernels, "value": w_value, "fore": w_fore, "back": w_back, "out": w_out}
        names = tuple(own)
        gathered = dict(zip(names, gather_weights(names, [own[m] for m in names])))
        kern = gathered["kern"].reshape(n_seq, parts, 2, some, LONG)
    else:
        own = {"filter": w_filter, "value": w_value, "fore": w_fore, "back": w_back, "out": w_out}
        gathered = {m: lax.all_gather(a, "seq", axis=0) for m, a in own.items()}
        kern = lax.all_gather(kernels.reshape(1, 2, some, LONG), "seq", axis=0)
    full = {m: a.reshape(-1, a.shape[-1]) for m, a in gathered.items() if m != "kern"}
    gain = lax.all_gather(ln_gain, "seq", axis=0, tiled=True).astype(F32)
    bias = lax.all_gather(ln_bias, "seq", axis=0, tiled=True).astype(F32)
    tile_step = max(1, 384 // channels)
    wave = jnp.asarray(wave_tables(), LOW)
    mask = same_item(lengths[:, 0], rows_each // BLK, n_seq).reshape(-1)

    token_rows = tokens.reshape(rows, width).astype(F32)
    normed, norm_pull = jax.vjp(layer_norm, token_rows, gain, bias)
    normed_low = normed.astype(LOW)
    pre_filter = dot_plain(normed_low, full["filter"])
    filter_act, filter_pull = jax.vjp(jax.nn.gelu, pre_filter)
    filter_low = filter_act.astype(LOW).reshape(micros, rows_each, -1)
    around = from_left(filter_low, n_seq) + [filter_low] + from_right(filter_low, n_seq)
    pre_value = dot_plain(normed_low, full["value"])
    value_act, value_pull = jax.vjp(jax.nn.gelu, pre_value)
    fore_low, back_low = [a.reshape(rows, -1) for a in conv_forward(mask, wave, kern, around, tile_step)]
    proj_fore = dot_plain(fore_low, full["fore"])
    proj_back = dot_plain(back_low, full["back"])
    hidden_low = (proj_fore * proj_back * value_act).astype(LOW)
    mixed = (token_rows + dot_plain(hidden_low, full["out"])).astype(LOW).reshape(tokens.shape)

    cot_rows = cotangent.reshape(rows, width)
    grad_hidden = dot_outer(cot_rows, full["out"])
    grad_proj_fore = (grad_hidden * proj_back * value_act).astype(LOW)
    grad_proj_back = (grad_hidden * proj_fore * value_act).astype(LOW)
    grad_pre_value = value_pull(grad_hidden * proj_fore * proj_back)[0].astype(LOW)
    grad_fore_low = dot_outer(grad_proj_fore, full["fore"]).astype(LOW).reshape(filter_low.shape)
    grad_back_low = dot_outer(grad_proj_back, full["back"]).astype(LOW).reshape(filter_low.shape)
    fore_around = [grad_fore_low] + from_right(grad_fore_low, n_seq)
    back_around = from_left(grad_back_low, n_seq) + [grad_back_low]
    grads = {}
    grads["out"] = dot_inner(hidden_low, cot_rows)
    grads["fore"] = dot_inner(fore_low, grad_proj_fore)
    grads["back"] = dot_inner(back_low, grad_proj_back)
    grads["value"] = dot_inner(normed_low, grad_pre_value)
    grad_filter_low, grad_kern = conv_backward(mask, wave, kern, around, fore_around, back_around, tile_step)
    grad_pre_filter = filter_pull(grad_filter_low.reshape(rows, -1).astype(F32))[0].astype(LOW)
    grads["filter"] = dot_inner(normed_low, grad_pre_filter)
    grad_normed = dot_outer(grad_pre_value, full["value"]) + dot_outer(grad_pre_filter, full["filter"])
    grad_rows, gain_grad, bias_grad = norm_pull(grad_normed)
    grad_tokens = (cot_rows.astype(F32) + grad_rows).astype(LOW).reshape(tokens.shape)

    grads = {m: a.reshape(n_seq, -1, a.shape[-1]) for m, a in grads.items()}
    if linked:
        grads = {m: a.astype(LOW) for m, a in grads.items()}
        order = ("out", "fore", "back", "kern", "value", "filter")
        grads["kern"] = grad_kern.reshape(n_seq, -1, LONG)
        sums = dict(zip(order, reduce_weights(order, [grads[m] for m in order])))
        sums = {m: a.astype(F32) for m, a in sums.items()}
    else:
        grads["kern"] = grad_kern.reshape(n_seq, -1, LONG)
        sums = {m: lax.psum_scatter(a.astype(F32), "seq", scatter_dimension=0, tiled=False) for m, a in grads.items()}
        sums = {m: lax.psum(a, "dp") for m, a in sums.items()}
    norm_grads = lax.psum(jnp.stack([gain_grad, bias_grad]), ("dp", "seq"))
    norm_grads = lax.dynamic_slice_in_dim(norm_grads, lax.axis_index("seq") * ln_gain.shape[0], ln_gain.shape[0], 1)
    modes_grad = jnp.stack(pull_kernels(sums["kern"], coef, rate, freq)).reshape(3, 2, some, modes)
    if linked:
        modes_grad = lax.all_gather(modes_grad, "dp", axis=2, tiled=True)
    return (
        mixed,
        grad_tokens,
        norm_grads[0],
        norm_grads[1],
        sums["value"],
        sums["filter"],
        sums["fore"],
        sums["back"],
        sums["out"],
        modes_grad[0],
        modes_grad[1],
        modes_grad[2],
    )


def solution(mesh):
    rows = P("seq", None)
    modes = P(None, "seq", None)
    tokens = P(None, ("dp", "seq"), None)
    return jax.shard_map(
        functools.partial(shards, mesh.shape["dp"], mesh.shape["seq"]),
        mesh=mesh,
        in_specs=(tokens, tokens, P(None, "dp", None), P("seq"), P("seq")) + (rows,) * 5 + (modes,) * 3,
        out_specs=(tokens, tokens, P("seq"), P("seq")) + (rows,) * 5 + (modes,) * 3,
        check_vma=False,
    )
```

time: 3930 us -> 672 us (0.17)
  other arithmetic: 1750 us -> 34 us
  local copies, waits for them, and re-layouts: 1020 us -> 28 us
  matrix products: 817 us -> 125 us
  Pallas kernels: 0 us -> 365 us
  waiting for transfers between devices: 210 us -> 13.2 us
    scatter-add x2 -> x0, other arithmetic: 918 us -> none  [banded(): jnp.take(kernel_rows, safe_lag.reshape(-1), axis=1)]
    dot_general x22 -> x7, matrix products: 708 us -> 57 us  [the longest x5 48.9 us: dot_plain(): return jnp.dot(left_side, right_side, preferred_element_type=F32)]
    gather x2 -> x0, local copies, waits for them, and re-layouts: 613 us -> none  [banded(): jnp.take(kernel_rows, safe_lag.reshape(-1), axis=1)]
    unnamed x11 -> x6, other arithmetic: 366 us -> 0.02 us
    pallas_call x0 -> x4, Pallas kernels: none -> 365 us  [the longest x1 185 us: reduce_weights(): pl.pallas_call(functools.partial(rs_kernel, names), out_shape=[jax.ShapeD...]
    reshape x4 -> x3, local copies, waits for them, and re-layouts: 328 us -> 0.1 us  [the longest x1 0.1 us: pull_kernels(): rows = grad.reshape(grad.shape[0], LONG // STEP_A, STEP_A)]
    reduce_sum x6 -> x4, other arithmetic: 241 us -> 5.25 us  [the longest x1 4.02 us: pull_kernels(): plain = jnp.sum(ar * zero_r - ai * zero_i, 1)]
    select_n x6 -> x0, other arithmetic: 195 us -> none  [the longest x4 110 us: banded(): jnp.take(kernel_rows, safe_lag.reshape(-1), axis=1)]
  transfers between devices with their start and end apart: 23 -> 8, of which waited for: 9 -> 2; matrix products, arithmetic and copies ran while one was open for 90% -> 13% of each run, Pallas kernels for 0% -> 0%
where the time goes in v1:
time: 672 us; the launch traced here: 666 us
  Pallas kernels  365 us (54%)
  matrix products  125 us (19%)
  blocking collectives  68.1 us (10%)
  other arithmetic  34 us (5%)
  starting transfers between devices  29.8 us (4%)
  local copies, waits for them, and re-layouts  28 us (4%)
  waiting for transfers between devices  13.2 us (2%)
    pallas_call x1, Pallas kernels, reduce_weights(): pl.pallas_call(functools.partial(rs_kernel, names), out_shape=[jax.ShapeD...  185 us
    pallas_call x1, Pallas kernels, gather_weights(): pl.pallas_call(functools.partial(ag_kernel, names), out_shape=shapes, in_...  123 us
    pallas_call x2, Pallas kernels, conv_call(): pl.pallas_call(body, grid=(steps,), out_shape=outs, in_specs=[pl.BlockSpe...  56.9 us
    dot_general x5, matrix products, dot_plain(): return jnp.dot(left_side, right_side, preferred_element_type=F32)  48.9 us
    psum x1, blocking collectives, shards(): norm_grads = lax.psum(jnp.stack([gain_grad, bias_grad]), ('dp', 'seq'))  39.2 us
    dot_general x5, matrix products, dot_inner(): lax.dot_general(left_side, right_side, (((0,), (0,)), ((), ())), preferre...  34.6 us
    dot_general x5, matrix products, dot_outer(): lax.dot_general(left_side, right_side, (((1,), (1,)), ((), ())), preferre...  33.8 us
    ppermute x8, starting transfers between devices, shift(): return lax.ppermute(array, 'seq', pairs)  29.8 us
  transfers between devices with their start and end apart: 8, of which 2 were waited for; matrix products, arithmetic and copies ran while one was open for 13% of the time, Pallas kernels for 0%

profile of v1, /device:TPU:0, one launch (start us, length us, event | category | flops | bytes accessed | tf_op | source)
XLA Modules:
  0.0 665.7 jit_solution(14229014299916727681)
XLA Ops:
  2.2 6.8 %fusion.33 = (f32[96,32,64]{2,1,0:T(8,128)S(1)}, f32[96,32,64]{2,1,0:T(8,128)}) fusion(f32[96,64]{1,0:T(8,128)S(1)} %bitcast.179, f32[32]{0:T(128)S(1)} %iota_convert_fusion, f32[96,64]{1,0:T(8,128)S(1)} %bitcast.182), kind=kLoop, calls=%fused_computation.56 | loop fusion | flops 786432 | bytes 1622144 | tf_op jit(solution)/shard_map/mul | solution.py:508
  9.0 3.0 fusion.60
  12.1 4.3 convolution_convert_fusion.7
  19.3 18.3 %all-reduce.3 = (bf16[768]{0:T(1024)(128)(2,1)S(1)}, bf16[768]{0:T(1024)(128)(2,1)S(1)}) all-reduce(bf16[768]{0:T(1024)(128)(2,1)S(1)} %dynamic-update-slice.1, bf16[768]{0:T(1024)(128)(2,1)S(1)} %dynamic-update-slice), channel_id=1, replica_groups=mesh['dp'=4,'seq'=8] {'seq'}, use_global_device_ids=true, to_apply=%add.2 | all-reduce | flops 1536 | bytes 6144
  38.5 122.7 %shard_map.229 = (bf16[8,96,1536]{2,1,0:T(8,128)(2,1)}, bf16[8,384,512]{2,1,0:T(8,128)(2,1)}, bf16[8,96,3072]{2,1,0:T(8,128)(2,1)}, bf16[8,192,3072]{2,1,0:T(8,1...) custom-call(bf16[96,1536]{1,0:T(8,128)(2,1)} %refs_0_.1, bf16[96,512]{1,0:T(8,128)(2,1)} %copy.71.refs_1_, ...), custom_call_target="tpu_custom_call" | custom-call | tf_op jit(solution)/shard_map/pallas_call | solution.py:346
  161.3 5.6 multiply_convert_fusion.3
  166.9 3.6 collective-permute-start.1
  170.5 1.3 collective-permute-start.2
  171.8 2.6 fusion.68
  174.4 3.9 collective-permute-start
  180.6 6.9 %fusion.71 = f32[512,3072]{1,0:T(8,128)} fusion(bf16[512,768]{1,0:T(8,128)(2,1)S(1)} %bitcast.163, bf16[768,3072]{1,0:T(8,128)(2,1)} %bitcast.157), kind=kOutput, calls=%fused_computation.153 | convolution fusion | flops 2415919104 | bytes 11796480 | tf_op jit(solution)/shard_map/dot_general | solution.py:541
  188.2 7.0 %fusion.72 = f32[3072,512]{0,1:T(8,128)} fusion(bf16[3072,768]{1,0:T(8,128)(2,1)} %bitcast.205, bf16[512,768]{1,0:T(8,128)(2,1)S(1)} %bitcast.174), kind=kOutput, calls=%fused_computation.154 | convolution fusion | flops 2415919104 | bytes 11796480 | tf_op jit(solution)/shard_map/dot_general | solution.py:549
  195.7 12.7 %collective-permute-done.3.refs_4_ = bf16[2,128,1536]{2,1,0:T(8,128)(2,1)} collective-permute-done((bf16[2,128,1536]{2,1,0:T(8,128)(2,1)}, bf16[2,128,1536]{2,1,0:T(8,128)(2,1)}, u32[]{:S(2)}, u32[]{:S(2)}) %collective-permute-start.3) | collective-permute-done | bytes 786464 | tf_op jit(solution)/shard_map/ppermute | solution.py:561
  208.4 20.8 %shard_map.230 = (bf16[2,256,1536]{2,1,0:T(8,128)(2,1)}, bf16[2,256,1536]{2,1,0:T(8,128)(2,1)}) custom-call(f32[28]{0:T(128)} %reshape.303.mask_ref, bf16[256,256]{1,0:T(8,128)(2,1)} %constant.70.clone.wave_ref, bf16[8,4,2,48,512]{4,3,2,1,0:T(8,128)(2,1)} %bitcast.207, bf16[2,128,1536]{2,1,0:T(8,128)(2,1)} %collective-permute-done.refs_0_, ...), custom_call_target="tpu_custom_call" | custom-call | flops 10000000000 | bytes 30000000 | tf_op jit(solution)/shard_map/pallas_call | solution.py:199
  229.3 9.9 %fusion.70 = f32[512,3072]{1,0:T(8,128)} fusion(bf16[512,1536]{1,0:T(8,128)(2,1)} %bitcast.168, bf16[1536,3072]{1,0:T(8,128)(2,1)} %bitcast.201), kind=kOutput, calls=%fused_computation.152 | convolution fusion | flops 4831838208 | bytes 17301504 | tf_op jit(solution)/shard_map/dot_general | solution.py:541
  239.2 19.0 %multiply_convert_fusion = (bf16[512,3072]{1,0:T(8,128)(2,1)}, bf16[512,3072]{1,0:T(8,128)(2,1)}, bf16[512,3072]{1,0:T(8,128)(2,1)}, f32[512,3072]{1,0:T(8,128)}) fusion(f32[3072,512]{0,1:T(8,128)} %fusion.72, f32[512,3072]{1,0:T(8,128)S(1)} %bitcast.152, f32[512,3072]{1,0:T(8,128)} %fusion.70, bf16[512,1536]{1,0:T(8,128)(2,1)S(1)} %bitcast.171, ...), kind=kOutput, calls=%fused_computation.25 | convolution fusion | flops 4875878400 | bytes 45613056 | tf_op jit(solution)/shard_map/dot_general | solution.py:541
  258.2 10.3 %convolution_convert_fusion.5 = bf16[512,1536]{1,0:T(8,128)(2,1)} fusion(bf16[512,3072]{1,0:T(8,128)(2,1)} %get-tuple-element.90, bf16[1536,3072]{1,0:T(8,128)(2,1)} %bitcast.204), kind=kOutput, calls=%fused_computation.50 | convolution fusion | flops 4832624640 | bytes 14155776 | tf_op jit(solution)/shard_map/dot_general | solution.py:549
  268.5 1.7 collective-permute-start.4
  270.2 2.2 slice.106
  272.4 11.1 %convolution_convert_fusion.4 = bf16[512,1536]{1,0:T(8,128)(2,1)} fusion(bf16[512,3072]{1,0:T(8,128)(2,1)} %get-tuple-element.88, bf16[1536,3072]{1,0:T(8,128)(2,1)} %bitcast.202), kind=kOutput, calls=%fused_computation.49 | convolution fusion | flops 4832624640 | bytes 14155776 | tf_op jit(solution)/shard_map/dot_general | solution.py:549
  283.5 2.1 slice.107
  285.6 4.2 collective-permute-start.7
  289.8 7.5 %fusion.51 = bf16[512,768]{1,0:T(8,128)(2,1)} fusion(bf16[2,256,768]{2,1,0:T(8,128)(2,1)S(1)} %copy-done.2, bf16[3072,768]{1,0:T(8,128)(2,1)} %bitcast.206, f32[512,3072]{1,0:T(8,128)S(1)} %bitcast.156, f32[512,3072]{1,0:T(8,128)S(1)} %bitcast.154, f32[512,3072]{1,0:T(8,128)S(1)} %bitcast.152), kind=kOutput, calls=%fused_computation.79 | convolution fusion | flops 2434400256 | bytes 25165824 | tf_op jit(solution)/shard_map/dot_general | solution.py:541
  297.3 3.6 fusion.15
  302.1 12.6 %collective-permute-start.6 = (bf16[2,128,1536]{2,1,0:T(8,128)(2,1)}, bf16[2,128,1536]{2,1,0:T(8,128)(2,1)}, u32[]{:S(2)}, u32[]{:S(2)}) collective-permute-start(bf16[2,128,1536]{2,1,0:T(8,128)(2,1)} %slice.107), channel_id=1, source_target_pairs={{0,2},{1,3},{2,4},{3,5},{4,6},{5,7},{8,10},{9,11},{10,12},{11,13},... | collective-permute-start | bytes 2359304 | tf_op jit(solution)/shard_map/ppermute | solution.py:561
  314.7 2.6 copy.74
  317.3 9.4 %convolution_convert_fusion.1.refs_1_ = bf16[8,192,3072]{2,1,0:T(8,128)(2,1)} fusion(bf16[8,192,512]{2,1,0:T(8,128)(2,1)} %bitcast.172, bf16[512,3072]{1,0:T(8,128)(2,1)} %get-tuple-element.90), kind=kOutput, calls=%fused_computation.4 | convolution fusion | flops 4836556800 | bytes 14155776 | tf_op jit(solution)/shard_map/dot_general | solution.py:545
  326.7 2.6 copy.75
  329.3 9.3 %convolution_convert_fusion.refs_2_ = bf16[8,192,3072]{2,1,0:T(8,128)(2,1)} fusion(bf16[8,192,512]{2,1,0:T(8,128)(2,1)} %bitcast.173, bf16[512,3072]{1,0:T(8,128)(2,1)} %get-tuple-element.88), kind=kOutput, calls=%fused_computation.3 | convolution fusion | flops 4836556800 | bytes 14155776 | tf_op jit(solution)/shard_map/dot_general | solution.py:545
  338.6 4.7 copy.83
  343.4 6.8 %convolution_convert_fusion.6.refs_0_ = bf16[8,384,768]{2,1,0:T(8,128)(2,1)} fusion(bf16[8,384,512]{2,1,0:T(8,128)(2,1)} %bitcast.165, bf16[512,768,1]{1,0,2:T(8,128)(2,1)S(1)} %bitcast.175), kind=kOutput, calls=%fused_computation.51 | convolution fusion | flops 2418278400 | bytes 8650752 | tf_op jit(solution)/shard_map/dot_general | solution.py:545
  350.2 3.8 fusion.73
  354.9 36.1 %shard_map.231 = (bf16[2,256,1536]{2,1,0:T(8,128)(2,1)}, bf16[8,4,2,48,512]{4,3,2,1,0:T(8,128)(2,1)}) custom-call(f32[28]{0:T(128)} %reshape.303.mask_ref, bf16[256,256]{1,0:T(8,128)(2,1)} %constant.70.clone.wave_ref, bf16[8,4,2,48,512]{4,3,2,1,0:T(8,128)(2,1)} %bitcast.208, bf16[2,128,1536]{2,1,0:T(8,128)(2,1)} %collective-permute-done.refs_0_, ...), custom_call_target="tpu_custom_call" | custom-call | flops 10000000000 | bytes 30000000 | tf_op jit(solution)/shard_map/pallas_call | solution.py:199
  391.0 3.5 fusion.20
  394.6 1.6 fusion.50
  397.0 1.7 fusion.45
  399.0 6.3 convolution_convert_fusion.2.refs_4_
  405.3 2.8 convolution_convert_fusion.3.refs_5_
  408.1 39.2 %psum.7 = f32[2,768]{1,0:T(2,128)S(1)} all-reduce(f32[2,768]{1,0:T(2,128)S(1)} %pad_maximum_fusion.5), channel_id=1, replica_groups=mesh['dp'=4,'seq'=8] {'dp','seq'}, use_global_device_ids=true, to_apply=%region_8.9 | all-reduce | flops 1536 | bytes 12288 | tf_op jit(solution)/shard_map/psum | solution.py:684
  447.9 185.2 %shard_map.232 = (bf16[384,768]{1,0:T(8,128)(2,1)}, bf16[192,3072]{1,0:T(8,128)(2,1)}, bf16[192,3072]{1,0:T(8,128)(2,1)}, bf16[96,512]{1,0:T(8,128)(2,1)}, bf16[...) custom-call(bf16[8,384,768]{2,1,0:T(8,128)(2,1)} %convolution_convert_fusion.6.refs_0_, ...), custom_call_target="tpu_custom_call" | custom-call | tf_op jit(solution)/shard_map/pallas_call | solution.py:483
  633.2 2.3 convert_element_type.176
  635.5 1.8 convert_element_type.177
  637.3 1.7 convert_element_type.178
  639.0 1.7 convert_element_type.179
  642.0 2.3 copy.78
  644.4 3.8 fusion.61
  648.2 4.0 fusion.55
  652.3 10.6 %all_gather.11 = f32[3,2,192,64]{3,2,1,0:T(8,128)S(1)} all-gather(f32[3,2,48,64]{3,2,1,0:T(8,128)S(1)} %pad_maximum_fusion.4), channel_id=1, replica_groups=mesh['dp'=4,'seq'=8] {'dp'}, dimensions={2}, use_global_device_ids=true | all-gather | bytes 368640 | tf_op jit(solution)/shard_map/all_gather | solution.py:688
  (153 shorter events, 15.8 us)
Async XLA Ops:
  0.6 1.3 copy-start
  0.7 11.4 %copy-start.23 = (f32[16]{0:T(128)}, f32[16]{0:T(128)S(1)}, u32[]{:S(2)}) copy-start(f32[16]{0:T(128)S(1)} %multiply_convert_fusion.6) | copy-start | bytes 196
  1.9 10.2 %copy-start.12 = (f32[2,48,64]{2,1,0:T(8,128)}, f32[2,48,64]{2,1,0:T(8,128)S(1)}, u32[]{:S(2)}) copy-start(f32[2,48,64]{2,1,0:T(8,128)S(1)} %copy.69) | copy-start | bytes 73732
  2.0 10.1 %copy-start.17 = (f32[2,48,64]{2,1,0:T(8,128)}, f32[2,48,64]{2,1,0:T(8,128)S(1)}, u32[]{:S(2)}) copy-start(f32[2,48,64]{2,1,0:T(8,128)S(1)} %copy.86) | copy-start | bytes 73732
  2.2 9.9 %copy-start.19 = (f32[2,48,64]{2,1,0:T(8,128)}, f32[2,48,64]{2,1,0:T(8,128)S(1)}, u32[]{:S(2)}) copy-start(f32[2,48,64]{2,1,0:T(8,128)S(1)} %copy.85) | copy-start | bytes 73732
  2.2 9.9 %copy-start.14 = (f32[2,48,64]{2,1,0:T(8,128)}, f32[2,48,64]{2,1,0:T(8,128)S(1)}, u32[]{:S(2)}) copy-start(f32[2,48,64]{2,1,0:T(8,128)S(1)} %get-tuple-element.105) | copy-start | bytes 73732
  9.0 3.1 copy-start.3
  12.0 5.6 copy-start.29
  12.0 6.8 %copy-start.27 = (bf16[96]{0:T(256)(128)(2,1)S(1)}, bf16[96]{0:T(256)(128)(2,1)}, u32[]{:S(2)}) copy-start(bf16[96]{0:T(256)(128)(2,1)} %param.18) | copy-start | bytes 580
  12.0 7.0 %copy-start.28 = (bf16[96]{0:T(256)(128)(2,1)S(1)}, bf16[96]{0:T(256)(128)(2,1)}, u32[]{:S(2)}) copy-start(bf16[96]{0:T(256)(128)(2,1)} %param.17) | copy-start | bytes 580
  12.0 25.6 %copy-start.2 = (bf16[2,256,768]{2,1,0:T(8,128)(2,1)S(1)}, bf16[2,256,768]{2,1,0:T(8,128)(2,1)}, u32[]{:S(2)}) copy-start(bf16[2,256,768]{2,1,0:T(8,128)(2,1)} %param.14) | copy-start | bytes 2359300
  166.9 12.7 %copy-start.22 = (s32[2,1,16]{2,1,0:T(1,128)S(1)}, s32[2,1,16]{2,1,0:T(1,128)}, u32[]{:S(2)}) copy-start(s32[2,1,16]{2,1,0:T(1,128)} %param.16) | copy-start | bytes 388
  166.9 41.5 %collective-permute-start.1 = (bf16[2,256,1536]{2,1,0:T(8,128)(2,1)}, bf16[2,256,1536]{2,1,0:T(8,128)(2,1)}, u32[]{:S(2)}, u32[]{:S(2)}) collective-permute-start(bf16[2,256,1536]{2,1,0:T(8,128)(2,1)} %bitcast.12.refs_2_), channel_id=1, source_target_pairs={{0,1},{1,2},{2,3},{3,4},{4,5},{5,6},{6,7},{8,9},{9,10},{10,11},{11... | collective-permute-start | bytes 4718600 | tf_op jit(solution)/shard_map/ppermute | solution.py:561
  170.5 37.9 %collective-permute-start.2 = (bf16[2,256,1536]{2,1,0:T(8,128)(2,1)}, bf16[2,256,1536]{2,1,0:T(8,128)(2,1)}, u32[]{:S(2)}, u32[]{:S(2)}) collective-permute-start(bf16[2,256,1536]{2,1,0:T(8,128)(2,1)} %bitcast.12.refs_2_), channel_id=1, source_target_pairs={{1,0},{2,1},{3,2},{4,3},{5,4},{6,5},{7,6},{9,8},{10,9},{11,10},{12... | collective-permute-start | bytes 4718600 | tf_op jit(solution)/shard_map/ppermute | solution.py:561
  174.4 21.3 %collective-permute-start = (bf16[2,128,1536]{2,1,0:T(8,128)(2,1)}, bf16[2,128,1536]{2,1,0:T(8,128)(2,1)}, u32[]{:S(2)}, u32[]{:S(2)}) collective-permute-start(bf16[2,128,1536]{2,1,0:T(8,128)(2,1)} %get-tuple-element.92), channel_id=1, source_target_pairs={{0,2},{1,3},{2,4},{3,5},{4,6},{5,7},{8,10},{9,11},{10,12},{11,13},... | collective-permute-start | bytes 2359304 | tf_op jit(solution)/shard_map/ppermute | solution.py:561
  178.3 30.1 %collective-permute-start.3 = (bf16[2,128,1536]{2,1,0:T(8,128)(2,1)}, bf16[2,128,1536]{2,1,0:T(8,128)(2,1)}, u32[]{:S(2)}, u32[]{:S(2)}) collective-permute-start(bf16[2,128,1536]{2,1,0:T(8,128)(2,1)} %get-tuple-element.91), channel_id=1, source_target_pairs={{2,0},{3,1},{4,2},{5,3},{6,4},{7,5},{10,8},{11,9},{12,10},{13,11},... | collective-permute-start | bytes 2359304 | tf_op jit(solution)/shard_map/ppermute | solution.py:561
  180.6 7.5 %copy-start.11 = (bf16[2,256,768]{2,1,0:T(8,128)(2,1)S(1)}, bf16[2,256,768]{2,1,0:T(8,128)(2,1)}, u32[]{:S(2)}) copy-start(bf16[2,256,768]{2,1,0:T(8,128)(2,1)} %param.15) | copy-start | bytes 2359300
  188.2 51.0 %slice-start = ((s8[6291456]{0:T(1024)(128)(4,1)}), s8[4194304]{0:T(1024)(128)(4,1)S(1)}, s32[]{:S(2)}) async-start(s8[6291456]{0:T(1024)(128)(4,1)} %bitcast.151), calls=%async_computation | async-start | bytes 8388608
  208.4 30.8 %slice-start.1 = ((s8[6291456]{0:T(1024)(128)(4,1)}), s8[2097152]{0:T(1024)(128)(4,1)S(1)}, s32[]{:S(2)}) async-start(s8[6291456]{0:T(1024)(128)(4,1)} %bitcast.151), calls=%async_computation.1 | async-start | bytes 4194304
  229.3 9.9 %copy-start.6 = (bf16[2,256,1536]{2,1,0:T(8,128)(2,1)S(1)}, bf16[2,256,1536]{2,1,0:T(8,128)(2,1)}, u32[]{:S(2)}) copy-start(bf16[2,256,1536]{2,1,0:T(8,128)(2,1)} %get-tuple-element.30) | copy-start | bytes 4718596
  268.5 85.5 %collective-permute-start.4 = (bf16[2,256,1536]{2,1,0:T(8,128)(2,1)}, bf16[2,256,1536]{2,1,0:T(8,128)(2,1)}, u32[]{:S(2)}, u32[]{:S(2)}) collective-permute-start(bf16[2,256,1536]{2,1,0:T(8,128)(2,1)} %bitcast.22.refs_5_), channel_id=1, source_target_pairs={{1,0},{2,1},{3,2},{4,3},{5,4},{6,5},{7,6},{9,8},{10,9},{11,10},{12... | collective-permute-start | bytes 4718600 | tf_op jit(solution)/shard_map/ppermute | solution.py:561
  270.2 19.6 %slice-start.2 = ((s8[6291456]{0:T(1024)(128)(4,1)}), s8[4194304]{0:T(1024)(128)(4,1)S(1)}, s32[]{:S(2)}) async-start(s8[6291456]{0:T(1024)(128)(4,1)} %bitcast.153), calls=%async_computation.2 | async-start | bytes 8388608
  270.2 19.6 %slice-start.4 = ((s8[6291456]{0:T(1024)(128)(4,1)}), s8[4194304]{0:T(1024)(128)(4,1)S(1)}, s32[]{:S(2)}) async-start(s8[6291456]{0:T(1024)(128)(4,1)} %bitcast.155), calls=%async_computation.4 | async-start | bytes 8388608
  272.4 17.3 %slice-start.3 = ((s8[6291456]{0:T(1024)(128)(4,1)}), s8[2097152]{0:T(1024)(128)(4,1)S(1)}, s32[]{:S(2)}) async-start(s8[6291456]{0:T(1024)(128)(4,1)} %bitcast.153), calls=%async_computation.3 | async-start | bytes 4194304
  272.4 17.3 %slice-start.5 = ((s8[6291456]{0:T(1024)(128)(4,1)}), s8[2097152]{0:T(1024)(128)(4,1)S(1)}, s32[]{:S(2)}) async-start(s8[6291456]{0:T(1024)(128)(4,1)} %bitcast.155), calls=%async_computation.5 | async-start | bytes 4194304
  285.6 68.5 %collective-permute-start.7 = (bf16[2,256,1536]{2,1,0:T(8,128)(2,1)}, bf16[2,256,1536]{2,1,0:T(8,128)(2,1)}, u32[]{:S(2)}, u32[]{:S(2)}) collective-permute-start(bf16[2,256,1536]{2,1,0:T(8,128)(2,1)} %bitcast.188), channel_id=1, source_target_pairs={{0,1},{1,2},{2,3},{3,4},{4,5},{5,6},{6,7},{8,9},{9,10},{10,11},{11... | collective-permute-start | bytes 4718600 | tf_op jit(solution)/shard_map/ppermute | solution.py:561
  300.8 53.1 %collective-permute-start.5 = (bf16[2,128,1536]{2,1,0:T(8,128)(2,1)}, bf16[2,128,1536]{2,1,0:T(8,128)(2,1)S(1)}, u32[]{:S(2)}, u32[]{:S(2)}) collective-permute-start(bf16[2,128,1536]{2,1,0:T(8,128)(2,1)} %slice.106), channel_id=1, source_target_pairs={{2,0},{3,1},{4,2},{5,3},{6,4},{7,5},{10,8},{11,9},{12,10},{13,11},... | collective-permute-start | bytes 2359304 | tf_op jit(solution)/shard_map/ppermute | solution.py:561
  302.1 51.9 %collective-permute-start.6 = (bf16[2,128,1536]{2,1,0:T(8,128)(2,1)}, bf16[2,128,1536]{2,1,0:T(8,128)(2,1)}, u32[]{:S(2)}, u32[]{:S(2)}) collective-permute-start(bf16[2,128,1536]{2,1,0:T(8,128)(2,1)} %slice.107), channel_id=1, source_target_pairs={{0,2},{1,3},{2,4},{3,5},{4,6},{5,7},{8,10},{9,11},{10,12},{11,13},... | collective-permute-start | bytes 2359304 | tf_op jit(solution)/shard_map/ppermute | solution.py:561
  338.6 11.5 %slice-start.6 = ((s8[4718592]{0:T(1024)(128)(4,1)}), s8[524288]{0:T(1024)(128)(4,1)S(1)}, s32[]{:S(2)}) async-start(s8[4718592]{0:T(1024)(128)(4,1)} %bitcast.158), calls=%async_computation.6 | async-start | bytes 1048576
  343.4 6.8 %slice-start.7 = ((s8[4718592]{0:T(1024)(128)(4,1)}), s8[4194304]{0:T(1024)(128)(4,1)S(1)}, s32[]{:S(2)}) async-start(s8[4718592]{0:T(1024)(128)(4,1)} %bitcast.158), calls=%async_computation.7 | async-start | bytes 8388608
  343.4 6.8 %copy-start.31 = (bf16[512,3072]{1,0:T(8,128)(2,1)S(1)}, bf16[512,3072]{1,0:T(8,128)(2,1)}, u32[]{:S(2)}) copy-start(bf16[512,3072]{1,0:T(8,128)(2,1)} %get-tuple-element.89) | copy-start | bytes 9437188
  354.0 37.0 %copy-start.5 = (f32[512,1536]{1,0:T(8,128)S(1)}, f32[512,1536]{1,0:T(8,128)}, u32[]{:S(2)}) copy-start(f32[512,1536]{1,0:T(8,128)} %get-tuple-element.128) | copy-start | bytes 9437188
  354.0 0.9 copy-start.26
  391.0 3.6 copy-start.25
  391.0 3.6 copy-start.30
  394.5 1.6 copy-start.7
  399.0 6.3 copy-start.8
  633.1 4.2 copy-start.10
  633.1 5.8 copy-start.9
  637.3 3.3 copy-start.16
  639.0 2.8 copy-start.21
  640.6 3.7 copy-start.4
  644.4 3.8 copy-start.13
  644.4 3.8 copy-start.15
  644.4 3.8 copy-start.24
  644.4 20.9 %copy-start.1 = (f32[2,192,64]{1,2,0:T(8,128)S(1)}, f32[2,192,64]{1,2,0:T(8,128)}, u32[]{:S(2)}) copy-start(f32[2,192,64]{1,2,0:T(8,128)} %param.24) | copy-start | bytes 294916
  648.2 4.0 copy-start.18
  648.2 4.0 copy-start.20

commit v2 on v1

--- a/solution.py
+++ b/solution.py
@@ -95,10 +95,10 @@
 
 
 def back_kernel(mask_ref, wave_ref, kern_ref, *refs):
-    parts = refs[:5]
-    fparts = refs[5:8]
-    bparts = refs[8:11]
-    gfil_ref, gk_ref, spec_ref, x_ref, f_ref, b_ref, y_ref, r_ref = refs[11:]
+    parts = refs[:-14]
+    fparts = refs[-14:-11]
+    bparts = refs[-11:-8]
+    gfil_ref, gk_ref, spec_ref, x_ref, f_ref, b_ref, y_ref, r_ref = refs[-8:]
     tile = gfil_ref.shape[-1]
     kernel_spectra(wave_ref, kern_ref, spec_ref, tile)
     fwd = wave_ref[:, BLK:]
@@ -215,22 +215,20 @@
 
 
 def conv_backward(mask, wave, kern, parts, fparts, bparts, step):
-    own = parts[2]
+    own = fparts[0]
     return conv_call(back_kernel, mask, wave, kern, list(parts) + list(fparts) + list(bparts),
                      [jax.ShapeDtypeStruct(own.shape, jnp.bfloat16), jax.ShapeDtypeStruct(kern.shape, jnp.bfloat16)],
                      [(2, 4, 256), (8, 256), (5, 256), (5, 256), (2, 256), (2, 4, 256)], step)
 
 
-AHEAD = 1
-L2 = 2
-L3 = 4
-
 def place(n_z):
     dp = lax.axis_index("dp"); s = lax.axis_index("seq")
     return dp, s, s // 2, lax.rem(s, 2)
 
 def cut(ref, geom, q, h=None):
     kind = geom
+    if kind is None:
+        return ref
     R, C = ref.shape[-2:]
     if kind == "col":
         cols = pl.ds(pl.multiple_of(q * (C // 4), 128), C // 4)
@@ -242,257 +240,777 @@
             return ref.at[pl.ds(pl.multiple_of(q * n, 16), n)]
         return ref.at[pl.ds(pl.multiple_of(q * n + h * (n // 2), 16), n // 2)]
 
-GEOM = {"filter": "col", "kern": "row", "value": "col", "fore": "col", "back": "col", "out": "row"}
-
-def ag_kernel(names, *refs):
+GEOM = {"filter": "col", "kern": "row", "value": "col", "fore": "col", "back": "col", "out": "row", "norm": None}
+
+
+FETCH = ("norm", "filter", "value", "out", "kern", "fore", "back")
+GELU_C = 0.7978845608028654
+GELU_D = 0.044715
+
+
+def gelu_parts(x):
+    sq = x * x
+    t = jnp.tanh(GELU_C * x * (1.0 + GELU_D * sq))
+    half = 0.5 * (1.0 + t)
+    return x * half, half + 0.5 * x * (1.0 - t * t) * (GELU_C * (1.0 + 3.0 * GELU_D * sq))
+
+
+def slab_forward(mask_ref, wave_ref, kr_ref, spec_ref, x_ref, y_ref, fb_ref, outs, chunk, slab):
+    tile = 128
+    rows = pl.ds(pl.multiple_of(slab * tile, tile), tile)
+    lanes = pl.ds(pl.multiple_of(chunk * 384 + slab * tile, tile), tile)
+    fwd = wave_ref[:, BLK:]
+    for side in range(2):
+        spec_ref[side, 0] = dot(fwd, kr_ref[side, rows, :BLK], 1, 1)
+        for d in range(1, REACH + 1):
+            spec_ref[side, d] = dot(wave_ref[...], kr_ref[side, rows, (d - 1) * BLK:(d + 1) * BLK], 1, 1)
+    for micro in range(2):
+        for b in range(8):
+            x_ref[b] = dot(fwd, fb_ref[micro, b * BLK:(b + 1) * BLK, lanes], 1, 0)
+
+        @pl.loop(0, BLK // 8)
+        def _(r):
+            re = pl.ds(pl.multiple_of(r * 8, 8), 8)
+            im = pl.ds(pl.multiple_of(r * 8 + BLK, 8), 8)
+            xr = [x_ref[b, re, :] for b in range(8)]
+            xi = [x_ref[b, im, :] for b in range(8)]
+            for side in range(2):
+                cr = [spec_ref[side, d, re, :] for d in range(4)]
+                ci = [spec_ref[side, d, im, :] for d in range(4)]
+                for own in range(2):
+                    yr = yi = None
+                    for d in range(4):
+                        at = own + 3 + (d if side else -d)
+                        pr = cr[d] * xr[at]
+                        pi = cr[d] * xi[at]
+                        qr = ci[d] * xi[at]
+                        qi = ci[d] * xr[at]
+                        if side:
+                            tr, ti = pr + qr, pi - qi
+                        else:
+                            tr, ti = pr - qr, pi + qi
+                        if d:
+                            m = mask_ref[(micro * 2 + own) * 7 + 3 + (d if side else -d)]
+                            tr, ti = tr * m, ti * m
+                        yr = tr if yr is None else yr + tr
+                        yi = ti if yi is None else yi + ti
+                    y_ref[side, own, re, :] = yr
+                    y_ref[side, own, im, :] = yi
+
+        for own in range(2):
+            for side in range(2):
+                y = dot(fwd, y_ref[side, own].astype(jnp.bfloat16), 0, 0)
+                at = micro * 256 + own * BLK
+                outs[side][at:at + BLK, lanes] = (y * (1.0 / BLK)).astype(jnp.bfloat16)
+
+
+def forward_kernel(width, mask_ref, *refs):
+    refs = list(refs)
+    take = lambda n: [refs.pop(0) for _ in range(n)]
+    names = FETCH
     n = len(names)
-    src = refs[:n]; out = refs[n:2 * n]
-    stage = refs[2 * n:3 * n]
-    isem, lsem, zs, zr, xs, xr, ys, yr, fxs, fxr, fys, fyr, ss, sr, ss0, sr0 = refs[3 * n:]
+    wave_in, tok_in, cot_in = take(3)
+    src = take(n)
+    out = take(n)
+    pre_out, fb_out, fore_out, back_out, hid_out, gpf_out, gpb_out, gpv_out, nrm_out = take(9)
+    stage = take(n)
+    wave_ref, tok, cot, nv, gb, nl, wa, wb, pf, pv, gh, fb, low_f, low_b, kv, kr, spec, xs_, ys_, ring = take(20)
+    isem, lsem, zs, zr, xs, xr, ys, yr, fxs, fxr, fys, fyr, ss, sr, ss0, sr0, hs, hr, misc, rsem = refs
     dp, s, z, c = place(4)
     core = (dp, s + 1 - 2 * c)
+    odd = (dp, lax.rem(s + 7 + 2 * c, 8))
     xn = (dp + 1 - 2 * lax.rem(dp, 2), s)
     yn = (lax.rem(dp + 2, 4), s)
-    q = dp; qx = xn[0]; qy = yn[0]; qd = lax.rem(qx + 2, 4)
-    def zdev(k): return (dp, lax.rem(s + 2 * k, 8))
+    q = dp
+    qx = xn[0]
+    qy = yn[0]
+
+    def zdev(k):
+        return (dp, lax.rem(s + 2 * k, 8))
+
+    first = {}
+    for i, (a, b) in enumerate([(wave_in, wave_ref), (tok_in, tok), (cot_in, cot)]):
+        first[i] = pltpu.make_async_copy(a, b, misc.at[i])
+        first[i].start()
+    lins = []
+    for a in range(n):
+        li = pltpu.make_async_copy(src[a], stage[a], isem.at[a])
+        li.start()
+        lins.append(li)
+    halo_rows = 3 * BLK
+
+    @pl.loop(0, halo_rows // 16)
+    def _(r):
+        lo = pl.ds(pl.multiple_of(r * 16, 16), 16)
+        hi = pl.ds(pl.multiple_of(r * 16 + halo_rows + 256, 16), 16)
+        zero = jnp.zeros((16, fb.shape[2]), jnp.bfloat16)
+        for micro in range(2):
+            fb[micro, lo, :] = zero
+            fb[micro, hi, :] = zero
+
     bar = pltpu.get_barrier_semaphore()
-    for d in [core, xn, yn] + [zdev(k) for k in (1, 2, 3)]:
+    for d in [core, odd, xn, yn, zdev(1), zdev(3)]:
         pl.semaphore_signal(bar, inc=1, device_id=d, device_id_type=MESH)
     pl.semaphore_wait(bar, 6)
 
     def rc(a_ref, b_ref, s1, s2, dev):
         return pltpu.make_async_remote_copy(src_ref=a_ref, dst_ref=b_ref, send_sem=s1, recv_sem=s2, device_id=dev, device_id_type=MESH)
+
     g = [GEOM[m] for m in names]
-    sends = []
-    locs = []
-    lins = []
-    zsend = {}
+    locs, own_sib, zsend = [], {}, {}
+    for a in range(n):
+        where = cut(out[a].at[s], g[a], q) if names[a] == "kern" else out[a].at[s]
+        locs.append(pltpu.make_async_copy(stage[a], where, lsem.at[a]))
+
+    def near(way, j):
+        return lax.rem(s + (8 - 2 * j if way == 0 else 2 * j), 8)
+
+    def here(u):
+        a, way, j = u
+        return True if j == 0 else (z >= j if way == 0 else z + j <= 3)
+
+    def when(cond, f):
+        if cond is True:
+            f()
+        else:
+            pl.when(cond)(f)
+
+    def onward(way):
+        return z < 3 if way == 0 else z > 0
+
+    def zgo(a):
+        if a < n:
+            for way in (0, 1):
+                pl.when(onward(way))(zsend[a, way, 0].start)
+
+    def sibgo(a):
+        if a < n and names[a] != "kern":
+            own_sib[a] = rc(src[a], out[a].at[s], ss0.at[a], sr0.at[a], core)
+            own_sib[a].start()
+
+    units = []
     for a in range(n):
         if names[a] == "kern":
-            lc = pltpu.make_async_copy(stage[a], cut(out[a].at[s], g[a], q), lsem.at[a])
+            units.append((a, 0, 0))
+        for j in (1, 2, 3):
+            units += [(a, 0, j), (a, 1, j)]
+    last_unit = {u[0]: i for i, u in enumerate(units)}
+    xc, yc, fx, fy, sb = {}, {}, {}, {}, {}
+    loc_done = set()
+
+    def slot(u):
+        return 6 if u[2] == 0 else u[1] * 3 + u[2] - 1
+
+    def blk(u):
+        return out[u[0]].at[s if u[2] == 0 else near(u[1], u[2])]
+
+    for a in range(n):
+        for way in (0, 1):
+            for j in range(3):
+                if j:
+                    piece = cut(blk((a, way, j)), g[a], q)
+                else:
+                    piece = src[a] if names[a] == "kern" else cut(src[a], g[a], q)
+                there = cut(out[a].at[near(way, j)], g[a], q)
+                zsend[a, way, j] = rc(piece, there, zs.at[a, way * 3 + j], zr.at[a, way * 3 + j], zdev(1 if way == 0 else 3))
+    zin = {}
+    for u in units:
+        a, i = u[0], slot(u)
+        whole = blk(u)
+        b = cut(whole, g[a], q)
+        if u[2]:
+            zin[u] = rc(b, b, zs.at[a, i], zr.at[a, i], zdev(1))
+        if g[a] is not None:
+            xc[u] = rc(b, b, xs.at[a, i], xr.at[a, i], xn)
+            yc[u] = rc(b, b, ys.at[a, i], yr.at[a, i], yn)
+            b = cut(whole, g[a], qx, 0)
+            fy[u] = rc(b, b, fys.at[a, i], fyr.at[a, i], yn)
+            b = cut(whole, g[a], qy, 1)
+            fx[u] = rc(b, b, fxs.at[a, i], fxr.at[a, i], xn)
+        sb[u] = rc(whole, whole, ss.at[a, i], sr.at[a, i], core)
+
+    zgo(0)
+    zgo(1)
+    sibgo(0)
+    sibgo(1)
+    for a in range(n):
+        lins[a].wait()
+        locs[a].start()
+
+    def st1(u):
+        a, way, j = u
+        if j == 0:
+            locs[a].wait()
+            loc_done.add(a)
         else:
-            lc = pltpu.make_async_copy(stage[a], out[a].at[s], lsem.at[a])
-        locs.append(lc)
-        li = pltpu.make_async_copy(src[a], stage[a], isem.at[a]); li.start(); lins.append(li)
-        for k in (1, 2, 3):
-            piece = src[a] if names[a] == "kern" else cut(src[a], g[a], q)
-            cp = rc(piece, cut(out[a].at[s], g[a], q), zs.at[a, k - 1], zr.at[a, k - 1], zdev(k))
-            zsend[a, k] = cp
-    def zgo(a):
-        if a >= n: return
-        for k in (1, 3, 2): zsend[a, k].start()
-    def sibgo(a):
-        if names[a] != "kern":
-            cp = rc(src[a], out[a].at[s], ss0.at[a], sr0.at[a], core)
-            cp.start(); sends.append(cp)
-    for a in range(AHEAD): zgo(a)
-    for a in range(n):
-        lins[a].wait(); locs[a].start()
-    sibgo(0)
-    units = []
-    for a in range(n):
-        if names[a] == "kern": units.append((a, 0))
-        for k in (1, 3, 2): units.append((a, k))
-    xc, yc, fx, fy, sb = {}, {}, {}, {}, {}
-    def blk(a, k):
-        return out[a].at[lax.rem(s + 8 - 2 * k, 8)]
-    def st1(u):
-        a, k = u
-        if k == 0:
+            zin[u].wait_recv()
+            if j < 3:
+                pl.when(onward(way))(zsend[a, way, j].start)
+        if u in xc:
+            xc[u].start()
+            yc[u].start()
+
+    def st2(u):
+        if u in xc:
+            xc[u].wait_recv()
+            fy[u].start()
+            yc[u].wait_recv()
+            fx[u].start()
+
+    def st3(u):
+        if u in xc:
+            fx[u].wait_recv()
+            fy[u].wait_recv()
+        sb[u].start()
+
+    state = {"t": 0}
+    total = len(units) + L3
+
+    def comm():
+        t = state["t"]
+        state["t"] += 1
+        for lag, stage_of in ((0, st1), (L2, st2), (L3, st3)):
+            if 0 <= t - lag < len(units):
+                u = units[t - lag]
+                when(here(u), functools.partial(stage_of, u))
+        if t < len(units) and t == last_unit[units[t][0]]:
+            zgo(units[t][0] + 2)
+            sibgo(units[t][0] + 2)
+
+    def complete(name):
+        a = names.index(name)
+        while state["t"] <= last_unit[a] + L3:
+            comm()
+        if a not in loc_done:
             locs[a].wait()
-        else:
-            zsend[a, k].wait_recv()
-        b = cut(blk(a, k), g[a], q)
-        xc[u] = rc(b, b, xs.at[a, k], xr.at[a, k], xn); xc[u].start()
-        yc[u] = rc(b, b, ys.at[a, k], yr.at[a, k], yn); yc[u].start()
-    def st2(u):
-        a, k = u
-        xc[u].wait_recv()
-        b = cut(blk(a, k), g[a], qx, 0)
-        fy[u] = rc(b, b, fys.at[a, k], fyr.at[a, k], yn); fy[u].start()
-        yc[u].wait_recv()
-        b = cut(blk(a, k), g[a], qy, 1)
-        fx[u] = rc(b, b, fxs.at[a, k], fxr.at[a, k], xn); fx[u].start()
-    def st3(u):
-        a, k = u
-        fx[u].wait_recv(); fy[u].wait_recv()
-        b = blk(a, k)
-        sb[u] = rc(b, b, ss.at[a, k], sr.at[a, k], core); sb[u].start()
-    for t in range(len(units) + L3):
-        if t < len(units):
-            st1(units[t])
-            if units[t][1] == 2:
-                zgo(units[t][0] + AHEAD)
-                if units[t][0] + 1 < n: sibgo(units[t][0] + 1)
-        if 0 <= t - L2 < len(units): st2(units[t - L2])
-        if 0 <= t - L3 < len(units): st3(units[t - L3])
+        if a in own_sib:
+            own_sib[a].wait_recv()
+        for u in units:
+            if u[0] == a:
+                when(here(u), sb[u].wait_recv)
+        return a
+
+    def fetch(pairs, sem0):
+        cps = [pltpu.make_async_copy(x, y, misc.at[sem0 + i]) for i, (x, y) in enumerate(pairs)]
+        for cp in cps:
+            cp.start()
+        for cp in cps:
+            cp.wait()
+
+    for i in range(3):
+        first[i].wait()
+    a = complete("norm")
+    fetch([(out[a], nv)], 3)
+    rows2 = jnp.zeros((16, width), jnp.float32)
+    piece = width // 8
+    for j in range(8):
+        r_ = lax.broadcasted_iota(jnp.int32, (128, width), 0)
+        c_ = lax.broadcasted_iota(jnp.int32, (128, width), 1)
+        spread = jnp.where((c_ == r_ + j * piece) & (r_ < piece), 1.0, 0.0).astype(jnp.bfloat16)
+        rows2 = rows2 + jnp.dot(nv[j], spread, preferred_element_type=jnp.float32)
+    gb[...] = rows2
+
+    @pl.loop(0, 512 // 64)
+    def _(r):
+        rows = pl.ds(pl.multiple_of(r * 64, 64), 64)
+        x = tok[rows, :].astype(jnp.float32)
+        x = x - jnp.mean(x, axis=-1, keepdims=True)
+        var = jnp.mean(x * x, axis=-1, keepdims=True)
+        nl[rows, :] = (x * lax.rsqrt(var + 1e-5) * gb[0:1, :] + gb[1:2, :]).astype(jnp.bfloat16)
+
+    nout = pltpu.make_async_copy(nl, nrm_out, misc.at[4])
+    nout.start()
+
+    a = complete("filter")
+    R = out[a].shape[1]
+    fetch([(out[a].at[j], wa.at[pl.ds(768 + j * R, R), pl.ds(0, 1536)]) for j in range(8)], 5)
+
+    @pl.loop(0, 4)
+    def _(j):
+        cols = pl.ds(pl.multiple_of(j * 384, 128), 384)
+        t = jnp.dot(nl[...], wa[768:1536, cols], preferred_element_type=jnp.float32)
+        pf[:, cols] = t
+        act = gelu_parts(t)[0].astype(jnp.bfloat16)
+        for micro in range(2):
+            fb[micro, halo_rows:halo_rows + 256, cols] = act[micro * 256:(micro + 1) * 256]
+
+    pre_cp = pltpu.make_async_copy(pf.at[:, pl.ds(0, 1536)], pre_out, misc.at[13])
+    pre_cp.start()
+    own_rows = pl.ds(halo_rows, 256)
+    halos = [
+        (1, own_rows, pl.ds(BLK, 256), s < 7, s > 0),
+        (2, pl.ds(halo_rows + BLK, BLK), pl.ds(0, BLK), s < 6, s > 1),
+        (-1, own_rows, pl.ds(halo_rows + 256, 256), s > 0, s < 7),
+        (-2, pl.ds(halo_rows, BLK), pl.ds(halo_rows + 512, BLK), s > 1, s < 6),
+    ]
+    hcps = {}
+    for chunk in range(4):
+        cols = pl.ds(chunk * 384, 384)
+        for i, (by, from_rows, to_rows, sends, recvs) in enumerate(halos):
+            cp = rc(fb.at[:, from_rows, cols], fb.at[:, to_rows, cols], hs.at[chunk, i], hr.at[chunk, i], (dp, lax.rem(s + 8 + by, 8)))
+            hcps[chunk, i] = (cp, sends, recvs)
+
+    def halo_go(chunk):
+        for i in range(4):
+            cp, sends, _ = hcps[chunk, i]
+            pl.when(sends)(cp.start)
+
+    def halo_here(chunk):
+        for i in range(4):
+            cp, _, recvs = hcps[chunk, i]
+            pl.when(recvs)(cp.wait_recv)
+
+    halo_go(0)
+
+    a = complete("value")
+    R = out[a].shape[1]
+    fetch([(out[a].at[j], wa.at[pl.ds(j * R, R)]) for j in range(8)], 5)
+    for half in range(2):
+        @pl.loop(half * 4, half * 4 + 4)
+        def _(j):
+            cols = pl.ds(pl.multiple_of(j * 384, 128), 384)
+            pv[:, cols] = jnp.dot(nl[...], wa[:768, cols], preferred_element_type=jnp.float32)
+
+        comm()
+
+    halo_go(1)
+    a = complete("out")
+    halo_go(2)
+    fetch([(out[a].at[j], wb.at[pl.ds((j % 2) * 384, 384), pl.ds((j // 2) * 768, 768)]) for j in range(8)], 5)
+    for j in range(4):
+        gh[:, j * 768:(j + 1) * 768] = dot(cot[...], wb[:768, j * 768:(j + 1) * 768], 1, 1)
+        comm()
+
+
+    def conv_chunk(chunk):
+        halo_here(chunk)
+        a = names.index("kern")
+        fetch([(out[a].at[pl.ds(2 * chunk, 2)], kv)], 3)
+        for side in range(2):
+            for j in range(2):
+                for p in range(4):
+                    at = (j * 4 + p) * 48
+                    kr[side, at:at + 48] = kv[j, (p * 2 + side) * 48:(p * 2 + side + 1) * 48]
+
+        @pl.loop(0, 3)
+        def _(slab):
+            slab_forward(mask_ref, wave_ref, kr, spec, xs_, ys_, fb, (low_f, low_b), chunk, slab)
+
+    complete("kern")
+    halo_go(3)
+    comm()
+    comm()
+    conv_chunk(0)
+    comm()
+    comm()
+    conv_chunk(1)
+    a = complete("fore")
+    conv_chunk(2)
+    comm()
+    comm()
+    conv_chunk(3)
+    fb_cp = pltpu.make_async_copy(fb, fb_out, misc.at[14])
+    fb_cp.start()
+    low_cp = [pltpu.make_async_copy(low_f, fore_out, misc.at[15]), pltpu.make_async_copy(low_b, back_out, misc.at[16])]
+    for cp in low_cp:
+        cp.start()
+
+    R = out[a].shape[1]
+    pre_cp.wait()
+    fetch([(out[a].at[j], wa.at[pl.ds(j * R, R)]) for j in range(8)], 5)
+    for half in range(2):
+        @pl.loop(half * 4, half * 4 + 4)
+        def _(j):
+            cols = pl.ds(pl.multiple_of(j * 384, 128), 384)
+            pf[:, cols] = jnp.dot(low_f[...], wa[:, cols], preferred_element_type=jnp.float32)
+
+        comm()
+    a = complete("back")
+    R = out[a].shape[1]
+    fetch([(out[a].at[j], wb.at[pl.ds(j * R, R)]) for j in range(8)], 5)
+    dests = (hid_out, gpf_out, gpb_out, gpv_out)
+
+    def ring_cp(j, w):
+        cols = pl.ds(pl.multiple_of(j * 256, 128), 256)
+        return pltpu.make_async_copy(ring.at[lax.rem(j, 2), w], dests[w].at[:, cols], rsem.at[lax.rem(j, 2), w])
+
+    @pl.loop(0, 12)
+    def _(j):
+        cols = pl.ds(pl.multiple_of(j * 256, 128), 256)
+        slot = lax.rem(j, 2)
+
+        @pl.when(j >= 2)
+        def _():
+            for w in range(4):
+                ring_cp(j - 2, w).wait()
+
+        pb = jnp.dot(low_b[...], wb[:, cols], preferred_element_type=jnp.float32)
+        p = pf[:, cols]
+        va, dva = gelu_parts(pv[:, cols])
+        h = gh[:, cols]
+        hv = h * va
+        ring[slot, 0] = (p * pb * va).astype(jnp.bfloat16)
+        ring[slot, 1] = (hv * pb).astype(jnp.bfloat16)
+        ring[slot, 2] = (hv * p).astype(jnp.bfloat16)
+        ring[slot, 3] = (h * p * pb * dva).astype(jnp.bfloat16)
+        for w in range(4):
+            ring_cp(j, w).start()
+
+    for j in (10, 11):
+        for w in range(4):
+            ring_cp(j, w).wait()
+
+    nout.wait()
+    fb_cp.wait()
+    for cp in low_cp:
+        cp.wait()
+    for cp, sends, recvs in hcps.values():
+        pl.when(sends)(cp.wait_send)
     for u in units:
-        a, k = u
-        sb[u].wait_recv()
-        for d in (xc, yc, fx, fy, sb): d[u].wait_send()
-    for cp in zsend.values(): cp.wait_send()
-    for cp in sends: cp.wait()
-    for a in range(n):
-        if names[a] != "kern": locs[a].wait()
-
-def gather_weights(names, arrs):
-    n = len(names)
-    shapes = []
-    for m, a in zip(names, arrs):
-        R, C = a.shape
-        if m == "kern": R = R * 4
-        shapes.append(jax.ShapeDtypeStruct((8, R, C), a.dtype))
+        def left():
+            for d in (xc, yc, fx, fy, sb):
+                if u in d:
+                    d[u].wait_send()
+
+        when(here(u), left)
+    for (a, way, j), cp in zsend.items():
+        gone = here((a, way, j))
+        more = onward(way)
+        when(more if gone is True else gone & more, cp.wait_send)
+    for cp in own_sib.values():
+        cp.wait_send()
+
+
+def gather_forward(mask, tokens, cot, shards):
+    rows, width = tokens.shape
+    n = len(FETCH)
     D = pltpu.SemaphoreType.DMA
+    V = lambda sh, t=jnp.bfloat16: pltpu.VMEM(sh, t)
+    full = []
+    for m in FETCH:
+        R, C = shards[m].shape
+        full.append(jax.ShapeDtypeStruct((8, R * (4 if m == "kern" else 1), C), jnp.bfloat16))
+    FH, FFN = shards["filter"].shape[1], shards["value"].shape[1]
+    f32 = jnp.float32
+    S = lambda sh, t=jnp.bfloat16: jax.ShapeDtypeStruct(sh, t)
+    extra = [S((rows, FH), f32), S((2, 1024, FH)), S((rows, FH)), S((rows, FH))] + [S((rows, FFN))] * 4 + [S((rows, width))]
+    any_ = pl.BlockSpec(memory_space=pl.ANY)
+    wave = jnp.asarray(wave_tables(), jnp.bfloat16)
     outs = pl.pallas_call(
-        functools.partial(ag_kernel, names),
-        out_shape=shapes,
-        in_specs=[pl.BlockSpec(memory_space=pl.ANY)] * n,
-        out_specs=[pl.BlockSpec(memory_space=pl.ANY)] * n,
-        scratch_shapes=[pltpu.VMEM(a.shape, a.dtype) for a in arrs] + [D((n,)), D((n,)), D((n, 3)), D((n, 3))] + [D((n, 4))] * 10 + [D((n,)), D((n,))],
-        compiler_params=pltpu.CompilerParams(collective_id=0, has_side_effects=True),
-    )(*arrs)
-    return outs
-
-
-SLOTS = 3
-LB, LC, LD, LE = 1, 2, 3, 4
+        functools.partial(forward_kernel, width),
+        out_shape=full + extra,
+        in_specs=[pl.BlockSpec(memory_space=pltpu.SMEM)] + [any_] * (3 + n),
+        out_specs=[any_] * (n + len(extra)),
+        scratch_shapes=[V(shards[m].shape) for m in FETCH]
+        + [V(wave.shape), V((rows, width)), V((rows, width)), V((8, 16, 128)), V((16, width), f32), V((rows, width))]
+        + [V((FH, FFN)), V((FH, FFN)), V((rows, FFN), f32), V((rows, FFN), f32), V((rows, FFN), f32)]
+        + [V((2, 1024, FH)), V((rows, FH)), V((rows, FH)), V((2, 384, 512)), V((2, 384, 512))]
+        + [V((2, 4, 256, 128), f32), V((8, 256, 128), f32), V((2, 2, 256, 128), f32), V((2, 4, rows, 256))]
+        + [D((n,)), D((n,)), D((n, 6)), D((n, 6))]
+        + [D((n, 7))] * 10
+        + [D((n,)), D((n,)), D((4, 4)), D((4, 4)), D((17,)), D((2, 4))],
+        compiler_params=pltpu.CompilerParams(collective_id=0, has_side_effects=True, vmem_limit_bytes=int(63.5 * 2**20)),
+        cost_estimate=pl.CostEstimate(flops=20 * 10**9, bytes_accessed=2 * 10**8, transcendentals=0),
+    )(mask, wave, tokens, cot, *[shards[m] for m in FETCH])
+    return dict(zip(FETCH, outs[:n])), outs[n:]
+
+
+L2, L3 = 3, 6
+
+
+ORDER = ("out", "fore", "back", "value", "kern", "filter")
+DEPTH = 3
+
 
 def add_into(dst, srcs):
     R = dst.shape[-2]
+
     @pl.loop(0, R // 16)
     def _(r):
         rows = pl.ds(pl.multiple_of(r * 16, 16), 16)
         t = dst[rows, :].astype(jnp.float32)
         for s_ in srcs:
             t = t + s_[rows, :].astype(jnp.float32)
-        dst[rows, :] = t.astype(jnp.bfloat16)
-
-def rs_kernel(names, *refs):
-    n = len(names)
-    G = refs[:n]; out = refs[n:2 * n]
-    P = refs[2 * n:3 * n]; bx = refs[3 * n:4 * n]; by = refs[4 * n:5 * n]; bc = refs[5 * n:6 * n]
-    stg = refs[6 * n]
-    lsem, as_, ar, xs, xr, ys, yr, cs, cr, gxs, gxr, gys, gyr, hxs, hxr, hys, hyr, osem = refs[6 * n + 1:]
+        dst[rows, :] = t.astype(dst.dtype)
+
+
+def grad_kernel(acts, rights, *refs):
+    refs = list(refs)
+    take = lambda n: [refs.pop(0) for _ in range(n)]
+    act_in = dict(zip(acts, take(len(acts))))
+    right_in = dict(zip(rights, take(len(rights))))
+    kern_in, norm_in = take(2)
+    out = dict(zip(ORDER, take(len(ORDER))))
+    norm_out, = take(1)
+    act = dict(zip(acts, take(len(acts))))
+    right = dict(zip(rights, take(len(rights))))
+    P = dict(zip(ORDER, take(len(ORDER))))
+    bx = dict(zip(ORDER, take(len(ORDER))))
+    by = dict(zip(ORDER, take(len(ORDER))))
+    bc = dict(zip(ORDER, take(len(ORDER))))
+    snd, stg, nbuf = take(3)
+    isem, ksem, as_, ar, xs, xr, ys, yr, cs, cr, gxs, gxr, gys, gyr, hxs, hxr, hys, hyr, osem, ns, nr = refs
     dp, s, z, c = place(4)
     core = (dp, s + 1 - 2 * c)
     xn = (dp + 1 - 2 * lax.rem(dp, 2), s)
     yn = (lax.rem(dp + 2, 4), s)
-    q = dp; qx = xn[0]; qy = yn[0]; qd = lax.rem(qx + 2, 4)
-    def zdev(k): return (dp, lax.rem(s + 2 * k, 8))
+    q = dp
+    qx = xn[0]
+    qy = yn[0]
+    qd = lax.rem(qx + 2, 4)
+
+    def zdev(k):
+        return (dp, lax.rem(s + 2 * k, 8))
+
+    loads = {}
+    for i, m in enumerate(acts):
+        loads["a", m] = pltpu.make_async_copy(act_in[m], act[m], isem.at[i])
+    for i, m in enumerate(rights):
+        loads["r", m] = pltpu.make_async_copy(right_in[m], right[m], isem.at[len(acts) + i])
+    for m in ORDER:
+        for kind, group in (("a", acts), ("r", rights)):
+            if m in group:
+                loads[kind, m].start()
+    kload = pltpu.make_async_copy(kern_in, stg, ksem)
+    kload.start()
     bar = pltpu.get_barrier_semaphore()
     for d in [core, xn, yn] + [zdev(k) for k in (1, 2, 3)]:
         pl.semaphore_signal(bar, inc=1, device_id=d, device_id_type=MESH)
     pl.semaphore_wait(bar, 6)
+
     def rc(a_ref, b_ref, s1, s2, dev):
         return pltpu.make_async_remote_copy(src_ref=a_ref, dst_ref=b_ref, send_sem=s1, recv_sem=s2, device_id=dev, device_id_type=MESH)
-    g = [GEOM[m] for m in names]
-    units = [(a, k) for a in range(n) for k in (1, 2, 3, 0)]
-    pend = []
-    A, X, Y, C, LCP = {}, {}, {}, {}, {}
+
+    g = GEOM
+    units = [(m, k) for m in ORDER for k in (1, 2, 3, 0)]
+    at = {m: j for j, m in enumerate(ORDER)}
+    A, X, Y, C, waited = {}, {}, {}, {}, set()
+
+    def ready(kind, m):
+        if (kind, m) not in waited:
+            waited.add((kind, m))
+            loads[kind, m].wait()
+
     def so(k, other):
         base = lax.rem(s + 2 * k, 8)
         return base + 1 - 2 * c if other else base
+
+    def product(m, shard, put):
+        R, cols = P[m].shape[-2:]
+        step = 768 if R <= 192 else 384
+        left = act[m].at[shard]
+
+        @pl.loop(0, cols // step)
+        def _(j):
+            at_cols = pl.ds(pl.multiple_of(j * step, 128), step)
+            put(at_cols, jnp.dot(left[...], right[m][:, at_cols], preferred_element_type=jnp.float32))
+
     def stA(i):
-        a, k = units[i]
-        A[i] = rc(G[a].at[so(k, True)], P[a].at[k], as_.at[a, k], ar.at[a, k], core); A[i].start()
-    def load(i):
-        a, k = units[i]
-        R, Cc = G[a].shape[-2:]
-        LCP[i] = pltpu.make_async_copy(G[a].at[so(k, False)], stg.at[i % SLOTS, pl.ds(0, R), pl.ds(0, Cc)] if False else stg[a].at[i % SLOTS], lsem.at[i % SLOTS])
-        LCP[i].start()
+        m, k = units[i]
+        j = at[m]
+        if m == "kern":
+            if k == 1:
+                kload.wait()
+            A[i] = rc(stg.at[so(k, True)], P[m].at[k], as_.at[j, k], ar.at[j, k], core)
+        else:
+            ready("a", m)
+            ready("r", m)
+            back = [u for u in range(i) if units[u][0] != "kern"]
+            if len(back) >= DEPTH:
+                A[back[-DEPTH]].wait_send()
+            slot = len(back) % DEPTH
+            R, cols = P[m].shape[-2:]
+            buf = snd.at[slot, pl.ds(0, R), pl.ds(0, cols)]
+
+            def put(cs_, t):
+                buf[:, cs_] = t.astype(jnp.bfloat16)
+
+            product(m, so(k, True), put)
+            A[i] = rc(buf, P[m].at[k], as_.at[j, k], ar.at[j, k], core)
+        A[i].start()
+
     def stB(i):
-        a, k = units[i]
-        A[i].wait_recv(); LCP[i].wait()
-        p = P[a].at[k]
-        add_into(p, [stg[a].at[i % SLOTS]])
-        X[i, 1] = rc(cut(p, g[a], qd, 0), bx[a].at[k, 1], xs.at[a, k, 1], xr.at[a, k, 1], xn)
-        X[i, 0] = rc(cut(p, g[a], qx, 0), bx[a].at[k, 0], xs.at[a, k, 0], xr.at[a, k, 0], xn)
-        Y[i, 1] = rc(cut(p, g[a], qd, 1), by[a].at[k, 1], ys.at[a, k, 1], yr.at[a, k, 1], yn)
-        Y[i, 0] = rc(cut(p, g[a], qy, 1), by[a].at[k, 0], ys.at[a, k, 0], yr.at[a, k, 0], yn)
-        for j in (1, 0): X[i, j].start(); Y[i, j].start()
+        m, k = units[i]
+        j = at[m]
+        A[i].wait_recv()
+        p = P[m].at[k]
+        if m == "kern":
+            add_into(p, [stg.at[so(k, False)]])
+        else:
+            def put(cs_, t):
+                p[:, cs_] = (p[:, cs_].astype(jnp.float32) + t).astype(jnp.bfloat16)
+
+            product(m, so(k, False), put)
+        X[i, 1] = rc(cut(p, g[m], qd, 0), bx[m].at[k, 1], xs.at[j, k, 1], xr.at[j, k, 1], xn)
+        X[i, 0] = rc(cut(p, g[m], qx, 0), bx[m].at[k, 0], xs.at[j, k, 0], xr.at[j, k, 0], xn)
+        Y[i, 1] = rc(cut(p, g[m], qd, 1), by[m].at[k, 1], ys.at[j, k, 1], yr.at[j, k, 1], yn)
+        Y[i, 0] = rc(cut(p, g[m], qy, 1), by[m].at[k, 0], ys.at[j, k, 0], yr.at[j, k, 0], yn)
+        for w in (1, 0):
+            X[i, w].start()
+            Y[i, w].start()
+
     def stC(i):
-        a, k = units[i]
-        p = P[a].at[k]
+        m, k = units[i]
+        j = at[m]
+        p = P[m].at[k]
         X[i, 1].wait_recv()
-        add_into(cut(p, g[a], qy, 0), [bx[a].at[k, 1]])
-        Y[i, 2] = rc(cut(p, g[a], qy, 0), by[a].at[k, 2], ys.at[a, k, 2], yr.at[a, k, 2], yn); Y[i, 2].start()
+        add_into(cut(p, g[m], qy, 0), [bx[m].at[k, 1]])
+        Y[i, 2] = rc(cut(p, g[m], qy, 0), by[m].at[k, 2], ys.at[j, k, 2], yr.at[j, k, 2], yn)
+        Y[i, 2].start()
         Y[i, 1].wait_recv()
-        add_into(cut(p, g[a], qx, 1), [by[a].at[k, 1]])
-        X[i, 2] = rc(cut(p, g[a], qx, 1), bx[a].at[k, 2], xs.at[a, k, 2], xr.at[a, k, 2], xn); X[i, 2].start()
+        add_into(cut(p, g[m], qx, 1), [by[m].at[k, 1]])
+        X[i, 2] = rc(cut(p, g[m], qx, 1), bx[m].at[k, 2], xs.at[j, k, 2], xr.at[j, k, 2], xn)
+        X[i, 2].start()
+
     def stD(i):
-        a, k = units[i]
-        p = P[a].at[k]
-        X[i, 0].wait_recv(); Y[i, 2].wait_recv()
-        add_into(cut(p, g[a], q, 0), [bx[a].at[k, 0], by[a].at[k, 2]])
-        Y[i, 0].wait_recv(); X[i, 2].wait_recv()
-        add_into(cut(p, g[a], q, 1), [by[a].at[k, 0], bx[a].at[k, 2]])
+        m, k = units[i]
+        j = at[m]
+        p = P[m].at[k]
+        X[i, 0].wait_recv()
+        Y[i, 2].wait_recv()
+        add_into(cut(p, g[m], q, 0), [bx[m].at[k, 0], by[m].at[k, 2]])
+        Y[i, 0].wait_recv()
+        X[i, 2].wait_recv()
+        add_into(cut(p, g[m], q, 1), [by[m].at[k, 0], bx[m].at[k, 2]])
         if k:
-            C[i] = rc(cut(p, g[a], q), bc[a].at[k - 1], cs.at[a, k - 1], cr.at[a, k - 1], zdev(k)); C[i].start()
+            C[i] = rc(cut(p, g[m], q), bc[m].at[k - 1], cs.at[j, k - 1], cr.at[j, k - 1], zdev(k))
+            C[i].start()
+
     ag = {}
-    def stE(a):
-        for k in (1, 2, 3): C[units.index((a, k))].wait_recv()
-        p = cut(P[a].at[0], g[a], q)
-        add_into(p, [bc[a].at[j] for j in range(3)])
-        own = out[a] if names[a] == "kern" else cut(out[a], g[a], q)
-        o = pltpu.make_async_copy(p, own, osem.at[a]); o.start()
-        ag[a, "o"] = o
-        if names[a] != "kern":
-            ag[a, "x"] = rc(p, own, gxs.at[a], gxr.at[a], xn); ag[a, "x"].start()
-            ag[a, "y"] = rc(p, own, gys.at[a], gyr.at[a], yn); ag[a, "y"].start()
-    def stF(a):
-        if names[a] == "kern": return
-        ag[a, "x"].wait_recv()
-        b = cut(out[a], g[a], qx, 0)
-        ag[a, "fy"] = rc(b, b, hys.at[a], hyr.at[a], yn); ag[a, "fy"].start()
-        ag[a, "y"].wait_recv()
-        b = cut(out[a], g[a], qy, 1)
-        ag[a, "fx"] = rc(b, b, hxs.at[a], hxr.at[a], xn); ag[a, "fx"].start()
-    N = len(units)
-    for i in range(min(AHEAD_A, N)): stA(i)
-    for i in range(min(SLOTS - 1, N)): load(i)
-    for t in range(N + LE + 5):
-        if t < N:
-            if t + AHEAD_A < N: stA(t + AHEAD_A)
-            if t + SLOTS - 1 < N: load(t + SLOTS - 1)
+
+    def stE(m):
+        j = at[m]
+        for k in (1, 2, 3):
+            C[units.index((m, k))].wait_recv()
+        p = cut(P[m].at[0], g[m], q)
+        add_into(p, [bc[m].at[w] for w in range(3)])
+        own = out[m] if m == "kern" else cut(out[m], g[m], q)
+        ag[m, "o"] = pltpu.make_async_copy(p, own, osem.at[j])
+        ag[m, "o"].start()
+        if m != "kern":
+            ag[m, "x"] = rc(p, own, gxs.at[j], gxr.at[j], xn)
+            ag[m, "y"] = rc(p, own, gys.at[j], gyr.at[j], yn)
+            ag[m, "x"].start()
+            ag[m, "y"].start()
+
+    def stF(m):
+        if m == "kern":
+            return
+        j = at[m]
+        ag[m, "x"].wait_recv()
+        b = cut(out[m], g[m], qx, 0)
+        ag[m, "fy"] = rc(b, b, hys.at[j], hyr.at[j], yn)
+        ag[m, "fy"].start()
+        ag[m, "y"].wait_recv()
+        b = cut(out[m], g[m], qy, 1)
+        ag[m, "fx"] = rc(b, b, hxs.at[j], hxr.at[j], xn)
+        ag[m, "fx"].start()
+
+    nload = pltpu.make_async_copy(norm_in, nbuf.at[0], ns.at[6])
+    nload.start()
+    N = {}
+
+    def norm_step(w):
+        if w == 0:
+            nload.wait()
+            N[0] = rc(nbuf.at[0], nbuf.at[1], ns.at[0], nr.at[0], core)
+            N[0].start()
+        elif w in (1, 2):
+            N[w - 1].wait()
+            nbuf[0] = nbuf[0] + nbuf[w]
+            N[w] = rc(nbuf.at[0], nbuf.at[w + 1], ns.at[w], nr.at[w], xn if w == 1 else yn)
+            N[w].start()
+        elif w == 3:
+            N[2].wait()
+            nbuf[0] = nbuf[0] + nbuf[3]
+            for k in (1, 2, 3):
+                N[2 + k] = rc(nbuf.at[0, so(k, False)], nbuf.at[4, k], ns.at[2 + k], nr.at[2 + k], zdev(k))
+                N[2 + k].start()
+        elif w == 4:
+            for k in (1, 2, 3):
+                N[2 + k].wait()
+            nbuf[4, 0] = nbuf[0, s] + nbuf[4, 1] + nbuf[4, 2] + nbuf[4, 3]
+            N[6] = pltpu.make_async_copy(nbuf.at[4, 0], norm_out, ns.at[7])
+            N[6].start()
+
+    n = len(units)
+    ahead = DEPTH - 1
+    for i in range(ahead):
+        stA(i)
+    for t in range(n + LE + 4):
+        if t < n:
+            if t + ahead < n:
+                stA(t + ahead)
             stB(t)
-        if 0 <= t - LC < N: stC(t - LC)
-        if 0 <= t - LD < N: stD(t - LD)
+        if 0 <= t - LC < n:
+            stC(t - LC)
+        if 0 <= t - LD < n:
+            stD(t - LD)
         j = t - LE
-        if 0 <= j < N and j % 4 == 3: stE(j // 4)
+        if 0 <= j < n and j % 4 == 3:
+            stE(units[j][0])
         j = t - LE - 2
-        if 0 <= j < N and j % 4 == 3: stF(j // 4)
-    for a in range(n):
-        if names[a] != "kern":
-            for w in ("fx", "fy"): ag[a, w].wait()
-            for w in ("x", "y"): ag[a, w].wait_send()
-        ag[a, "o"].wait()
-    for d in (A, X, Y, C):
-        for v in d.values(): v.wait_send()
-AHEAD_A = 3
-
-def halfshape(m, R, C):
+        if 0 <= j < n and j % 4 == 3:
+            stF(units[j][0])
+        if t >= 4 and t % 2 == 0 and t // 2 - 2 < 5:
+            norm_step(t // 2 - 2)
+    for m in ORDER:
+        if m != "kern":
+            for w in ("fx", "fy"):
+                ag[m, w].wait()
+            for w in ("x", "y"):
+                ag[m, w].wait_send()
+        ag[m, "o"].wait()
+    N[6].wait()
+    plain = [u for u in range(n) if units[u][0] != "kern"][-DEPTH:]
+    for i in A:
+        if i in plain or units[i][0] == "kern":
+            A[i].wait_send()
+    for d in (X, Y, C):
+        for v in d.values():
+            v.wait_send()
+
+
+LC, LD, LE = 1, 2, 3
+
+
+def half_shape(m, R, C):
     return (R // 2, C // 4) if GEOM[m] == "col" else (R // 8, C)
-def qshape(m, R, C):
+
+
+def quarter_shape(m, R, C):
     return (R, C // 4) if GEOM[m] == "col" else (R // 4, C)
 
-def reduce_weights(names, arrs):
-    n = len(names)
+
+def reduce_gradients(act, right, kern, norm):
     D = pltpu.SemaphoreType.DMA
     V = lambda sh: pltpu.VMEM(sh, jnp.bfloat16)
-    shp = [a.shape[1:] for a in arrs]
+    shp = {m: kern.shape[1:] if m == "kern" else (act[m].shape[1], right[m].shape[1]) for m in ORDER}
+    n = len(ORDER)
+    acts, rights = tuple(act), tuple(right)
+    any_ = pl.BlockSpec(memory_space=pl.ANY)
+    snd = max(shp[m][0] for m in acts), max(shp[m][1] for m in acts)
     outs = pl.pallas_call(
-        functools.partial(rs_kernel, names),
-        out_shape=[jax.ShapeDtypeStruct(qshape(m, *sh) if m == "kern" else sh, jnp.bfloat16) for m, sh in zip(names, shp)],
-        in_specs=[pl.BlockSpec(memory_space=pl.ANY)] * n,
-        out_specs=[pl.BlockSpec(memory_space=pl.ANY)] * n,
-        scratch_shapes=[V((4,) + sh) for sh in shp]
-        + [V((4, 3) + halfshape(m, *sh)) for m, sh in zip(names, shp)] * 2
-        + [V((3,) + qshape(m, *sh)) for m, sh in zip(names, shp)]
-        + [[V((SLOTS,) + sh) for sh in shp]]
-        + [D((SLOTS,)), D((n, 4)), D((n, 4))] + [D((n, 4, 3))] * 4 + [D((n, 3))] * 2 + [D((n,))] * 9,
-        compiler_params=pltpu.CompilerParams(collective_id=1, has_side_effects=True, vmem_limit_bytes=62 * 2**20),
-    )(*arrs)
-    return outs
+        functools.partial(grad_kernel, acts, rights),
+        out_shape=[jax.ShapeDtypeStruct(quarter_shape(m, *shp[m]) if m == "kern" else shp[m], jnp.bfloat16) for m in ORDER]
+        + [jax.ShapeDtypeStruct(norm.shape[1:], jnp.float32)],
+        in_specs=[any_] * (len(acts) + len(rights) + 2),
+        out_specs=[any_] * (n + 1),
+        scratch_shapes=[V(act[m].shape) for m in acts]
+        + [V(right[m].shape) for m in rights]
+        + [V((4,) + shp[m]) for m in ORDER]
+        + [V((4, 3) + half_shape(m, *shp[m])) for m in ORDER] * 2
+        + [V((3,) + quarter_shape(m, *shp[m])) for m in ORDER]
+        + [V((DEPTH,) + snd), V(kern.shape), pltpu.VMEM((5,) + norm.shape, jnp.float32)]
+        + [D((len(acts) + len(rights),)), D(()), D((n, 4)), D((n, 4))]
+        + [D((n, 4, 3))] * 4
+        + [D((n, 3))] * 2
+        + [D((n,))] * 9
+        + [D((8,))] * 2,
+        compiler_params=pltpu.CompilerParams(collective_id=1, has_side_effects=True, vmem_limit_bytes=63 * 2**20),
+        cost_estimate=pl.CostEstimate(flops=16 * 10**9, bytes_accessed=10**8, transcendentals=0),
+    )(*[act[m] for m in acts], *[right[m] for m in rights], kern, norm)
+    return dict(zip(ORDER, outs[:-1])), outs[-1]
 
 
 STEP_A = 32
@@ -618,71 +1136,72 @@
 
     coef, rate, freq = mine(ssm_coef), mine(ssm_rate), mine(ssm_freq)
     kernels = make_kernels(coef, rate, freq).astype(LOW)
+    mask = same_item(lengths[:, 0], rows_each // BLK, n_seq).reshape(-1)
+    wave = jnp.asarray(wave_tables(), LOW)
+    tile_step = max(1, 384 // channels)
+    cot_rows = cotangent.reshape(rows, width)
+    token_rows = tokens.reshape(rows, width).astype(F32)
     if linked:
-        own = {"filter": w_filter, "kern": kernels, "value": w_value, "fore": w_fore, "back": w_back, "out": w_out}
-        names = tuple(own)
-        gathered = dict(zip(names, gather_weights(names, [own[m] for m in names])))
-        kern = gathered["kern"].reshape(n_seq, parts, 2, some, LONG)
+        pack = jnp.pad(jnp.stack([ln_gain, ln_bias]), ((0, 14), (0, 128 - ln_gain.shape[0])))
+        own = {"norm": pack, "filter": w_filter, "kern": kernels, "value": w_value, "fore": w_fore, "back": w_back, "out": w_out}
+        gathered, made = gather_forward(mask, tokens.reshape(rows, width), cot_rows, own)
+        pre_filter, filter_near, fore_low, back_low, hidden_low, grad_proj_fore, grad_proj_back, grad_pre_value, normed_low = made
+        kern = gathered.pop("kern").reshape(n_seq, parts, 2, some, LONG)
+        norm = gathered.pop("norm")[:, :2, : ln_gain.shape[0]].astype(F32)
+        gain, bias = norm[:, 0].reshape(-1), norm[:, 1].reshape(-1)
+        full = {m: a.reshape(-1, a.shape[-1]) for m, a in gathered.items()}
+        around = [filter_near]
     else:
         own = {"filter": w_filter, "value": w_value, "fore": w_fore, "back": w_back, "out": w_out}
-        gathered = {m: lax.all_gather(a, "seq", axis=0) for m, a in own.items()}
+        full = {m: lax.all_gather(a, "seq", axis=0, tiled=True) for m, a in own.items()}
         kern = lax.all_gather(kernels.reshape(1, 2, some, LONG), "seq", axis=0)
-    full = {m: a.reshape(-1, a.shape[-1]) for m, a in gathered.items() if m != "kern"}
-    gain = lax.all_gather(ln_gain, "seq", axis=0, tiled=True).astype(F32)
-    bias = lax.all_gather(ln_bias, "seq", axis=0, tiled=True).astype(F32)
-    tile_step = max(1, 384 // channels)
-    wave = jnp.asarray(wave_tables(), LOW)
-    mask = same_item(lengths[:, 0], rows_each // BLK, n_seq).reshape(-1)
-
-    token_rows = tokens.reshape(rows, width).astype(F32)
-    normed, norm_pull = jax.vjp(layer_norm, token_rows, gain, bias)
-    normed_low = normed.astype(LOW)
-    pre_filter = dot_plain(normed_low, full["filter"])
-    filter_act, filter_pull = jax.vjp(jax.nn.gelu, pre_filter)
-    filter_low = filter_act.astype(LOW).reshape(micros, rows_each, -1)
-    around = from_left(filter_low, n_seq) + [filter_low] + from_right(filter_low, n_seq)
-    pre_value = dot_plain(normed_low, full["value"])
-    value_act, value_pull = jax.vjp(jax.nn.gelu, pre_value)
-    fore_low, back_low = [a.reshape(rows, -1) for a in conv_forward(mask, wave, kern, around, tile_step)]
-    proj_fore = dot_plain(fore_low, full["fore"])
-    proj_back = dot_plain(back_low, full["back"])
-    hidden_low = (proj_fore * proj_back * value_act).astype(LOW)
+        gain = lax.all_gather(ln_gain, "seq", axis=0, tiled=True).astype(F32)
+        bias = lax.all_gather(ln_bias, "seq", axis=0, tiled=True).astype(F32)
+        normed_low = layer_norm(token_rows, gain, bias).astype(LOW)
+        pre_filter = dot_plain(normed_low, full["filter"])
+        filter_low = jax.nn.gelu(pre_filter).astype(LOW).reshape(micros, rows_each, -1)
+        around = from_left(filter_low, n_seq) + [filter_low] + from_right(filter_low, n_seq)
+        pre_value = dot_plain(normed_low, full["value"])
+        value_act, value_pull = jax.vjp(jax.nn.gelu, pre_value)
+        fore_low, back_low = [a.reshape(rows, -1) for a in conv_forward(mask, wave, kern, around, tile_step)]
+        proj_fore = dot_plain(fore_low, full["fore"])
+        proj_back = dot_plain(back_low, full["back"])
+        hidden_low = (proj_fore * proj_back * value_act).astype(LOW)
+        grad_hidden = dot_outer(cot_rows, full["out"])
+        grad_proj_fore = (grad_hidden * proj_back * value_act).astype(LOW)
+        grad_proj_back = (grad_hidden * proj_fore * value_act).astype(LOW)
+        grad_pre_value = value_pull(grad_hidden * proj_fore * proj_back)[0].astype(LOW)
+    filter_pull = jax.vjp(jax.nn.gelu, pre_filter)[1]
+    norm_pull = jax.vjp(layer_norm, token_rows, gain, bias)[1]
     mixed = (token_rows + dot_plain(hidden_low, full["out"])).astype(LOW).reshape(tokens.shape)
 
-    cot_rows = cotangent.reshape(rows, width)
-    grad_hidden = dot_outer(cot_rows, full["out"])
-    grad_proj_fore = (grad_hidden * proj_back * value_act).astype(LOW)
-    grad_proj_back = (grad_hidden * proj_fore * value_act).astype(LOW)
-    grad_pre_value = value_pull(grad_hidden * proj_fore * proj_back)[0].astype(LOW)
-    grad_fore_low = dot_outer(grad_proj_fore, full["fore"]).astype(LOW).reshape(filter_low.shape)
-    grad_back_low = dot_outer(grad_proj_back, full["back"]).astype(LOW).reshape(filter_low.shape)
+    grad_fore_low = dot_outer(grad_proj_fore, full["fore"]).astype(LOW).reshape(micros, rows_each, -1)
+    grad_back_low = dot_outer(grad_proj_back, full["back"]).astype(LOW).reshape(micros, rows_each, -1)
     fore_around = [grad_fore_low] + from_right(grad_fore_low, n_seq)
     back_around = from_left(grad_back_low, n_seq) + [grad_back_low]
-    grads = {}
-    grads["out"] = dot_inner(hidden_low, cot_rows)
-    grads["fore"] = dot_inner(fore_low, grad_proj_fore)
-    grads["back"] = dot_inner(back_low, grad_proj_back)
-    grads["value"] = dot_inner(normed_low, grad_pre_value)
     grad_filter_low, grad_kern = conv_backward(mask, wave, kern, around, fore_around, back_around, tile_step)
     grad_pre_filter = filter_pull(grad_filter_low.reshape(rows, -1).astype(F32))[0].astype(LOW)
-    grads["filter"] = dot_inner(normed_low, grad_pre_filter)
     grad_normed = dot_outer(grad_pre_value, full["value"]) + dot_outer(grad_pre_filter, full["filter"])
     grad_rows, gain_grad, bias_grad = norm_pull(grad_normed)
     grad_tokens = (cot_rows.astype(F32) + grad_rows).astype(LOW).reshape(tokens.shape)
 
-    grads = {m: a.reshape(n_seq, -1, a.shape[-1]) for m, a in grads.items()}
+    left = {"out": hidden_low, "fore": fore_low, "back": back_low, "value": normed_low, "filter": normed_low}
+    right = {"out": cot_rows, "fore": grad_proj_fore, "back": grad_proj_back, "value": grad_pre_value, "filter": grad_pre_filter}
+    grad_kern = grad_kern.reshape(n_seq, -1, LONG)
+    norm_grads = jnp.stack([gain_grad, bias_grad]).reshape(2, n_seq, -1)
     if linked:
-        grads = {m: a.astype(LOW) for m, a in grads.items()}
-        order = ("out", "fore", "back", "kern", "value", "filter")
-        grads["kern"] = grad_kern.reshape(n_seq, -1, LONG)
-        sums = dict(zip(order, reduce_weights(order, [grads[m] for m in order])))
+        pack = jnp.pad(jnp.swapaxes(norm_grads, 0, 1), ((0, 0), (0, 6), (0, 128 - norm_grads.shape[2])))
+        left = {m: jnp.transpose(a).reshape(n_seq, -1, rows) for m, a in left.items()}
+        sums, norm_grads = reduce_gradients(left, right, grad_kern, pack)
         sums = {m: a.astype(F32) for m, a in sums.items()}
+        norm_grads = norm_grads[:2, : ln_gain.shape[0]]
     else:
-        grads["kern"] = grad_kern.reshape(n_seq, -1, LONG)
-        sums = {m: lax.psum_scatter(a.astype(F32), "seq", scatter_dimension=0, tiled=False) for m, a in grads.items()}
+        grads = {m: dot_inner(left[m], right[m]).reshape(n_seq, -1, right[m].shape[1]) for m in left}
+        grads["kern"] = grad_kern.astype(F32)
+        sums = {m: lax.psum_scatter(a, "seq", scatter_dimension=0, tiled=False) for m, a in grads.items()}
         sums = {m: lax.psum(a, "dp") for m, a in sums.items()}
-    norm_grads = lax.psum(jnp.stack([gain_grad, bias_grad]), ("dp", "seq"))
-    norm_grads = lax.dynamic_slice_in_dim(norm_grads, lax.axis_index("seq") * ln_gain.shape[0], ln_gain.shape[0], 1)
+        norm_grads = lax.psum_scatter(norm_grads, "seq", scatter_dimension=1, tiled=False)
+        norm_grads = lax.psum(norm_grads, "dp")
     modes_grad = jnp.stack(pull_kernels(sums["kern"], coef, rate, freq)).reshape(3, 2, some, modes)
     if linked:
         modes_grad = lax.all_gather(modes_grad, "dp", axis=2, tiled=True)

time: 672 us -> 544 us (0.81)
  matrix products: 125 us -> 35 us
  blocking collectives: 68.1 us -> 9.79 us
  Pallas kernels: 365 us -> 418 us
  starting transfers between devices: 29.8 us -> 10.9 us
  waiting for transfers between devices: 13.2 us -> 0.01 us
    pallas_call x2, Pallas kernels: 308 us -> 382 us  [the longest x1 195 us: reduce_gradients(): pl.pallas_call(functools.partial(grad_kernel, acts, rights), out_shape=[j...]
    dot_general x5 -> x1, matrix products: 48.9 us -> 6.77 us  [dot_plain(): return jnp.dot(left_side, right_side, preferred_element_type=F32)]
    psum x1 -> x0, blocking collectives: 39.2 us -> none  [shards(): norm_grads = lax.psum(jnp.stack([gain_grad, bias_grad]), ('dp', 'seq'))]
    dot_general x5 -> x0, matrix products: 34.6 us -> none  [dot_inner(): lax.dot_general(left_side, right_side, (((0,), (0,)), ((), ())), preferre...]
    pallas_call x2 -> x1, Pallas kernels: 56.9 us -> 36.1 us  [conv_call(): pl.pallas_call(body, grid=(steps,), out_shape=outs, in_specs=[pl.BlockSpe...]
    ppermute x8 -> x4, starting transfers between devices: 29.8 us -> 10.9 us  [shift(): return lax.ppermute(array, 'seq', pairs)]
    unnamed x1 -> x0, blocking collectives: 18.3 us -> none
    ppermute x8 -> x4, waiting for transfers between devices: 13.2 us -> 0.01 us  [shift(): return lax.ppermute(array, 'seq', pairs)]
  transfers between devices with their start and end apart: 8 -> 4, of which waited for: 2 -> 0; matrix products, arithmetic and copies ran while one was open for 13% -> 6% of each run, Pallas kernels for 0% -> 0%
where the time goes in v2:
time: 544 us; the launch traced here: 534 us
  Pallas kernels  418 us (77%)
  matrix products  35 us (6%)
  other arithmetic  31.9 us (6%)
  local copies, waits for them, and re-layouts  26.6 us (5%)
  starting transfers between devices  10.9 us (2%)
  blocking collectives  9.79 us (2%)
    pallas_call x1, Pallas kernels, reduce_gradients(): pl.pallas_call(functools.partial(grad_kernel, acts, rights), out_shape=[j...  195 us
    pallas_call x1, Pallas kernels, gather_forward(): pl.pallas_call(functools.partial(forward_kernel, width), out_shape=full +...  187 us
    pallas_call x1, Pallas kernels, conv_call(): pl.pallas_call(body, grid=(steps,), out_shape=outs, in_specs=[pl.BlockSpe...  36.1 us
    dot_general x4, matrix products, dot_outer(): lax.dot_general(left_side, right_side, (((1,), (1,)), ((), ())), preferre...  22.2 us
    ppermute x4, starting transfers between devices, shift(): return lax.ppermute(array, 'seq', pairs)  10.9 us
  transfers between devices with their start and end apart: 4, of which 0 were waited for; matrix products, arithmetic and copies ran while one was open for 6% of the time, Pallas kernels for 0%

profile of v2, /device:TPU:0, one launch (start us, length us, event | category | flops | bytes accessed | tf_op | source)
XLA Modules:
  0.0 534.1 jit_solution(18356438526122303461)
XLA Ops:
  0.7 0.7 broadcast_compare_fusion
  1.4 1.0 reduce_window_sum.11
  2.4 0.7 sub.32
  3.8 0.6 reshape.257.mask_ref
  4.4 1.1 constant_dynamic-slice_fusion
  5.9 5.7 %fusion.19 = (f32[96,32,64]{2,1,0:T(8,128)S(1)}, f32[96,32,64]{2,1,0:T(8,128)S(1)}) fusion(f32[96,64]{1,0:T(8,128)S(1)} %bitcast.100, f32[32]{0:T(128)S(1)} %iota_convert_fusion, f32[96,64]{1,0:T(8,128)S(1)} %bitcast.103), kind=kLoop, calls=%fused_computation.32 | loop fusion | flops 786432 | bytes 1622144 | tf_op jit(solution)/shard_map/mul | solution.py:1026
  11.7 3.0 fusion.29
  14.7 2.8 convolution_convert_fusion.2
  17.5 0.6 copy.67
  18.1 0.8 copy.68.refs_7_
  18.8 0.6 fusion.36.refs_3_
  19.4 187.0 %shard_map.238 = (bf16[8,16,128]{2,1,0:T(8,128)(2,1)}, bf16[8,96,1536]{2,1,0:T(8,128)(2,1)}, bf16[8,96,3072]{2,1,0:T(8,128)(2,1)}, bf16[8,384,768]{2,1,0:T(8,128...) custom-call(f32[28]{0:T(128)} %reshape.257.mask_ref, ...), custom_call_target="tpu_custom_call" | custom-call | flops 20000000000 | bytes 200000000 | tf_op jit(solution)/shard_map/pallas_call | solution.py:699
  206.5 10.5 %convolution_convert_fusion.1 = bf16[512,1536]{1,0:T(8,128)(2,1)} fusion(bf16[512,3072]{1,0:T(8,128)(2,1)} %get-tuple-element.43.refs_6_, bf16[1536,3072]{1,0:T(8,128)(2,1)} %bitcast.124), kind=kOutput, calls=%fused_computation.15 | convolution fusion | flops 4832624640 | bytes 14155776 | tf_op jit(solution)/shard_map/dot_general | solution.py:1067
  217.0 1.3 collective-permute-start
  218.3 2.1 slice.106
  220.3 1.3 collective-permute-start.1
  221.7 6.3 %convolution_convert_fusion = bf16[512,1536]{1,0:T(8,128)(2,1)} fusion(bf16[512,3072]{1,0:T(8,128)(2,1)S(1)} %copy-done.28, bf16[1536,3072]{1,0:T(8,128)(2,1)S(1)} %bitcast.123), kind=kOutput, calls=%fused_computation.14 | convolution fusion | flops 4832624640 | bytes 14155776 | tf_op jit(solution)/shard_map/dot_general | solution.py:1067
  228.0 4.3 collective-permute-start.3
  232.3 2.1 slice.107
  234.4 4.0 collective-permute-start.2
  238.6 0.7 convert_reduce_fusion.2
  239.7 3.8 fusion.42
  243.6 4.8 copy.69
  248.5 2.7 copy.70
  251.2 1.6 copy.71
  252.8 1.2 copy.72
  254.0 6.8 %fusion.16 = bf16[512,768]{1,0:T(8,128)(2,1)} fusion(bf16[512,768]{1,0:T(8,128)(2,1)S(1)} %bitcast.85, bf16[512,3072]{1,0:T(8,128)(2,1)} %get-tuple-element.37, bf16[3072,768]{1,0:T(8,128)(2,1)} %bitcast.125), kind=kOutput, calls=%fused_computation.29 | convolution fusion | flops 2417098752 | bytes 9437184 | tf_op jit(solution)/shard_map/dot_general | solution.py:1059
  260.8 36.1 %shard_map.239 = (bf16[2,256,1536]{2,1,0:T(8,128)(2,1)}, bf16[8,4,2,48,512]{4,3,2,1,0:T(8,128)(2,1)}) custom-call(f32[28]{0:T(128)} %reshape.257.mask_ref, bf16[256,256]{1,0:T(8,128)(2,1)} %constant.63.clone.refs_0_.wave_ref, bf16[8,4,2,48,512]{4,3,2,1,0:T(8,128)(2,1)} %bitcast.129, bf16[2,1024,1536]{2,1,0:T(8,128)(2,1)} %get-tuple-element.42.refs_0_, ...), custom_call_target="tpu_custom_call" | custom-call | flops 10000000000 | bytes 30000000 | tf_op jit(solution)/shard_map/pallas_call | solution.py:199
  296.9 3.5 fusion.2.refs_9_
  300.4 1.6 fusion.13
  302.1 0.9 fusion.15
  303.2 1.5 add_convert_fusion
  304.9 0.6 pad.14.refs_11_
  305.5 195.1 %shard_map.240 = (bf16[384,768]{1,0:T(8,128)(2,1)}, bf16[192,3072]{1,0:T(8,128)(2,1)}, bf16[192,3072]{1,0:T(8,128)(2,1)}, bf16[96,3072]{1,0:T(8,128)(2,1)}, bf16...) custom-call(bf16[8,384,512]{2,1,0:T(8,128)(2,1)} %bitcast.86, bf16[8,192,512]{2,1,0:T(8,128)(2,1)} %bitcast.90, ...), custom_call_target="tpu_custom_call" | custom-call | flops 16000000000 | bytes 100000000 | tf_op jit(solution)/shard_map/pallas_call | solution.py:993
  500.6 1.3 slice_bitcast_fusion.3
  501.9 2.2 convert_element_type.111
  504.1 0.9 convert_element_type.112
  505.0 1.7 convert_element_type.113
  506.6 1.7 convert_element_type.114
  508.3 1.1 convert_element_type.115
  509.6 0.9 pad_maximum_fusion.1
  510.5 3.6 copy.74
  514.1 3.3 fusion.30
  517.4 4.0 fusion.24
  521.5 9.8 %all_gather.3 = f32[3,2,192,64]{3,2,1,0:T(8,128)S(1)} all-gather(f32[3,2,48,64]{3,2,1,0:T(8,128)S(1)} %pad_maximum_fusion.4), channel_id=1, replica_groups=mesh['dp'=4,'seq'=8] {'dp'}, dimensions={2}, use_global_device_ids=true | all-gather | bytes 368640 | tf_op jit(solution)/shard_map/all_gather | solution.py:1207
  531.4 0.8 copy.75
  532.1 0.8 copy.76
  532.9 0.8 copy.77
  (111 shorter events, 2.5 us)
Async XLA Ops:
  0.6 5.0 copy-start
  5.5 6.1 %copy-start.14 = (f32[2,48,64]{2,1,0:T(8,128)}, f32[2,48,64]{2,1,0:T(8,128)S(1)}, u32[]{:S(2)}) copy-start(f32[2,48,64]{2,1,0:T(8,128)S(1)} %copy.66) | copy-start | bytes 73732
  5.6 6.0 %copy-start.17 = (f32[2,48,64]{2,1,0:T(8,128)}, f32[2,48,64]{2,1,0:T(8,128)S(1)}, u32[]{:S(2)}) copy-start(f32[2,48,64]{2,1,0:T(8,128)S(1)} %copy.80) | copy-start | bytes 73732
  5.8 5.8 %copy-start.19 = (f32[2,48,64]{2,1,0:T(8,128)}, f32[2,48,64]{2,1,0:T(8,128)S(1)}, u32[]{:S(2)}) copy-start(f32[2,48,64]{2,1,0:T(8,128)S(1)} %copy.79) | copy-start | bytes 73732
  11.6 3.0 copy-start.2
  11.6 3.0 copy-start.4
  14.6 4.2 copy-start.23
  14.6 4.2 copy-start.24
  206.5 15.2 %slice-start = ((s8[9437184]{0:T(1024)(128)(4,1)}), s8[4194304]{0:T(1024)(128)(4,1)S(1)}, s32[]{:S(2)}) async-start(s8[9437184]{0:T(1024)(128)(4,1)} %bitcast.121), calls=%async_computation | async-start | bytes 8388608
  206.5 15.2 %slice-start.1 = ((s8[9437184]{0:T(1024)(128)(4,1)}), s8[4194304]{0:T(1024)(128)(4,1)S(1)}, s32[]{:S(2)}) async-start(s8[9437184]{0:T(1024)(128)(4,1)} %bitcast.121), calls=%async_computation.1 | async-start | bytes 8388608
  206.5 15.2 %slice-start.2 = ((s8[9437184]{0:T(1024)(128)(4,1)}), s8[1048576]{0:T(1024)(128)(4,1)S(1)}, s32[]{:S(2)}) async-start(s8[9437184]{0:T(1024)(128)(4,1)} %bitcast.121), calls=%async_computation.2 | async-start | bytes 2097152
  206.5 15.2 %copy-start.28 = (bf16[512,3072]{1,0:T(8,128)(2,1)S(1)}, bf16[512,3072]{1,0:T(8,128)(2,1)}, u32[]{:S(2)}) copy-start(bf16[512,3072]{1,0:T(8,128)(2,1)} %get-tuple-element.45.refs_7_) | copy-start | bytes 9437188
  217.0 43.8 %collective-permute-start = (bf16[2,256,1536]{2,1,0:T(8,128)(2,1)}, bf16[2,256,1536]{2,1,0:T(8,128)(2,1)}, u32[]{:S(2)}, u32[]{:S(2)}) collective-permute-start(bf16[2,256,1536]{2,1,0:T(8,128)(2,1)} %bitcast.16.refs_1_), channel_id=1, source_target_pairs={{1,0},{2,1},{3,2},{4,3},{5,4},{6,5},{7,6},{9,8},{10,9},{11,10},{12... | collective-permute-start | bytes 4718600 | tf_op jit(solution)/shard_map/ppermute | solution.py:1079
  220.3 40.4 %collective-permute-start.1 = (bf16[2,128,1536]{2,1,0:T(8,128)(2,1)}, bf16[2,128,1536]{2,1,0:T(8,128)(2,1)}, u32[]{:S(2)}, u32[]{:S(2)}) collective-permute-start(bf16[2,128,1536]{2,1,0:T(8,128)(2,1)} %slice.106), channel_id=1, source_target_pairs={{2,0},{3,1},{4,2},{5,3},{6,4},{7,5},{10,8},{11,9},{12,10},{13,11},... | collective-permute-start | bytes 2359304 | tf_op jit(solution)/shard_map/ppermute | solution.py:1079
  221.6 18.1 %slice-start.3 = ((s8[4718592]{0:T(1024)(128)(4,1)}), s8[4194304]{0:T(1024)(128)(4,1)S(1)}, s32[]{:S(2)}) async-start(s8[4718592]{0:T(1024)(128)(4,1)} %bitcast.126), calls=%async_computation.3 | async-start | bytes 8388608
  221.7 18.0 %slice-start.4 = ((s8[4718592]{0:T(1024)(128)(4,1)}), s8[524288]{0:T(1024)(128)(4,1)S(1)}, s32[]{:S(2)}) async-start(s8[4718592]{0:T(1024)(128)(4,1)} %bitcast.126), calls=%async_computation.4 | async-start | bytes 1048576
  221.7 18.0 %copy-start.27 = (bf16[512,3072]{1,0:T(8,128)(2,1)S(1)}, bf16[512,3072]{1,0:T(8,128)(2,1)}, u32[]{:S(2)}) copy-start(bf16[512,3072]{1,0:T(8,128)(2,1)} %get-tuple-element.39.refs_8_) | copy-start | bytes 9437188
  228.0 10.4 %copy-start.6 = (bf16[2,256,768]{2,1,0:T(8,128)(2,1)S(1)}, bf16[2,256,768]{2,1,0:T(8,128)(2,1)}, u32[]{:S(2)}) copy-start(bf16[2,256,768]{2,1,0:T(8,128)(2,1)} %param.15) | copy-start | bytes 2359300
  228.0 32.8 %collective-permute-start.3 = (bf16[2,256,1536]{2,1,0:T(8,128)(2,1)}, bf16[2,256,1536]{2,1,0:T(8,128)(2,1)}, u32[]{:S(2)}, u32[]{:S(2)}) collective-permute-start(bf16[2,256,1536]{2,1,0:T(8,128)(2,1)} %bitcast.18.refs_6_), channel_id=1, source_target_pairs={{0,1},{1,2},{2,3},{3,4},{4,5},{5,6},{6,7},{8,9},{9,10},{10,11},{11... | collective-permute-start | bytes 4718600 | tf_op jit(solution)/shard_map/ppermute | solution.py:1079
  234.4 26.4 %collective-permute-start.2 = (bf16[2,128,1536]{2,1,0:T(8,128)(2,1)}, bf16[2,128,1536]{2,1,0:T(8,128)(2,1)}, u32[]{:S(2)}, u32[]{:S(2)}) collective-permute-start(bf16[2,128,1536]{2,1,0:T(8,128)(2,1)} %slice.107), channel_id=1, source_target_pairs={{0,2},{1,3},{2,4},{3,5},{4,6},{5,7},{8,10},{9,11},{10,12},{11,13},... | collective-permute-start | bytes 2359304 | tf_op jit(solution)/shard_map/ppermute | solution.py:1079
  248.5 2.8 copy-start.8
  251.2 1.6 copy-start.12
  260.8 36.1 %copy-start.7 = (f32[512,1536]{1,0:T(8,128)S(1)}, f32[512,1536]{1,0:T(8,128)}, u32[]{:S(2)}) copy-start(f32[512,1536]{1,0:T(8,128)} %get-tuple-element.48) | copy-start | bytes 9437188
  296.8 3.6 copy-start.25
  296.9 3.6 copy-start.26
  300.4 1.6 copy-start.9
  302.0 1.1 copy-start.13
  500.6 3.5 copy-start.21
  500.6 4.4 copy-start.11
  505.0 1.7 copy-start.10
  506.6 1.7 copy-start.16
  508.3 1.1 copy-start.22
  509.6 4.5 copy-start.3
  509.6 4.5 copy-start.5
  514.1 3.3 copy-start.15
  517.4 4.0 copy-start.18
  517.4 4.0 copy-start.20
  521.5 12.2 %copy-start.1 = (f32[2,192,64]{1,2,0:T(8,128)S(1)}, f32[2,192,64]{1,2,0:T(8,128)}, u32[]{:S(2)}) copy-start(f32[2,192,64]{1,2,0:T(8,128)} %param.25) | copy-start | bytes 294916

commit v3 on v2

--- a/solution.py
+++ b/solution.py
@@ -243,7 +243,8 @@
 GEOM = {"filter": "col", "kern": "row", "value": "col", "fore": "col", "back": "col", "out": "row", "norm": None}
 
 
-FETCH = ("norm", "filter", "value", "out", "kern", "fore", "back")
+FETCH = ("norm", "filter", "kern", "fore", "back", "value", "out")
+SMALL = ("norm", "kern")
 GELU_C = 0.7978845608028654
 GELU_D = 0.044715
 
@@ -255,10 +256,9 @@
     return x * half, half + 0.5 * x * (1.0 - t * t) * (GELU_C * (1.0 + 3.0 * GELU_D * sq))
 
 
-def slab_forward(mask_ref, wave_ref, kr_ref, spec_ref, x_ref, y_ref, fb_ref, outs, chunk, slab):
-    tile = 128
-    rows = pl.ds(pl.multiple_of(slab * tile, tile), tile)
-    lanes = pl.ds(pl.multiple_of(chunk * 384 + slab * tile, tile), tile)
+def slab_forward(mask_ref, wave_ref, kr_ref, spec_ref, x_ref, y_ref, fb_ref, outs, chunk):
+    rows = slice(None)
+    lanes = slice(chunk * 384, chunk * 384 + 384)
     fwd = wave_ref[:, BLK:]
     for side in range(2):
         spec_ref[side, 0] = dot(fwd, kr_ref[side, rows, :BLK], 1, 1)
@@ -268,38 +268,40 @@
         for b in range(8):
             x_ref[b] = dot(fwd, fb_ref[micro, b * BLK:(b + 1) * BLK, lanes], 1, 0)
 
-        @pl.loop(0, BLK // 8)
+        @pl.loop(0, BLK // 16)
         def _(r):
-            re = pl.ds(pl.multiple_of(r * 8, 8), 8)
-            im = pl.ds(pl.multiple_of(r * 8 + BLK, 8), 8)
-            xr = [x_ref[b, re, :] for b in range(8)]
-            xi = [x_ref[b, im, :] for b in range(8)]
-            for side in range(2):
-                cr = [spec_ref[side, d, re, :] for d in range(4)]
-                ci = [spec_ref[side, d, im, :] for d in range(4)]
-                for own in range(2):
-                    yr = yi = None
-                    for d in range(4):
-                        at = own + 3 + (d if side else -d)
-                        pr = cr[d] * xr[at]
-                        pi = cr[d] * xi[at]
-                        qr = ci[d] * xi[at]
-                        qi = ci[d] * xr[at]
-                        if side:
-                            tr, ti = pr + qr, pi - qi
-                        else:
-                            tr, ti = pr - qr, pi + qi
-                        if d:
-                            m = mask_ref[(micro * 2 + own) * 7 + 3 + (d if side else -d)]
-                            tr, ti = tr * m, ti * m
-                        yr = tr if yr is None else yr + tr
-                        yi = ti if yi is None else yi + ti
-                    y_ref[side, own, re, :] = yr
-                    y_ref[side, own, im, :] = yi
+            re = pl.ds(pl.multiple_of(r * 16, 16), 16)
+            im = pl.ds(pl.multiple_of(r * 16 + BLK, 16), 16)
+            for lane in range(3):
+                ln = slice(lane * 128, lane * 128 + 128)
+                xr = [x_ref[b, re, ln] for b in range(8)]
+                xi = [x_ref[b, im, ln] for b in range(8)]
+                for side in range(2):
+                    cr = [spec_ref[side, d, re, ln] for d in range(4)]
+                    ci = [spec_ref[side, d, im, ln] for d in range(4)]
+                    for own in range(2):
+                        yr = yi = None
+                        for d in range(4):
+                            at = own + 3 + (d if side else -d)
+                            pr = cr[d] * xr[at]
+                            pi = cr[d] * xi[at]
+                            qr = ci[d] * xi[at]
+                            qi = ci[d] * xr[at]
+                            if side:
+                                tr, ti = pr + qr, pi - qi
+                            else:
+                                tr, ti = pr - qr, pi + qi
+                            if d:
+                                m = mask_ref[(micro * 2 + own) * 7 + 3 + (d if side else -d)]
+                                tr, ti = tr * m, ti * m
+                            yr = tr if yr is None else yr + tr
+                            yi = ti if yi is None else yi + ti
+                        y_ref[side, own, re, ln] = yr.astype(jnp.bfloat16)
+                        y_ref[side, own, im, ln] = yi.astype(jnp.bfloat16)
 
         for own in range(2):
             for side in range(2):
-                y = dot(fwd, y_ref[side, own].astype(jnp.bfloat16), 0, 0)
+                y = dot(fwd, y_ref[side, own], 0, 0)
                 at = micro * 256 + own * BLK
                 outs[side][at:at + BLK, lanes] = (y * (1.0 / BLK)).astype(jnp.bfloat16)
 
@@ -313,9 +315,9 @@
     src = take(n)
     out = take(n)
     pre_out, fb_out, fore_out, back_out, hid_out, gpf_out, gpb_out, gpv_out, nrm_out = take(9)
-    stage = take(n)
-    wave_ref, tok, cot, nv, gb, nl, wa, wb, pf, pv, gh, fb, low_f, low_b, kv, kr, spec, xs_, ys_, ring = take(20)
-    isem, lsem, zs, zr, xs, xr, ys, yr, fxs, fxr, fys, fyr, ss, sr, ss0, sr0, hs, hr, misc, rsem = refs
+    stage = dict(zip(SMALL, take(len(SMALL))))
+    wave_ref, tok, cot, nv, gb, nl, wa, wb, pf, pv, pk, fb, low_f, low_b, kv, kr, spec, xs_, ys_, ring = take(20)
+    isem, lsem, fsem, zs, zr, xs, xr, ys, yr, fxs, fxr, fys, fyr, ss, sr, ss0, sr0, hs, hr, misc, rsem = refs
     dp, s, z, c = place(4)
     core = (dp, s + 1 - 2 * c)
     odd = (dp, lax.rem(s + 7 + 2 * c, 8))
@@ -332,11 +334,11 @@
     for i, (a, b) in enumerate([(wave_in, wave_ref), (tok_in, tok), (cot_in, cot)]):
         first[i] = pltpu.make_async_copy(a, b, misc.at[i])
         first[i].start()
-    lins = []
-    for a in range(n):
-        li = pltpu.make_async_copy(src[a], stage[a], isem.at[a])
-        li.start()
-        lins.append(li)
+    lins = {}
+    for m in SMALL:
+        a = names.index(m)
+        lins[a] = pltpu.make_async_copy(src[a], stage[m], isem.at[a])
+        lins[a].start()
     halo_rows = 3 * BLK
 
     @pl.loop(0, halo_rows // 16)
@@ -357,10 +359,19 @@
         return pltpu.make_async_remote_copy(src_ref=a_ref, dst_ref=b_ref, send_sem=s1, recv_sem=s2, device_id=dev, device_id_type=MESH)
 
     g = [GEOM[m] for m in names]
+    def place_of(m, shard):
+        R = out[names.index(m)].shape[1]
+        if m == "filter":
+            return wa.at[pl.ds(pl.multiple_of(768 + shard * R, 16), R), pl.ds(0, 1536)]
+        if m == "out":
+            return wa.at[pl.ds(pl.multiple_of(768 + lax.rem(shard, 2) * R, 16), R), pl.ds(pl.multiple_of(lax.div(shard, 2) * 768, 128), 768)]
+        return (wb if m == "back" else wa).at[pl.ds(pl.multiple_of(shard * R, 16), R)]
+
     locs, own_sib, zsend = [], {}, {}
     for a in range(n):
         where = cut(out[a].at[s], g[a], q) if names[a] == "kern" else out[a].at[s]
-        locs.append(pltpu.make_async_copy(stage[a], where, lsem.at[a]))
+        held = stage[names[a]] if names[a] in SMALL else place_of(names[a], s)
+        locs.append(pltpu.make_async_copy(held, where, lsem.at[a]))
 
     def near(way, j):
         return lax.rem(s + (8 - 2 * j if way == 0 else 2 * j), 8)
@@ -433,11 +444,11 @@
     zgo(1)
     sibgo(0)
     sibgo(1)
-    for a in range(n):
+    for a in lins:
         lins[a].wait()
         locs[a].start()
 
-    def st1(u):
+    def st0(u):
         a, way, j = u
         if j == 0:
             locs[a].wait()
@@ -446,6 +457,8 @@
             zin[u].wait_recv()
             if j < 3:
                 pl.when(onward(way))(zsend[a, way, j].start)
+
+    def st1(u):
         if u in xc:
             xc[u].start()
             yc[u].start()
@@ -463,13 +476,33 @@
             fy[u].wait_recv()
         sb[u].start()
 
-    state = {"t": 0}
-    total = len(units) + L3
+    loaded = {}
+    for u in units:
+        a = u[0]
+        if names[a] in ("filter", "value", "out", "fore", "back"):
+            shard = near(u[1], u[2])
+            other = shard + 1 - 2 * c
+            for w, sh in ((0, shard), (1, other)):
+                loaded[u, w] = pltpu.make_async_copy(out[a].at[sh], place_of(names[a], sh), fsem.at[a, slot(u), w])
+    for a in range(n):
+        if names[a] in ("filter", "value", "out", "fore", "back"):
+            for w, sh in ((0, s), (1, s + 1 - 2 * c)):
+                origin = src[a] if w == 0 else out[a].at[sh]
+                loaded[(a, 0, 0), w] = pltpu.make_async_copy(origin, place_of(names[a], sh), fsem.at[a, 6, w])
+
+    def st4(u):
+        sb[u].wait_recv()
+        for w in (0, 1):
+            if (u, w) in loaded:
+                assert names[u[0]] not in ("value", "out") or state["free"]
+                loaded[u, w].start()
+
+    state = {"t": 0, "free": False}
 
     def comm():
         t = state["t"]
         state["t"] += 1
-        for lag, stage_of in ((0, st1), (L2, st2), (L3, st3)):
+        for lag, stage_of in ((0, st0), (L1, st1), (L2, st2), (L3, st3), (L4, st4)):
             if 0 <= t - lag < len(units):
                 u = units[t - lag]
                 when(here(u), functools.partial(stage_of, u))
@@ -479,15 +512,23 @@
 
     def complete(name):
         a = names.index(name)
-        while state["t"] <= last_unit[a] + L3:
+        while state["t"] <= last_unit[a] + L4:
             comm()
-        if a not in loc_done:
+        if a not in loc_done and name in SMALL:
             locs[a].wait()
         if a in own_sib:
             own_sib[a].wait_recv()
-        for u in units:
-            if u[0] == a:
-                when(here(u), sb[u].wait_recv)
+        own = (a, 0, 0)
+        for w in (0, 1):
+            if (own, w) in loaded:
+                loaded[own, w].start()
+        for u in [own] + [u for u in units if u[0] == a]:
+            for w in (0, 1):
+                if (u, w) in loaded:
+                    when(here(u), loaded[u, w].wait)
+        if name not in SMALL:
+            locs[a].start()
+            locs[a].wait()
         return a
 
     def fetch(pairs, sem0):
@@ -522,12 +563,10 @@
     nout.start()
 
     a = complete("filter")
-    R = out[a].shape[1]
-    fetch([(out[a].at[j], wa.at[pl.ds(768 + j * R, R), pl.ds(0, 1536)]) for j in range(8)], 5)
-
-    @pl.loop(0, 4)
+
+    @pl.loop(0, 3)
     def _(j):
-        cols = pl.ds(pl.multiple_of(j * 384, 128), 384)
+        cols = pl.ds(pl.multiple_of(j * 512, 128), 512)
         t = jnp.dot(nl[...], wa[768:1536, cols], preferred_element_type=jnp.float32)
         pf[:, cols] = t
         act = gelu_parts(t)[0].astype(jnp.bfloat16)
@@ -562,25 +601,6 @@
 
     halo_go(0)
 
-    a = complete("value")
-    R = out[a].shape[1]
-    fetch([(out[a].at[j], wa.at[pl.ds(j * R, R)]) for j in range(8)], 5)
-    for half in range(2):
-        @pl.loop(half * 4, half * 4 + 4)
-        def _(j):
-            cols = pl.ds(pl.multiple_of(j * 384, 128), 384)
-            pv[:, cols] = jnp.dot(nl[...], wa[:768, cols], preferred_element_type=jnp.float32)
-
-        comm()
-
-    halo_go(1)
-    a = complete("out")
-    halo_go(2)
-    fetch([(out[a].at[j], wb.at[pl.ds((j % 2) * 384, 384), pl.ds((j // 2) * 768, 768)]) for j in range(8)], 5)
-    for j in range(4):
-        gh[:, j * 768:(j + 1) * 768] = dot(cot[...], wb[:768, j * 768:(j + 1) * 768], 1, 1)
-        comm()
-
 
     def conv_chunk(chunk):
         halo_here(chunk)
@@ -592,23 +612,24 @@
                     at = (j * 4 + p) * 48
                     kr[side, at:at + 48] = kv[j, (p * 2 + side) * 48:(p * 2 + side + 1) * 48]
 
-        @pl.loop(0, 3)
-        def _(slab):
-            slab_forward(mask_ref, wave_ref, kr, spec, xs_, ys_, fb, (low_f, low_b), chunk, slab)
+        slab_forward(mask_ref, wave_ref, kr, spec, xs_, ys_, fb, (low_f, low_b), chunk)
 
     complete("kern")
-    halo_go(3)
+    halo_go(1)
     comm()
-    comm()
+    halo_go(2)
     conv_chunk(0)
     comm()
     comm()
+    halo_go(3)
     conv_chunk(1)
-    a = complete("fore")
+    comm()
+    comm()
     conv_chunk(2)
     comm()
     comm()
     conv_chunk(3)
+    complete("fore")
     fb_cp = pltpu.make_async_copy(fb, fb_out, misc.at[14])
     fb_cp.start()
     low_cp = [pltpu.make_async_copy(low_f, fore_out, misc.at[15]), pltpu.make_async_copy(low_b, back_out, misc.at[16])]
@@ -617,17 +638,32 @@
 
     R = out[a].shape[1]
     pre_cp.wait()
-    fetch([(out[a].at[j], wa.at[pl.ds(j * R, R)]) for j in range(8)], 5)
     for half in range(2):
-        @pl.loop(half * 4, half * 4 + 4)
+        @pl.loop(half * 3, half * 3 + 3)
         def _(j):
-            cols = pl.ds(pl.multiple_of(j * 384, 128), 384)
+            cols = pl.ds(pl.multiple_of(j * 512, 128), 512)
             pf[:, cols] = jnp.dot(low_f[...], wa[:, cols], preferred_element_type=jnp.float32)
 
         comm()
-    a = complete("back")
-    R = out[a].shape[1]
-    fetch([(out[a].at[j], wb.at[pl.ds(j * R, R)]) for j in range(8)], 5)
+    state["free"] = True
+    complete("back")
+    for half in range(2):
+        @pl.loop(half * 3, half * 3 + 3)
+        def _(j):
+            cols = pl.ds(pl.multiple_of(j * 512, 128), 512)
+            pk[:, cols] = jnp.dot(low_b[...], wb[:, cols], preferred_element_type=jnp.float32)
+
+        comm()
+    a = complete("value")
+    for half in range(2):
+        @pl.loop(half * 3, half * 3 + 3)
+        def _(j):
+            cols = pl.ds(pl.multiple_of(j * 512, 128), 512)
+            pv[:, cols] = jnp.dot(nl[...], wa[:768, cols], preferred_element_type=jnp.float32)
+
+        comm()
+
+    complete("out")
     dests = (hid_out, gpf_out, gpb_out, gpv_out)
 
     def ring_cp(j, w):
@@ -644,10 +680,12 @@
             for w in range(4):
                 ring_cp(j - 2, w).wait()
 
-        pb = jnp.dot(low_b[...], wb[:, cols], preferred_element_type=jnp.float32)
+        out_rows = pl.ds(pl.multiple_of(768 + lax.rem(j, 3) * 256, 16), 256)
+        out_cols = pl.ds(pl.multiple_of(lax.div(j, 3) * 768, 128), 768)
+        h = dot(cot[...], wa[out_rows, out_cols], 1, 1)
+        pb = pk[:, cols]
         p = pf[:, cols]
         va, dva = gelu_parts(pv[:, cols])
-        h = gh[:, cols]
         hv = h * va
         ring[slot, 0] = (p * pb * va).astype(jnp.bfloat16)
         ring[slot, 1] = (hv * pb).astype(jnp.bfloat16)
@@ -701,12 +739,12 @@
         out_shape=full + extra,
         in_specs=[pl.BlockSpec(memory_space=pltpu.SMEM)] + [any_] * (3 + n),
         out_specs=[any_] * (n + len(extra)),
-        scratch_shapes=[V(shards[m].shape) for m in FETCH]
+        scratch_shapes=[V(shards[m].shape) for m in SMALL]
         + [V(wave.shape), V((rows, width)), V((rows, width)), V((8, 16, 128)), V((16, width), f32), V((rows, width))]
         + [V((FH, FFN)), V((FH, FFN)), V((rows, FFN), f32), V((rows, FFN), f32), V((rows, FFN), f32)]
         + [V((2, 1024, FH)), V((rows, FH)), V((rows, FH)), V((2, 384, 512)), V((2, 384, 512))]
-        + [V((2, 4, 256, 128), f32), V((8, 256, 128), f32), V((2, 2, 256, 128), f32), V((2, 4, rows, 256))]
-        + [D((n,)), D((n,)), D((n, 6)), D((n, 6))]
+        + [V((2, 4, 256, 384), f32), V((8, 256, 384), f32), V((2, 2, 256, 384)), V((2, 4, rows, 256))]
+        + [D((n,)), D((n,)), D((n, 7, 2)), D((n, 6)), D((n, 6))]
         + [D((n, 7))] * 10
         + [D((n,)), D((n,)), D((4, 4)), D((4, 4)), D((17,)), D((2, 4))],
         compiler_params=pltpu.CompilerParams(collective_id=0, has_side_effects=True, vmem_limit_bytes=int(63.5 * 2**20)),
@@ -715,9 +753,10 @@
     return dict(zip(FETCH, outs[:n])), outs[n:]
 
 
-L2, L3 = 3, 6
-
-
+L1, L2, L3, L4 = 0, 2, 5, 7
+
+
+FIRST_Z = ()
 ORDER = ("out", "fore", "back", "value", "kern", "filter")
 DEPTH = 3
 
@@ -748,7 +787,7 @@
     bx = dict(zip(ORDER, take(len(ORDER))))
     by = dict(zip(ORDER, take(len(ORDER))))
     bc = dict(zip(ORDER, take(len(ORDER))))
-    snd, stg, nbuf = take(3)
+    snd, snd2, stg, nbuf = take(4)
     isem, ksem, as_, ar, xs, xr, ys, yr, cs, cr, gxs, gxr, gys, gyr, hxs, hxr, hys, hyr, osem, ns, nr = refs
     dp, s, z, c = place(4)
     core = (dp, s + 1 - 2 * c)
@@ -782,9 +821,14 @@
         return pltpu.make_async_remote_copy(src_ref=a_ref, dst_ref=b_ref, send_sem=s1, recv_sem=s2, device_id=dev, device_id_type=MESH)
 
     g = GEOM
-    units = [(m, k) for m in ORDER for k in (1, 2, 3, 0)]
+    units = [(m, k) for m in FIRST_Z for k in (1, 2, 3)]
+    for m in ORDER:
+        if m == ORDER[-2]:
+            units += [(w, 0) for w in FIRST_Z]
+        if m not in FIRST_Z:
+            units += [(m, k) for k in (1, 2, 3, 0)]
     at = {m: j for j, m in enumerate(ORDER)}
-    A, X, Y, C, waited = {}, {}, {}, {}, set()
+    A, X, Y, C, waited, left_behind = {}, {}, {}, {}, set(), set()
 
     def ready(kind, m):
         if (kind, m) not in waited:
@@ -815,18 +859,20 @@
         else:
             ready("a", m)
             ready("r", m)
-            back = [u for u in range(i) if units[u][0] != "kern"]
+            back = [u for u in range(i) if units[u][0] != "kern" and (units[u][0] in FIRST_Z) == (m in FIRST_Z)]
             if len(back) >= DEPTH:
                 A[back[-DEPTH]].wait_send()
+                left_behind.discard(back[-DEPTH])
             slot = len(back) % DEPTH
             R, cols = P[m].shape[-2:]
-            buf = snd.at[slot, pl.ds(0, R), pl.ds(0, cols)]
+            buf = (snd2 if m in FIRST_Z else snd).at[slot, pl.ds(0, R), pl.ds(0, cols)]
 
             def put(cs_, t):
                 buf[:, cs_] = t.astype(jnp.bfloat16)
 
             product(m, so(k, True), put)
             A[i] = rc(buf, P[m].at[k], as_.at[j, k], ar.at[j, k], core)
+        left_behind.add(i)
         A[i].start()
 
     def stB(i):
@@ -841,6 +887,14 @@
                 p[:, cs_] = (p[:, cs_].astype(jnp.float32) + t).astype(jnp.bfloat16)
 
             product(m, so(k, False), put)
+        if m in FIRST_Z:
+            if k:
+                C[i] = rc(p, bc[m].at[k - 1], cs.at[j, k - 1], cr.at[j, k - 1], zdev(k))
+                C[i].start()
+                return
+            for w in (1, 2, 3):
+                C[units.index((m, w))].wait_recv()
+            add_into(p, [bc[m].at[w] for w in range(3)])
         X[i, 1] = rc(cut(p, g[m], qd, 0), bx[m].at[k, 1], xs.at[j, k, 1], xr.at[j, k, 1], xn)
         X[i, 0] = rc(cut(p, g[m], qx, 0), bx[m].at[k, 0], xs.at[j, k, 0], xr.at[j, k, 0], xn)
         Y[i, 1] = rc(cut(p, g[m], qd, 1), by[m].at[k, 1], ys.at[j, k, 1], yr.at[j, k, 1], yn)
@@ -851,6 +905,8 @@
 
     def stC(i):
         m, k = units[i]
+        if m in FIRST_Z and k:
+            return
         j = at[m]
         p = P[m].at[k]
         X[i, 1].wait_recv()
@@ -864,6 +920,8 @@
 
     def stD(i):
         m, k = units[i]
+        if m in FIRST_Z and k:
+            return
         j = at[m]
         p = P[m].at[k]
         X[i, 0].wait_recv()
@@ -880,10 +938,11 @@
 
     def stE(m):
         j = at[m]
-        for k in (1, 2, 3):
-            C[units.index((m, k))].wait_recv()
         p = cut(P[m].at[0], g[m], q)
-        add_into(p, [bc[m].at[w] for w in range(3)])
+        if m not in FIRST_Z:
+            for k in (1, 2, 3):
+                C[units.index((m, k))].wait_recv()
+            add_into(p, [bc[m].at[w] for w in range(3)])
         own = out[m] if m == "kern" else cut(out[m], g[m], q)
         ag[m, "o"] = pltpu.make_async_copy(p, own, osem.at[j])
         ag[m, "o"].start()
@@ -937,7 +996,7 @@
     ahead = DEPTH - 1
     for i in range(ahead):
         stA(i)
-    for t in range(n + LE + 4):
+    for t in range(n + LE + 6):
         if t < n:
             if t + ahead < n:
                 stA(t + ahead)
@@ -946,12 +1005,13 @@
             stC(t - LC)
         if 0 <= t - LD < n:
             stD(t - LD)
-        j = t - LE
-        if 0 <= j < n and j % 4 == 3:
-            stE(units[j][0])
-        j = t - LE - 2
-        if 0 <= j < n and j % 4 == 3:
-            stF(units[j][0])
+        for j in range(n):
+            m, k = units[j]
+            wait = LATE if m in ORDER[1:-2] and m not in FIRST_Z else LE
+            if k == 0 and t == j + wait:
+                stE(m)
+            if k == 0 and t == j + wait + 2:
+                stF(m)
         if t >= 4 and t % 2 == 0 and t // 2 - 2 < 5:
             norm_step(t // 2 - 2)
     for m in ORDER:
@@ -962,16 +1022,14 @@
                 ag[m, w].wait_send()
         ag[m, "o"].wait()
     N[6].wait()
-    plain = [u for u in range(n) if units[u][0] != "kern"][-DEPTH:]
-    for i in A:
-        if i in plain or units[i][0] == "kern":
-            A[i].wait_send()
+    for i in sorted(left_behind):
+        A[i].wait_send()
     for d in (X, Y, C):
         for v in d.values():
             v.wait_send()
 
 
-LC, LD, LE = 1, 2, 3
+LC, LD, LE, LATE = 1, 2, 3, 6
 
 
 def half_shape(m, R, C):
@@ -989,7 +1047,8 @@
     n = len(ORDER)
     acts, rights = tuple(act), tuple(right)
     any_ = pl.BlockSpec(memory_space=pl.ANY)
-    snd = max(shp[m][0] for m in acts), max(shp[m][1] for m in acts)
+    snd = max(shp[m][0] for m in acts if m not in FIRST_Z), max(shp[m][1] for m in acts if m not in FIRST_Z)
+    snd2 = (16, 128)
     outs = pl.pallas_call(
         functools.partial(grad_kernel, acts, rights),
         out_shape=[jax.ShapeDtypeStruct(quarter_shape(m, *shp[m]) if m == "kern" else shp[m], jnp.bfloat16) for m in ORDER]
@@ -999,9 +1058,9 @@
         scratch_shapes=[V(act[m].shape) for m in acts]
         + [V(right[m].shape) for m in rights]
         + [V((4,) + shp[m]) for m in ORDER]
-        + [V((4, 3) + half_shape(m, *shp[m])) for m in ORDER] * 2
-        + [V((3,) + quarter_shape(m, *shp[m])) for m in ORDER]
-        + [V((DEPTH,) + snd), V(kern.shape), pltpu.VMEM((5,) + norm.shape, jnp.float32)]
+        + [V((1 if m in FIRST_Z else 4, 3) + half_shape(m, *shp[m])) for m in ORDER] * 2
+        + [V((3,) + (shp[m] if m in FIRST_Z else quarter_shape(m, *shp[m]))) for m in ORDER]
+        + [V((DEPTH,) + snd), V((DEPTH,) + snd2), V(kern.shape), pltpu.VMEM((5,) + norm.shape, jnp.float32)]
         + [D((len(acts) + len(rights),)), D(()), D((n, 4)), D((n, 4))]
         + [D((n, 4, 3))] * 4
         + [D((n, 3))] * 2
@@ -1193,7 +1252,6 @@
         pack = jnp.pad(jnp.swapaxes(norm_grads, 0, 1), ((0, 0), (0, 6), (0, 128 - norm_grads.shape[2])))
         left = {m: jnp.transpose(a).reshape(n_seq, -1, rows) for m, a in left.items()}
         sums, norm_grads = reduce_gradients(left, right, grad_kern, pack)
-        sums = {m: a.astype(F32) for m, a in sums.items()}
         norm_grads = norm_grads[:2, : ln_gain.shape[0]]
     else:
         grads = {m: dot_inner(left[m], right[m]).reshape(n_seq, -1, right[m].shape[1]) for m in left}
@@ -1202,9 +1260,16 @@
         sums = {m: lax.psum(a, "dp") for m, a in sums.items()}
         norm_grads = lax.psum_scatter(norm_grads, "seq", scatter_dimension=1, tiled=False)
         norm_grads = lax.psum(norm_grads, "dp")
-    modes_grad = jnp.stack(pull_kernels(sums["kern"], coef, rate, freq)).reshape(3, 2, some, modes)
+    modes_grad = jnp.stack(pull_kernels(sums["kern"].astype(F32), coef, rate, freq)).reshape(3, 2, some, modes)
     if linked:
-        modes_grad = lax.all_gather(modes_grad, "dp", axis=2, tiled=True)
+        modes_grad, sums = lax.optimization_barrier((modes_grad, sums))
+        sums = {m: a.astype(F32) for m, a in sums.items()}
+        column = lax.axis_index("dp")
+        hand = [modes_grad] + [lax.ppermute(modes_grad, "dp", [(i, i ^ w) for i in range(n_dp)]) for w in (1, 2, 3)]
+        odd, high = column % 2 == 1, column >= 2
+        hand = [jnp.where(odd, hand[w ^ 1], hand[w]) for w in range(4)]
+        hand = [jnp.where(high, hand[w ^ 2], hand[w]) for w in range(4)]
+        modes_grad = jnp.concatenate(hand, 2)
     return (
         mixed,
         grad_tokens,

time: 544 us -> 530 us (0.974)
  blocking collectives: 9.79 us -> 0 us
  Pallas kernels: 418 us -> 410 us
    pallas_call x1, Pallas kernels: 187 us -> 176 us  [gather_forward(): pl.pallas_call(functools.partial(forward_kernel, width), out_shape=full +...]
    all_gather x1 -> x0, blocking collectives: 9.79 us -> none  [shards(): modes_grad = lax.all_gather(modes_grad, 'dp', axis=2, tiled=True)]
  transfers between devices with their start and end apart: 4 -> 7, of which waited for: 0 -> 0; matrix products, arithmetic and copies ran while one was open for 6% -> 8% of each run, Pallas kernels for 0% -> 0%
where the time goes in v3:
time: 530 us; the launch traced here: 521 us
  Pallas kernels  410 us (77%)
  matrix products  35 us (7%)
  other arithmetic  30.9 us (6%)
  local copies, waits for them, and re-layouts  27.5 us (5%)
  starting transfers between devices  16.1 us (3%)
    pallas_call x1, Pallas kernels, reduce_gradients(): pl.pallas_call(functools.partial(grad_kernel, acts, rights), out_shape=[j...  198 us
    pallas_call x1, Pallas kernels, gather_forward(): pl.pallas_call(functools.partial(forward_kernel, width), out_shape=full +...  176 us
    pallas_call x1, Pallas kernels, conv_call(): pl.pallas_call(body, grid=(steps,), out_shape=outs, in_specs=[pl.BlockSpe...  36 us
    dot_general x4, matrix products, dot_outer(): lax.dot_general(left_side, right_side, (((1,), (1,)), ((), ())), preferre...  22.2 us
    ppermute x4, starting transfers between devices, shift(): return lax.ppermute(array, 'seq', pairs)  12.5 us
  transfers between devices with their start and end apart: 7, of which 0 were waited for; matrix products, arithmetic and copies ran while one was open for 8% of the time, Pallas kernels for 0%

profile of v3, /device:TPU:0, one launch (start us, length us, event | category | flops | bytes accessed | tf_op | source)
XLA Modules:
  0.0 520.7 jit_solution(4220832479492212711)
XLA Ops:
  0.7 0.7 broadcast_compare_fusion
  1.4 1.0 reduce_window_sum.11
  2.4 0.7 sub.32
  4.4 1.1 constant_dynamic-slice_fusion
  5.9 5.7 %fusion.19 = (f32[96,32,64]{2,1,0:T(8,128)S(1)}, f32[96,32,64]{2,1,0:T(8,128)S(1)}) fusion(f32[96,64]{1,0:T(8,128)S(1)} %bitcast.100, f32[32]{0:T(128)S(1)} %iota_convert_fusion, f32[96,64]{1,0:T(8,128)S(1)} %bitcast.103), kind=kLoop, calls=%fused_computation.32 | loop fusion | flops 786432 | bytes 1622144 | tf_op jit(solution)/shard_map/mul | solution.py:1085
  11.7 3.0 fusion.29
  14.7 2.8 convolution_convert_fusion.2
  18.1 0.8 copy.68.refs_5_
  19.4 175.6 %shard_map.238 = (bf16[8,16,128]{2,1,0:T(8,128)(2,1)}, bf16[8,96,1536]{2,1,0:T(8,128)(2,1)}, bf16[8,384,512]{2,1,0:T(8,128)(2,1)}, bf16[8,192,3072]{2,1,0:T(8,12...) custom-call(f32[28]{0:T(128)} %reshape.257.mask_ref, ...), custom_call_target="tpu_custom_call" | custom-call | flops 20000000000 | bytes 200000000 | tf_op jit(solution)/shard_map/pallas_call | solution.py:737
  195.1 10.5 %convolution_convert_fusion.1 = bf16[512,1536]{1,0:T(8,128)(2,1)} fusion(bf16[512,3072]{1,0:T(8,128)(2,1)} %get-tuple-element.49.refs_6_, bf16[1536,3072]{1,0:T(8,128)(2,1)} %bitcast.124), kind=kOutput, calls=%fused_computation.15 | convolution fusion | flops 4832624640 | bytes 14155776 | tf_op jit(solution)/shard_map/dot_general | solution.py:1126
  205.6 1.3 collective-permute-start
  206.9 2.1 slice.106
  208.9 1.3 collective-permute-start.1
  210.3 6.3 %convolution_convert_fusion = bf16[512,1536]{1,0:T(8,128)(2,1)} fusion(bf16[512,3072]{1,0:T(8,128)(2,1)S(1)} %copy-done.31, bf16[1536,3072]{1,0:T(8,128)(2,1)S(1)} %bitcast.123), kind=kOutput, calls=%fused_computation.14 | convolution fusion | flops 4832624640 | bytes 14155776 | tf_op jit(solution)/shard_map/dot_general | solution.py:1126
  216.6 5.8 %collective-permute-start.3 = (bf16[2,256,1536]{2,1,0:T(8,128)(2,1)}, bf16[2,256,1536]{2,1,0:T(8,128)(2,1)}, u32[]{:S(2)}, u32[]{:S(2)}) collective-permute-start(bf16[2,256,1536]{2,1,0:T(8,128)(2,1)} %bitcast.18.refs_6_), channel_id=1, source_target_pairs={{0,1},{1,2},{2,3},{3,4},{4,5},{5,6},{6,7},{8,9},{9,10},{10,11},{11... | collective-permute-start | bytes 4718600 | tf_op jit(solution)/shard_map/ppermute | solution.py:1138
  222.3 2.1 slice.107
  224.4 4.2 collective-permute-start.2
  228.8 0.7 convert_reduce_fusion.2
  229.9 3.8 fusion.42
  233.8 4.7 copy.69
  238.6 2.7 copy.70
  241.3 1.6 copy.71
  242.9 1.2 copy.72
  244.1 6.8 %fusion.16 = bf16[512,768]{1,0:T(8,128)(2,1)} fusion(bf16[512,768]{1,0:T(8,128)(2,1)S(1)} %bitcast.85, bf16[512,3072]{1,0:T(8,128)(2,1)} %get-tuple-element.43, bf16[3072,768]{1,0:T(8,128)(2,1)} %bitcast.125), kind=kOutput, calls=%fused_computation.29 | convolution fusion | flops 2417098752 | bytes 9437184 | tf_op jit(solution)/shard_map/dot_general | solution.py:1118
  250.9 36.0 %shard_map.239 = (bf16[2,256,1536]{2,1,0:T(8,128)(2,1)}, bf16[8,4,2,48,512]{4,3,2,1,0:T(8,128)(2,1)}) custom-call(f32[28]{0:T(128)} %reshape.257.mask_ref, bf16[256,256]{1,0:T(8,128)(2,1)} %constant.74.clone.refs_0_.wave_ref, bf16[8,4,2,48,512]{4,3,2,1,0:T(8,128)(2,1)} %bitcast.129, bf16[2,1024,1536]{2,1,0:T(8,128)(2,1)} %get-tuple-element.48.refs_0_, ...), custom_call_target="tpu_custom_call" | custom-call | flops 10000000000 | bytes 30000000 | tf_op jit(solution)/shard_map/pallas_call | solution.py:199
  286.9 3.5 fusion.2.refs_9_
  290.5 1.6 fusion.13
  292.1 0.9 fusion.15
  293.4 0.6 pad.14.refs_11_
  294.1 197.8 %shard_map.240 = (bf16[384,768]{1,0:T(8,128)(2,1)}, bf16[192,3072]{1,0:T(8,128)(2,1)}, bf16[192,3072]{1,0:T(8,128)(2,1)}, bf16[96,3072]{1,0:T(8,128)(2,1)}, bf16...) custom-call(bf16[8,384,512]{2,1,0:T(8,128)(2,1)} %bitcast.87, bf16[8,192,512]{2,1,0:T(8,128)(2,1)} %bitcast.90, ...), custom_call_target="tpu_custom_call" | custom-call | flops 16000000000 | bytes 100000000 | tf_op jit(solution)/shard_map/pallas_call | solution.py:1052
  491.9 1.0 copy.73
  493.1 0.8 pad_maximum_fusion.2
  493.9 3.6 copy.74
  497.5 3.3 fusion.30
  500.8 4.0 fusion.24
  504.9 1.5 collective-permute-start.4
  506.5 1.3 collective-permute-start.5
  507.8 0.8 collective-permute-start.6
  508.5 1.5 add_convert_fusion
  510.1 1.3 slice_bitcast_fusion.3
  511.4 1.1 convert_element_type.112
  512.5 0.9 convert_element_type.113
  513.4 1.7 convert_element_type.114
  515.0 1.7 convert_element_type.115
  516.7 1.1 convert_element_type.116
  518.0 0.8 copy.75
  518.7 0.8 copy.76
  519.5 0.8 copy.77
  (124 shorter events, 4.4 us)
Async XLA Ops:
  0.6 5.0 copy-start
  5.5 6.1 %copy-start.17 = (f32[2,48,64]{2,1,0:T(8,128)}, f32[2,48,64]{2,1,0:T(8,128)S(1)}, u32[]{:S(2)}) copy-start(f32[2,48,64]{2,1,0:T(8,128)S(1)} %copy.66) | copy-start | bytes 73732
  5.6 6.0 %copy-start.21 = (f32[2,48,64]{2,1,0:T(8,128)}, f32[2,48,64]{2,1,0:T(8,128)S(1)}, u32[]{:S(2)}) copy-start(f32[2,48,64]{2,1,0:T(8,128)S(1)} %copy.80) | copy-start | bytes 73732
  5.8 5.8 %copy-start.23 = (f32[2,48,64]{2,1,0:T(8,128)}, f32[2,48,64]{2,1,0:T(8,128)S(1)}, u32[]{:S(2)}) copy-start(f32[2,48,64]{2,1,0:T(8,128)S(1)} %copy.79) | copy-start | bytes 73732
  11.6 3.0 copy-start.2
  11.6 3.0 copy-start.4
  14.6 4.2 copy-start.26
  14.6 4.2 copy-start.27
  195.1 15.2 %slice-start = ((s8[9437184]{0:T(1024)(128)(4,1)}), s8[4194304]{0:T(1024)(128)(4,1)S(1)}, s32[]{:S(2)}) async-start(s8[9437184]{0:T(1024)(128)(4,1)} %bitcast.121), calls=%async_computation | async-start | bytes 8388608
  195.1 15.2 %slice-start.1 = ((s8[9437184]{0:T(1024)(128)(4,1)}), s8[4194304]{0:T(1024)(128)(4,1)S(1)}, s32[]{:S(2)}) async-start(s8[9437184]{0:T(1024)(128)(4,1)} %bitcast.121), calls=%async_computation.1 | async-start | bytes 8388608
  195.1 15.2 %slice-start.2 = ((s8[9437184]{0:T(1024)(128)(4,1)}), s8[1048576]{0:T(1024)(128)(4,1)S(1)}, s32[]{:S(2)}) async-start(s8[9437184]{0:T(1024)(128)(4,1)} %bitcast.121), calls=%async_computation.2 | async-start | bytes 2097152
  195.1 15.2 %copy-start.31 = (bf16[512,3072]{1,0:T(8,128)(2,1)S(1)}, bf16[512,3072]{1,0:T(8,128)(2,1)}, u32[]{:S(2)}) copy-start(bf16[512,3072]{1,0:T(8,128)(2,1)} %get-tuple-element.51.refs_7_) | copy-start | bytes 9437188
  205.6 45.3 %collective-permute-start = (bf16[2,256,1536]{2,1,0:T(8,128)(2,1)}, bf16[2,256,1536]{2,1,0:T(8,128)(2,1)}, u32[]{:S(2)}, u32[]{:S(2)}) collective-permute-start(bf16[2,256,1536]{2,1,0:T(8,128)(2,1)} %bitcast.16.refs_1_), channel_id=1, source_target_pairs={{1,0},{2,1},{3,2},{4,3},{5,4},{6,5},{7,6},{9,8},{10,9},{11,10},{12... | collective-permute-start | bytes 4718600 | tf_op jit(solution)/shard_map/ppermute | solution.py:1138
  208.9 41.9 %collective-permute-start.1 = (bf16[2,128,1536]{2,1,0:T(8,128)(2,1)}, bf16[2,128,1536]{2,1,0:T(8,128)(2,1)}, u32[]{:S(2)}, u32[]{:S(2)}) collective-permute-start(bf16[2,128,1536]{2,1,0:T(8,128)(2,1)} %slice.106), channel_id=1, source_target_pairs={{2,0},{3,1},{4,2},{5,3},{6,4},{7,5},{10,8},{11,9},{12,10},{13,11},... | collective-permute-start | bytes 2359304 | tf_op jit(solution)/shard_map/ppermute | solution.py:1138
  210.2 19.7 %slice-start.3 = ((s8[4718592]{0:T(1024)(128)(4,1)}), s8[4194304]{0:T(1024)(128)(4,1)S(1)}, s32[]{:S(2)}) async-start(s8[4718592]{0:T(1024)(128)(4,1)} %bitcast.126), calls=%async_computation.3 | async-start | bytes 8388608
  210.3 19.6 %slice-start.4 = ((s8[4718592]{0:T(1024)(128)(4,1)}), s8[524288]{0:T(1024)(128)(4,1)S(1)}, s32[]{:S(2)}) async-start(s8[4718592]{0:T(1024)(128)(4,1)} %bitcast.126), calls=%async_computation.4 | async-start | bytes 1048576
  210.3 19.6 %copy-start.30 = (bf16[512,3072]{1,0:T(8,128)(2,1)S(1)}, bf16[512,3072]{1,0:T(8,128)(2,1)}, u32[]{:S(2)}) copy-start(bf16[512,3072]{1,0:T(8,128)(2,1)} %get-tuple-element.45.refs_8_) | copy-start | bytes 9437188
  216.6 12.0 %copy-start.6 = (bf16[2,256,768]{2,1,0:T(8,128)(2,1)S(1)}, bf16[2,256,768]{2,1,0:T(8,128)(2,1)}, u32[]{:S(2)}) copy-start(bf16[2,256,768]{2,1,0:T(8,128)(2,1)} %param.15) | copy-start | bytes 2359300
  216.6 34.3 %collective-permute-start.3 = (bf16[2,256,1536]{2,1,0:T(8,128)(2,1)}, bf16[2,256,1536]{2,1,0:T(8,128)(2,1)}, u32[]{:S(2)}, u32[]{:S(2)}) collective-permute-start(bf16[2,256,1536]{2,1,0:T(8,128)(2,1)} %bitcast.18.refs_6_), channel_id=1, source_target_pairs={{0,1},{1,2},{2,3},{3,4},{4,5},{5,6},{6,7},{8,9},{9,10},{10,11},{11... | collective-permute-start | bytes 4718600 | tf_op jit(solution)/shard_map/ppermute | solution.py:1138
  224.4 26.4 %collective-permute-start.2 = (bf16[2,128,1536]{2,1,0:T(8,128)(2,1)}, bf16[2,128,1536]{2,1,0:T(8,128)(2,1)}, u32[]{:S(2)}, u32[]{:S(2)}) collective-permute-start(bf16[2,128,1536]{2,1,0:T(8,128)(2,1)} %slice.107), channel_id=1, source_target_pairs={{0,2},{1,3},{2,4},{3,5},{4,6},{5,7},{8,10},{9,11},{10,12},{11,13},... | collective-permute-start | bytes 2359304 | tf_op jit(solution)/shard_map/ppermute | solution.py:1138
  238.6 2.7 copy-start.11
  241.3 1.6 copy-start.15
  250.9 36.0 %copy-start.10 = (f32[512,1536]{1,0:T(8,128)S(1)}, f32[512,1536]{1,0:T(8,128)}, u32[]{:S(2)}) copy-start(f32[512,1536]{1,0:T(8,128)} %get-tuple-element.54) | copy-start | bytes 9437188
  286.9 3.6 copy-start.28
  286.9 3.6 copy-start.29
  290.5 1.6 copy-start.12
  292.1 1.1 copy-start.8
  493.0 4.5 copy-start.3
  493.0 4.5 copy-start.5
  497.5 3.3 copy-start.18
  500.8 4.1 copy-start.22
  500.8 4.1 copy-start.24
  500.8 7.7 %copy-start.7 = (bf16[2,256,768]{2,1,0:T(8,128)(2,1)S(1)}, bf16[2,256,768]{2,1,0:T(8,128)(2,1)}, u32[]{:S(2)}) copy-start(bf16[2,256,768]{2,1,0:T(8,128)(2,1)} %param.15) | copy-start | bytes 2359300
  500.8 7.7 %copy-start.9 = (f32[512,768]{1,0:T(8,128)S(1)}, f32[512,768]{1,0:T(8,128)}, u32[]{:S(2)}) copy-start(f32[512,768]{1,0:T(8,128)} %copy-done.8) | copy-start | bytes 4718596
  500.8 7.7 %copy-start.16 = (bf16[2,256,768]{2,1,0:T(8,128)(2,1)S(1)}, bf16[2,256,768]{2,1,0:T(8,128)(2,1)}, u32[]{:S(2)}) copy-start(bf16[2,256,768]{2,1,0:T(8,128)(2,1)} %param.16) | copy-start | bytes 2359300
  504.9 12.8 %collective-permute-start.4 = (f32[3,2,48,64]{3,2,1,0:T(8,128)S(1)}, f32[3,2,48,64]{3,2,1,0:T(8,128)S(1)}, u32[]{:S(2)}, u32[]{:S(2)}) collective-permute-start(f32[3,2,48,64]{3,2,1,0:T(8,128)S(1)} %pad_maximum_fusion.5), channel_id=1, source_target_pairs={{0,24},{8,16},{16,8},{24,0},{1,25},{9,17},{17,9},{25,1},{2,26},{10... | collective-permute-start | bytes 221192 | tf_op jit(solution)/shard_map/ppermute | solution.py:1268
  506.5 11.3 %collective-permute-start.5 = (f32[3,2,48,64]{3,2,1,0:T(8,128)S(1)}, f32[3,2,48,64]{3,2,1,0:T(8,128)S(1)}, u32[]{:S(2)}, u32[]{:S(2)}) collective-permute-start(f32[3,2,48,64]{3,2,1,0:T(8,128)S(1)} %pad_maximum_fusion.5), channel_id=1, source_target_pairs={{0,16},{8,24},{16,0},{24,8},{1,17},{9,25},{17,1},{25,9},{2,18},{10... | collective-permute-start | bytes 221192 | tf_op jit(solution)/shard_map/ppermute | solution.py:1268
  507.8 10.0 %collective-permute-start.6 = (f32[3,2,48,64]{3,2,1,0:T(8,128)S(1)}, f32[3,2,48,64]{3,2,1,0:T(8,128)S(1)}, u32[]{:S(2)}, u32[]{:S(2)}) collective-permute-start(f32[3,2,48,64]{3,2,1,0:T(8,128)S(1)} %pad_maximum_fusion.5), channel_id=1, source_target_pairs={{0,8},{8,0},{16,24},{24,16},{1,9},{9,1},{17,25},{25,17},{2,10},{10... | collective-permute-start | bytes 221192 | tf_op jit(solution)/shard_map/ppermute | solution.py:1268
  508.5 2.8 copy-start.20
  510.1 2.4 copy-start.25
  510.1 3.3 copy-start.14
  513.4 1.7 copy-start.13
  515.0 1.7 copy-start.19
  517.9 2.4 copy-start.1

commit v4 on v3

--- a/solution.py
+++ b/solution.py
@@ -1087,8 +1087,8 @@
     return powers(coarse), powers(fine)
 
 
-def make_kernels(coef, rate, freq):
-    (ar, ai), (br, bi) = mode_powers(rate, freq)
+def make_kernels(coef, rate, powers):
+    (ar, ai), (br, bi) = powers
     weight = (coef * jnp.sqrt(rate))[:, None, :]
     left = jnp.concatenate([weight * ar, -weight * ai], -1)
     right = jnp.concatenate([br, bi], -1)
@@ -1096,8 +1096,8 @@
     return rows.reshape(rows.shape[0], LONG)
 
 
-def pull_kernels(grad, coef, rate, freq):
-    (ar, ai), (br, bi) = mode_powers(rate, freq)
+def pull_kernels(grad, coef, rate, powers):
+    (ar, ai), (br, bi) = powers
     rows = grad.reshape(grad.shape[0], LONG // STEP_A, STEP_A)
     lags = jnp.arange(LONG).astype(F32).reshape(LONG // STEP_A, STEP_A)
     both = jnp.concatenate([rows, rows * lags[None]], 1)
@@ -1147,7 +1147,8 @@
 
 
 def same_item(lengths, own_blocks, count):
-    starts = jnp.cumsum(lengths, axis=1) - lengths
+    slots = jnp.arange(lengths.shape[1])
+    starts = jnp.sum(jnp.where(slots[None, :] < slots[:, None], lengths[:, None, :], 0), -1)
     total = own_blocks * count
     places = jnp.arange(total) * BLK
     present = (starts[:, None, :] <= places[None, :, None]) & (lengths[:, None, :] > 0)
@@ -1194,7 +1195,8 @@
         return lax.dynamic_slice_in_dim(array, first, some, 1).reshape(2 * some, modes)
 
     coef, rate, freq = mine(ssm_coef), mine(ssm_rate), mine(ssm_freq)
-    kernels = make_kernels(coef, rate, freq).astype(LOW)
+    powers = lax.optimization_barrier(mode_powers(rate, freq))
+    kernels = make_kernels(coef, rate, powers).astype(LOW)
     mask = same_item(lengths[:, 0], rows_each // BLK, n_seq).reshape(-1)
     wave = jnp.asarray(wave_tables(), LOW)
     tile_step = max(1, 384 // channels)
@@ -1260,7 +1262,7 @@
         sums = {m: lax.psum(a, "dp") for m, a in sums.items()}
         norm_grads = lax.psum_scatter(norm_grads, "seq", scatter_dimension=1, tiled=False)
         norm_grads = lax.psum(norm_grads, "dp")
-    modes_grad = jnp.stack(pull_kernels(sums["kern"].astype(F32), coef, rate, freq)).reshape(3, 2, some, modes)
+    modes_grad = jnp.stack(pull_kernels(sums["kern"].astype(F32), coef, rate, powers)).reshape(3, 2, some, modes)
     if linked:
         modes_grad, sums = lax.optimization_barrier((modes_grad, sums))
         sums = {m: a.astype(F32) for m, a in sums.items()}

time: 530 us -> 532 us (level)
  Pallas kernels: 410 us -> 417 us
    pallas_call x1, Pallas kernels: 176 us -> 182 us  [gather_forward(): pl.pallas_call(functools.partial(forward_kernel, width), out_shape=full +...]
where the time goes in v4:
time: 532 us; the launch traced here: 527 us
  Pallas kernels  417 us (78%)
  matrix products  35.1 us (7%)
  local copies, waits for them, and re-layouts  29.3 us (6%)
  other arithmetic  27.2 us (5%)
  starting transfers between devices  16 us (3%)
    pallas_call x1, Pallas kernels, reduce_gradients(): pl.pallas_call(functools.partial(grad_kernel, acts, rights), out_shape=[j...  200 us
    pallas_call x1, Pallas kernels, gather_forward(): pl.pallas_call(functools.partial(forward_kernel, width), out_shape=full +...  182 us
    pallas_call x1, Pallas kernels, conv_call(): pl.pallas_call(body, grid=(steps,), out_shape=outs, in_specs=[pl.BlockSpe...  36 us
    dot_general x4, matrix products, dot_outer(): lax.dot_general(left_side, right_side, (((1,), (1,)), ((), ())), preferre...  22.2 us
    ppermute x4, starting transfers between devices, shift(): return lax.ppermute(array, 'seq', pairs)  12.5 us
  transfers between devices with their start and end apart: 7, of which 0 were waited for; matrix products, arithmetic and copies ran while one was open for 8% of the time, Pallas kernels for 0%

profile of v4, /device:TPU:0, one launch (start us, length us, event | category | flops | bytes accessed | tf_op | source)
XLA Modules:
  0.0 526.6 jit_solution(3638241115035505778)
XLA Ops:
  0.7 0.7 broadcast_compare_fusion
  1.4 0.8 select_reduce_fusion
  3.5 1.1 constant_dynamic-slice_fusion
  4.9 2.9 fusion.22
  7.9 5.7 %fusion.20 = (f32[96,32,64]{2,1,0:T(8,128)S(1)}, f32[96,32,64]{2,1,0:T(8,128)S(1)}) fusion(f32[96,64]{1,0:T(8,128)S(1)} %bitcast.103, f32[32]{0:T(128)S(1)} %iota_convert_fusion, f32[96,64]{1,0:T(8,128)S(1)} %bitcast.105), kind=kLoop, calls=%fused_computation.33 | loop fusion | flops 786432 | bytes 1622144 | tf_op jit(solution)/shard_map/mul | solution.py:1085
  13.9 0.9 copy-done.2
  15.3 2.8 convolution_convert_fusion.2
  18.2 0.6 copy.67
  18.8 0.8 copy.68.refs_5_
  20.1 181.6 %shard_map.238 = (bf16[8,16,128]{2,1,0:T(8,128)(2,1)}, bf16[8,96,1536]{2,1,0:T(8,128)(2,1)}, bf16[8,384,512]{2,1,0:T(8,128)(2,1)}, bf16[8,192,3072]{2,1,0:T(8,12...) custom-call(f32[28]{0:T(128)} %reshape.255.mask_ref, ...), custom_call_target="tpu_custom_call" | custom-call | flops 20000000000 | bytes 200000000 | tf_op jit(solution)/shard_map/pallas_call | solution.py:737
  201.8 10.5 %convolution_convert_fusion.1 = bf16[512,1536]{1,0:T(8,128)(2,1)} fusion(bf16[512,3072]{1,0:T(8,128)(2,1)} %get-tuple-element.57.refs_6_, bf16[1536,3072]{1,0:T(8,128)(2,1)} %bitcast.122), kind=kOutput, calls=%fused_computation.15 | convolution fusion | flops 4832624640 | bytes 14155776 | tf_op jit(solution)/shard_map/dot_general | solution.py:1126
  212.3 1.3 collective-permute-start
  213.6 2.1 slice.106
  215.6 1.3 collective-permute-start.1
  217.0 6.3 %convolution_convert_fusion = bf16[512,1536]{1,0:T(8,128)(2,1)} fusion(bf16[512,3072]{1,0:T(8,128)(2,1)S(1)} %copy-done.33, bf16[1536,3072]{1,0:T(8,128)(2,1)S(1)} %bitcast.121), kind=kOutput, calls=%fused_computation.14 | convolution fusion | flops 4832624640 | bytes 14155776 | tf_op jit(solution)/shard_map/dot_general | solution.py:1126
  223.3 5.9 %collective-permute-start.3 = (bf16[2,256,1536]{2,1,0:T(8,128)(2,1)}, bf16[2,256,1536]{2,1,0:T(8,128)(2,1)}, u32[]{:S(2)}, u32[]{:S(2)}) collective-permute-start(bf16[2,256,1536]{2,1,0:T(8,128)(2,1)} %bitcast.18.refs_6_), channel_id=1, source_target_pairs={{0,1},{1,2},{2,3},{3,4},{4,5},{5,6},{6,7},{8,9},{9,10},{10,11},{11... | collective-permute-start | bytes 4718600 | tf_op jit(solution)/shard_map/ppermute | solution.py:1138
  229.1 2.1 slice.107
  231.2 4.0 collective-permute-start.2
  235.4 0.7 convert_reduce_fusion.2
  236.6 3.8 fusion.39
  240.5 5.1 copy.69
  245.6 2.7 copy.70
  248.3 1.6 copy.71
  249.9 1.2 copy.72
  251.1 6.8 %fusion.16 = bf16[512,768]{1,0:T(8,128)(2,1)} fusion(bf16[512,768]{1,0:T(8,128)(2,1)S(1)} %bitcast.85, bf16[512,3072]{1,0:T(8,128)(2,1)} %get-tuple-element.51, bf16[3072,768]{1,0:T(8,128)(2,1)} %bitcast.123), kind=kOutput, calls=%fused_computation.29 | convolution fusion | flops 2417098752 | bytes 9437184 | tf_op jit(solution)/shard_map/dot_general | solution.py:1118
  257.9 36.0 %shard_map.239 = (bf16[2,256,1536]{2,1,0:T(8,128)(2,1)}, bf16[8,4,2,48,512]{4,3,2,1,0:T(8,128)(2,1)}) custom-call(f32[28]{0:T(128)} %reshape.255.mask_ref, bf16[256,256]{1,0:T(8,128)(2,1)} %constant.71.clone.refs_0_.wave_ref, bf16[8,4,2,48,512]{4,3,2,1,0:T(8,128)(2,1)} %bitcast.127, bf16[2,1024,1536]{2,1,0:T(8,128)(2,1)} %get-tuple-element.56.refs_0_, ...), custom_call_target="tpu_custom_call" | custom-call | flops 10000000000 | bytes 30000000 | tf_op jit(solution)/shard_map/pallas_call | solution.py:199
  293.9 3.5 fusion.2.refs_9_
  297.5 1.6 fusion.13
  299.2 0.9 fusion.15
  300.5 0.6 pad.14.refs_11_
  301.1 199.7 %shard_map.240 = (bf16[384,768]{1,0:T(8,128)(2,1)}, bf16[192,3072]{1,0:T(8,128)(2,1)}, bf16[192,3072]{1,0:T(8,128)(2,1)}, bf16[96,3072]{1,0:T(8,128)(2,1)}, bf16...) custom-call(bf16[8,384,512]{2,1,0:T(8,128)(2,1)} %bitcast.87, bf16[8,192,512]{2,1,0:T(8,128)(2,1)} %bitcast.90, ...), custom_call_target="tpu_custom_call" | custom-call | flops 16000000000 | bytes 100000000 | tf_op jit(solution)/shard_map/pallas_call | solution.py:1052
  500.8 1.0 copy.73
  501.9 0.8 pad_maximum_fusion.2
  502.8 3.6 copy.74
  506.4 3.4 fusion.28
  509.9 1.0 fusion.24
  511.0 1.5 collective-permute-start.4
  512.9 1.7 collective-permute-start.6
  514.6 1.5 add_convert_fusion
  516.1 1.3 slice_bitcast_fusion.3
  517.4 1.1 convert_element_type.110
  518.5 0.9 convert_element_type.111
  519.4 1.7 convert_element_type.112
  521.1 1.7 convert_element_type.113
  522.7 1.1 convert_element_type.114
  524.0 0.8 copy.75
  524.8 0.8 copy.76
  525.5 0.8 copy.77
  (130 shorter events, 4.8 us)
Async XLA Ops:
  0.6 4.0 copy-start
  4.8 8.8 %copy-start.23 = (f32[2,48,64]{2,1,0:T(8,128)}, f32[2,48,64]{2,1,0:T(8,128)S(1)}, u32[]{:S(2)}) copy-start(f32[2,48,64]{2,1,0:T(8,128)S(1)} %copy.79) | copy-start | bytes 73732
  4.9 8.7 %copy-start.25 = (f32[2,48,64]{2,1,0:T(8,128)}, f32[2,48,64]{2,1,0:T(8,128)S(1)}, u32[]{:S(2)}) copy-start(f32[2,48,64]{2,1,0:T(8,128)S(1)} %copy.80) | copy-start | bytes 73732
  7.9 5.8 %copy-start.8 = (f32[96,16,64]{2,1,0:T(8,128)}, f32[96,16,64]{2,1,0:T(8,128)S(1)}, u32[]{:S(2)}) copy-start(f32[96,16,64]{2,1,0:T(8,128)S(1)} %get-tuple-element.48) | copy-start | bytes 1179652
  7.9 5.9 %copy-start.10 = (f32[96,16,64]{2,1,0:T(8,128)}, f32[96,16,64]{2,1,0:T(8,128)S(1)}, u32[]{:S(2)}) copy-start(f32[96,16,64]{2,1,0:T(8,128)S(1)} %get-tuple-element.47) | copy-start | bytes 1179652
  13.6 1.2 copy-start.2
  13.7 1.7 copy-start.4
  15.3 4.2 copy-start.28
  15.3 4.2 copy-start.29
  201.8 15.2 %slice-start = ((s8[9437184]{0:T(1024)(128)(4,1)}), s8[4194304]{0:T(1024)(128)(4,1)S(1)}, s32[]{:S(2)}) async-start(s8[9437184]{0:T(1024)(128)(4,1)} %bitcast.119), calls=%async_computation | async-start | bytes 8388608
  201.8 15.2 %slice-start.1 = ((s8[9437184]{0:T(1024)(128)(4,1)}), s8[4194304]{0:T(1024)(128)(4,1)S(1)}, s32[]{:S(2)}) async-start(s8[9437184]{0:T(1024)(128)(4,1)} %bitcast.119), calls=%async_computation.1 | async-start | bytes 8388608
  201.8 15.2 %slice-start.2 = ((s8[9437184]{0:T(1024)(128)(4,1)}), s8[1048576]{0:T(1024)(128)(4,1)S(1)}, s32[]{:S(2)}) async-start(s8[9437184]{0:T(1024)(128)(4,1)} %bitcast.119), calls=%async_computation.2 | async-start | bytes 2097152
  201.8 15.2 %copy-start.33 = (bf16[512,3072]{1,0:T(8,128)(2,1)S(1)}, bf16[512,3072]{1,0:T(8,128)(2,1)}, u32[]{:S(2)}) copy-start(bf16[512,3072]{1,0:T(8,128)(2,1)} %get-tuple-element.59.refs_7_) | copy-start | bytes 9437188
  212.3 45.6 %collective-permute-start = (bf16[2,256,1536]{2,1,0:T(8,128)(2,1)}, bf16[2,256,1536]{2,1,0:T(8,128)(2,1)}, u32[]{:S(2)}, u32[]{:S(2)}) collective-permute-start(bf16[2,256,1536]{2,1,0:T(8,128)(2,1)} %bitcast.16.refs_1_), channel_id=1, source_target_pairs={{1,0},{2,1},{3,2},{4,3},{5,4},{6,5},{7,6},{9,8},{10,9},{11,10},{12... | collective-permute-start | bytes 4718600 | tf_op jit(solution)/shard_map/ppermute | solution.py:1138
  215.6 42.2 %collective-permute-start.1 = (bf16[2,128,1536]{2,1,0:T(8,128)(2,1)}, bf16[2,128,1536]{2,1,0:T(8,128)(2,1)}, u32[]{:S(2)}, u32[]{:S(2)}) collective-permute-start(bf16[2,128,1536]{2,1,0:T(8,128)(2,1)} %slice.106), channel_id=1, source_target_pairs={{2,0},{3,1},{4,2},{5,3},{6,4},{7,5},{10,8},{11,9},{12,10},{13,11},... | collective-permute-start | bytes 2359304 | tf_op jit(solution)/shard_map/ppermute | solution.py:1138
  216.9 19.6 %slice-start.3 = ((s8[4718592]{0:T(1024)(128)(4,1)}), s8[4194304]{0:T(1024)(128)(4,1)S(1)}, s32[]{:S(2)}) async-start(s8[4718592]{0:T(1024)(128)(4,1)} %bitcast.124), calls=%async_computation.3 | async-start | bytes 8388608
  217.0 19.6 %slice-start.4 = ((s8[4718592]{0:T(1024)(128)(4,1)}), s8[524288]{0:T(1024)(128)(4,1)S(1)}, s32[]{:S(2)}) async-start(s8[4718592]{0:T(1024)(128)(4,1)} %bitcast.124), calls=%async_computation.4 | async-start | bytes 1048576
  217.0 19.6 %copy-start.32 = (bf16[512,3072]{1,0:T(8,128)(2,1)S(1)}, bf16[512,3072]{1,0:T(8,128)(2,1)}, u32[]{:S(2)}) copy-start(bf16[512,3072]{1,0:T(8,128)(2,1)} %get-tuple-element.53.refs_8_) | copy-start | bytes 9437188
  223.3 12.0 %copy-start.6 = (bf16[2,256,768]{2,1,0:T(8,128)(2,1)S(1)}, bf16[2,256,768]{2,1,0:T(8,128)(2,1)}, u32[]{:S(2)}) copy-start(bf16[2,256,768]{2,1,0:T(8,128)(2,1)} %param.15) | copy-start | bytes 2359300
  223.3 34.6 %collective-permute-start.3 = (bf16[2,256,1536]{2,1,0:T(8,128)(2,1)}, bf16[2,256,1536]{2,1,0:T(8,128)(2,1)}, u32[]{:S(2)}, u32[]{:S(2)}) collective-permute-start(bf16[2,256,1536]{2,1,0:T(8,128)(2,1)} %bitcast.18.refs_6_), channel_id=1, source_target_pairs={{0,1},{1,2},{2,3},{3,4},{4,5},{5,6},{6,7},{8,9},{9,10},{10,11},{11... | collective-permute-start | bytes 4718600 | tf_op jit(solution)/shard_map/ppermute | solution.py:1138
  231.2 26.6 %collective-permute-start.2 = (bf16[2,128,1536]{2,1,0:T(8,128)(2,1)}, bf16[2,128,1536]{2,1,0:T(8,128)(2,1)}, u32[]{:S(2)}, u32[]{:S(2)}) collective-permute-start(bf16[2,128,1536]{2,1,0:T(8,128)(2,1)} %slice.107), channel_id=1, source_target_pairs={{0,2},{1,3},{2,4},{3,5},{4,6},{5,7},{8,10},{9,11},{10,12},{11,13},... | collective-permute-start | bytes 2359304 | tf_op jit(solution)/shard_map/ppermute | solution.py:1138
  245.6 2.7 copy-start.15
  248.3 1.6 copy-start.19
  257.9 36.0 %copy-start.14 = (f32[512,1536]{1,0:T(8,128)S(1)}, f32[512,1536]{1,0:T(8,128)}, u32[]{:S(2)}) copy-start(f32[512,1536]{1,0:T(8,128)} %get-tuple-element.62) | copy-start | bytes 9437188
  293.9 3.6 copy-start.30
  293.9 3.6 copy-start.31
  297.5 1.7 copy-start.16
  299.1 1.1 copy-start.12
  501.9 4.5 copy-start.3
  501.9 4.5 copy-start.5
  506.4 3.4 copy-start.9
  506.4 3.4 copy-start.11
  509.8 1.1 copy-start.24
  509.8 1.1 copy-start.26
  509.8 4.7 copy-start.7
  509.8 4.7 copy-start.13
  509.8 4.7 copy-start.20
  511.0 12.8 %collective-permute-start.4 = (f32[3,2,48,64]{3,2,1,0:T(8,128)S(1)}, f32[3,2,48,64]{3,2,1,0:T(8,128)S(1)}, u32[]{:S(2)}, u32[]{:S(2)}) collective-permute-start(f32[3,2,48,64]{3,2,1,0:T(8,128)S(1)} %pad_maximum_fusion.5), channel_id=1, source_target_pairs={{0,24},{8,16},{16,8},{24,0},{1,25},{9,17},{17,9},{25,1},{2,26},{10... | collective-permute-start | bytes 221192 | tf_op jit(solution)/shard_map/ppermute | solution.py:1270
  512.5 11.3 %collective-permute-start.5 = (f32[3,2,48,64]{3,2,1,0:T(8,128)S(1)}, f32[3,2,48,64]{3,2,1,0:T(8,128)S(1)}, u32[]{:S(2)}, u32[]{:S(2)}) collective-permute-start(f32[3,2,48,64]{3,2,1,0:T(8,128)S(1)} %pad_maximum_fusion.5), channel_id=1, source_target_pairs={{0,16},{8,24},{16,0},{24,8},{1,17},{9,25},{17,1},{25,9},{2,18},{10... | collective-permute-start | bytes 221192 | tf_op jit(solution)/shard_map/ppermute | solution.py:1270
  512.9 11.0 %collective-permute-start.6 = (f32[3,2,48,64]{3,2,1,0:T(8,128)S(1)}, f32[3,2,48,64]{3,2,1,0:T(8,128)S(1)}, u32[]{:S(2)}, u32[]{:S(2)}) collective-permute-start(f32[3,2,48,64]{3,2,1,0:T(8,128)S(1)} %pad_maximum_fusion.5), channel_id=1, source_target_pairs={{0,8},{8,0},{16,24},{24,16},{1,9},{9,1},{17,25},{25,17},{2,10},{10... | collective-permute-start | bytes 221192 | tf_op jit(solution)/shard_map/ppermute | solution.py:1270
  514.6 2.8 copy-start.22
  516.1 2.4 copy-start.27
  516.1 3.3 copy-start.18
  519.4 1.7 copy-start.17
  521.1 1.7 copy-start.21
  523.9 2.4 copy-start.1
